TPU v7x, 128 devices: a whole 4x4x4 slice. The times are simulated.
128 devices in a mesh: dp: 16 (over y_lo, x, core), tensor: 8 (over z, y_hi).
Axes of the slice: x: 4, y: 4 (y_hi: 2, y_lo: 2; y = y_hi * 2 + y_lo), z: 4, core: 2. Of those that a mesh axis runs over, the one named last changes fastest.
Arguments:
- inputs: bfloat16 [12288, 2048], P('dp'), may hold values from -6 to 6
- segments: int32 [16, 768], P('dp'), may hold values from 0 to 2, never falling along the last dimension, each value on 1 to 384 neighbouring positions
- attn_gain: float32 [2048], replicated, may hold values from 0.1 to 1.9
- w_query: bfloat16 [2048, 2048], P(None, 'tensor'), may hold values from -0.125 to 0.125
- w_key: bfloat16 [2048, 2048], P(None, 'tensor'), may hold values from -0.125 to 0.125
- w_value: bfloat16 [2048, 4096], P(None, 'tensor'), may hold values from -0.125 to 0.125
- w_gate: bfloat16 [2048, 4096], P(None, 'tensor'), may hold values from -0.125 to 0.125
- w_beta: bfloat16 [2048, 16], P(None, 'tensor'), may hold values from -0.125 to 0.125
- w_alpha: bfloat16 [2048, 16], P(None, 'tensor'), may hold values from -0.125 to 0.125
- conv_query: float32 [4, 2048], P(None, 'tensor'), may hold values from -3 to 3
- conv_key: float32 [4, 2048], P(None, 'tensor'), may hold values from -3 to 3
- conv_value: float32 [4, 4096], P(None, 'tensor'), may hold values from -3 to 3
- decay_log: float32 [16], P('tensor'), may hold values from -6.5 to -2.5
- decay_bias: float32 [16], P('tensor'), may hold values from -1 to 1
- head_gain: float32 [256], replicated, may hold values from 0.1 to 1.9
- w_out: bfloat16 [4096, 2048], P('tensor'), may hold values from -0.09375 to 0.09375
- ffn_gain: float32 [2048], replicated, may hold values from 0.1 to 1.9
- w_up_gate: bfloat16 [2048, 5632], P(None, 'tensor'), may hold values from -0.125 to 0.125
- w_up: bfloat16 [2048, 5632], P(None, 'tensor'), may hold values from -0.125 to 0.125
- w_down: bfloat16 [5632, 2048], P('tensor'), may hold values from -0.078125 to 0.078125
- out_grad: bfloat16 [12288, 2048], P('dp'), may hold values from -6 to 6
Outputs:
- outputs: bfloat16 [12288, 2048], P('dp')
- input_grad: bfloat16 [12288, 2048], P('dp')
- grad_attn_gain: float32 [2048], replicated
- grad_query: float32 [2048, 2048], P('dp', 'tensor')
- grad_key: float32 [2048, 2048], P('dp', 'tensor')
- grad_value: float32 [2048, 4096], P('dp', 'tensor')
- grad_gate: float32 [2048, 4096], P('dp', 'tensor')
- grad_beta: float32 [2048, 16], P('dp', 'tensor')
- grad_alpha: float32 [2048, 16], P('dp', 'tensor')
- grad_conv_query: float32 [4, 2048], P(None, 'tensor')
- grad_conv_key: float32 [4, 2048], P(None, 'tensor')
- grad_conv_value: float32 [4, 4096], P(None, 'tensor')
- grad_decay_log: float32 [16], P('tensor')
- grad_decay_bias: float32 [16], P('tensor')
- grad_head_gain: float32 [256], replicated
- grad_out: float32 [4096, 2048], P('tensor', 'dp')
- grad_ffn_gain: float32 [2048], replicated
- grad_up_gate: float32 [2048, 5632], P('dp', 'tensor')
- grad_up: float32 [2048, 5632], P('dp', 'tensor')
- grad_down: float32 [5632, 2048], P('tensor', 'dp')
Inputs may be any that keep to these rules, and one draw needn't show every extreme that they name: `segments`: within each sequence document numbers never fall, every number 0 to 2 is used, and the longest document has exactly half of 768 tokens.
All inputs are finite; a program needn't handle non-finite values.
Results may differ from a plain program's by a relative error of at most 0.015.
Values sent between devices are 32-bit elements; how exact they have to be, the bound alone decides.
A program may use at most 256 MiB of HBM per device.

v0:
```python
import jax
import jax.numpy as jnp
from jax import lax
from jax.sharding import PartitionSpec as P

BLOCK = 64


def mean_norm(values):
    return values * lax.rsqrt(jnp.mean(values * values, axis=-1, keepdims=True) + 1e-05)


def norm_back(raw, normed, grad_normed):
    scale = lax.rsqrt(jnp.mean(raw * raw, axis=-1, keepdims=True) + 1e-05)
    return scale * (grad_normed - normed * jnp.mean(grad_normed * normed, axis=-1, keepdims=True))


def short_conv(signal, taps, seg_table):
    seq_count, length = seg_table.shape
    shaped = signal.reshape(seq_count, length, signal.shape[-1])
    total = shaped * taps[0]
    for offset in range(1, taps.shape[0]):
        moved = jnp.pad(shaped, ((0, 0), (offset, 0), (0, 0)))[:, :length]
        seg_moved = jnp.pad(seg_table, ((0, 0), (offset, 0)), constant_values=-1)[:, :length]
        same_doc = (seg_moved == seg_table).astype(jnp.float32)[:, :, None]
        total = total + moved * same_doc * taps[offset]
    return total.reshape(signal.shape)


def block_step(memory_state, pieces):
    query_rows, key, value_rows, beta, log_decay, seg_rows, prev_seg = pieces
    highest_precision = lax.Precision.HIGHEST
    span = seg_rows.shape[-1]
    row_index = lax.broadcasted_iota(jnp.int32, (span, span), 0)
    col_index = lax.broadcasted_iota(jnp.int32, (span, span), 1)
    cumul = jnp.cumsum(log_decay, axis=-1)
    keep = (seg_rows[:, :, None] == seg_rows[:, None, :]) & (row_index >= col_index)[None]
    spread = cumul[:, :, None] - cumul[:, None, :]
    decay = jnp.where(keep, jnp.exp(jnp.where(keep, spread, 0.0)), 0.0)
    carried_state = jnp.where(seg_rows == prev_seg[:, None], jnp.exp(cumul), 0.0)
    key_key = jnp.einsum("nik,njk->nij", key, key, precision=highest_precision)
    strict = jnp.where((row_index > col_index)[None], decay, 0.0) * key_key * beta[:, None, :]
    ident_mat = (row_index == col_index).astype(strict.dtype)[None]
    target_value = value_rows - carried_state[:, :, None] * jnp.einsum(
        "fmc,fcq->fmq", key, memory_state, precision=highest_precision
    )
    delta_update = jax.scipy.linalg.solve_triangular(
        ident_mat + strict, target_value, lower=True, unit_diagonal=True
    )
    query_key = jnp.einsum("nik,njk->nij", query_rows, key, precision=highest_precision)
    within = decay * query_key * beta[:, None, :]
    result_value = carried_state[:, :, None] * jnp.einsum(
        "fmc,fcq->fmq", query_rows, memory_state, precision=highest_precision
    )
    result_value = result_value + jnp.einsum(
        "nij,njv->niv", within, delta_update, precision=highest_precision
    )
    final_tap_weight = decay[:, -1, :] * beta
    updated_state = carried_state[:, -1][:, None, None] * memory_state
    updated_state = updated_state + jnp.einsum(
        "ite,itr->ier",
        key * final_tap_weight[:, :, None],
        delta_update,
        precision=highest_precision,
    )
    return (updated_state, result_value)


def delta_rule(query_rows, key, value_rows, beta, log_decay, seg_table, span):
    seq_count, length, heads, key_size = query_rows.shape
    blocks = length // span

    def arrange(tensor):
        moved = jnp.transpose(tensor, (0, 2, 1, 3)).reshape(
            seq_count * heads, blocks, span, tensor.shape[-1]
        )
        return jnp.transpose(moved, (1, 0, 2, 3))

    def arrange_flat(tensor):
        moved = jnp.transpose(tensor, (0, 2, 1)).reshape(seq_count * heads, blocks, span)
        return jnp.transpose(moved, (1, 0, 2))

    seg_rows = jnp.broadcast_to(seg_table[:, None, :], (seq_count, heads, length))
    seg_blocks = jnp.transpose(seg_rows.reshape(seq_count * heads, blocks, span), (1, 0, 2))
    prev_seg = jnp.concatenate([seg_blocks[:1, :, 0], seg_blocks[:-1, :, -1]], axis=0)
    memory_state = jnp.zeros((seq_count * heads, key_size, value_rows.shape[-1]), jnp.float32)
    final_state, results = lax.scan(
        jax.checkpoint(block_step),
        memory_state,
        (
            arrange(query_rows),
            arrange(key),
            arrange(value_rows),
            arrange_flat(beta),
            arrange_flat(log_decay),
            seg_blocks,
            prev_seg,
        ),
    )
    results = jnp.transpose(results, (1, 0, 2, 3)).reshape(
        seq_count, heads, length, value_rows.shape[-1]
    )
    return jnp.transpose(results, (0, 2, 1, 3))


def mixer(
    query_pre,
    key_pre,
    value_pre,
    gate_in,
    beta_pre,
    alpha_pre,
    conv_q,
    conv_k,
    conv_v,
    rate_log,
    rate_bias,
    gain_heads,
    seg_table,
):
    seq_count, length = seg_table.shape
    heads = rate_log.shape[0]
    key_size = query_pre.shape[-1] // heads
    value_size = value_pre.shape[-1] // heads
    query_rows = jax.nn.silu(short_conv(query_pre, conv_q, seg_table)).reshape(
        seq_count, length, heads, key_size
    )
    query_rows = (
        query_rows
        * lax.rsqrt(jnp.sum(query_rows * query_rows, axis=-1, keepdims=True) + 1e-06)
        * key_size ** (-0.5)
    )
    key = jax.nn.silu(short_conv(key_pre, conv_k, seg_table)).reshape(
        seq_count, length, heads, key_size
    )
    key = key * lax.rsqrt(jnp.sum(key * key, axis=-1, keepdims=True) + 1e-06)
    value_rows = jax.nn.silu(short_conv(value_pre, conv_v, seg_table)).reshape(
        seq_count, length, heads, value_size
    )
    beta = jax.nn.sigmoid(beta_pre).reshape(seq_count, length, heads)
    log_decay = (-jnp.exp(rate_log) * jax.nn.softplus(alpha_pre + rate_bias)).reshape(
        seq_count, length, heads
    )
    mixed = delta_rule(query_rows, key, value_rows, beta, log_decay, seg_table, BLOCK)
    gate = jax.nn.silu(gate_in).reshape(seq_count, length, heads, value_size)
    normed = mean_norm(mixed) * gain_heads * gate
    return normed.reshape(seq_count * length, heads * value_size)


def matmul(left, right):
    return jnp.dot(left, right, preferred_element_type=jnp.float32)


def per_device(
    inputs,
    segments,
    attn_gain,
    w_query,
    w_key,
    w_value,
    w_gate,
    w_beta,
    w_alpha,
    conv_query,
    conv_key,
    conv_value,
    decay_log,
    decay_bias,
    head_gain,
    w_out,
    ffn_gain,
    w_up_gate,
    w_up,
    w_down,
    out_grad,
):
    tokens_in = inputs.astype(jnp.float32)
    normed_in = mean_norm(tokens_in)
    hidden_in = (normed_in * attn_gain).astype(jnp.bfloat16)
    query_pre = matmul(hidden_in, w_query)
    key_pre = matmul(hidden_in, w_key)
    value_pre = matmul(hidden_in, w_value)
    gate_pre = matmul(hidden_in, w_gate)
    beta_pre = matmul(hidden_in, w_beta)
    alpha_pre = matmul(hidden_in, w_alpha)

    def mixer_local(
        query_val,
        key_val,
        value_val,
        gate_val,
        beta_val,
        alpha_val,
        conv_q,
        conv_k,
        conv_v,
        rate_log,
        rate_bias,
        gain_heads,
    ):
        return mixer(
            query_val,
            key_val,
            value_val,
            gate_val,
            beta_val,
            alpha_val,
            conv_q,
            conv_k,
            conv_v,
            rate_log,
            rate_bias,
            gain_heads,
            segments,
        )

    mixed, mixer_back = jax.vjp(
        mixer_local,
        query_pre,
        key_pre,
        value_pre,
        gate_pre,
        beta_pre,
        alpha_pre,
        conv_query,
        conv_key,
        conv_value,
        decay_log,
        decay_bias,
        head_gain,
    )
    mixed_low = mixed.astype(jnp.bfloat16)
    attn_total = lax.psum(matmul(mixed_low, w_out), "tensor")
    resid_mid = tokens_in + attn_total
    normed_mid = mean_norm(resid_mid)
    hidden_mid = (normed_mid * ffn_gain).astype(jnp.bfloat16)
    ffn_gate_pre = matmul(hidden_mid, w_up_gate)
    up_pre = matmul(hidden_mid, w_up)
    gate_sigmoid = jax.nn.sigmoid(ffn_gate_pre)
    gate_active = ffn_gate_pre * gate_sigmoid
    inner = (gate_active * up_pre).astype(jnp.bfloat16)
    ffn_total = lax.psum(matmul(inner, w_down), "tensor")
    outputs = (resid_mid + ffn_total).astype(jnp.bfloat16)
    grad_inner = matmul(out_grad, w_down.T)
    grad_down = matmul(inner.T, out_grad)
    grad_gate_pre = (
        grad_inner * up_pre * gate_sigmoid * (1.0 + ffn_gate_pre * (1.0 - gate_sigmoid))
    ).astype(jnp.bfloat16)
    grad_up_pre = (grad_inner * gate_active).astype(jnp.bfloat16)
    grad_up_gate = matmul(hidden_mid.T, grad_gate_pre)
    grad_up = matmul(hidden_mid.T, grad_up_pre)
    back_mid = lax.psum(matmul(grad_gate_pre, w_up_gate.T) + matmul(grad_up_pre, w_up.T), "tensor")
    grad_ffn_gain = jnp.sum(back_mid * normed_mid, axis=0)
    grad_resid = out_grad.astype(jnp.float32) + norm_back(
        resid_mid, normed_mid, back_mid * ffn_gain
    )
    grad_attn = grad_resid.astype(jnp.bfloat16)
    grad_out = matmul(mixed_low.T, grad_attn)
    grad_mixed = matmul(grad_attn, w_out.T)
    back_pieces = mixer_back(grad_mixed)
    grad_query_pre = back_pieces[0].astype(jnp.bfloat16)
    grad_key_pre = back_pieces[1].astype(jnp.bfloat16)
    grad_value_pre = back_pieces[2].astype(jnp.bfloat16)
    grad_gatein_pre = back_pieces[3].astype(jnp.bfloat16)
    grad_beta_pre = back_pieces[4].astype(jnp.bfloat16)
    grad_alpha_pre = back_pieces[5].astype(jnp.bfloat16)
    grad_query = matmul(hidden_in.T, grad_query_pre)
    grad_key = matmul(hidden_in.T, grad_key_pre)
    grad_value = matmul(hidden_in.T, grad_value_pre)
    grad_gate = matmul(hidden_in.T, grad_gatein_pre)
    grad_beta = matmul(hidden_in.T, grad_beta_pre)
    grad_alpha = matmul(hidden_in.T, grad_alpha_pre)
    back_part = matmul(grad_query_pre, w_query.T) + matmul(grad_key_pre, w_key.T)
    back_part = back_part + matmul(grad_value_pre, w_value.T) + matmul(grad_gatein_pre, w_gate.T)
    back_part = back_part + matmul(grad_beta_pre, w_beta.T) + matmul(grad_alpha_pre, w_alpha.T)
    back_in, head_gain_sum = lax.psum((back_part, back_pieces[11]), "tensor")
    grad_attn_gain = jnp.sum(back_in * normed_in, axis=0)
    input_grad = (grad_resid + norm_back(tokens_in, normed_in, back_in * attn_gain)).astype(
        jnp.bfloat16
    )
    small_sums = lax.psum(
        (
            grad_attn_gain,
            grad_ffn_gain,
            head_gain_sum,
            back_pieces[6],
            back_pieces[7],
            back_pieces[8],
            back_pieces[9],
            back_pieces[10],
        ),
        "dp",
    )
    matrix_sums = (
        lax.psum_scatter(grad_query, "dp", scatter_dimension=0, tiled=True),
        lax.psum_scatter(grad_key, "dp", scatter_dimension=0, tiled=True),
        lax.psum_scatter(grad_value, "dp", scatter_dimension=0, tiled=True),
        lax.psum_scatter(grad_gate, "dp", scatter_dimension=0, tiled=True),
        lax.psum_scatter(grad_beta, "dp", scatter_dimension=0, tiled=True),
        lax.psum_scatter(grad_alpha, "dp", scatter_dimension=0, tiled=True),
        lax.psum_scatter(grad_out, "dp", scatter_dimension=1, tiled=True),
        lax.psum_scatter(grad_up_gate, "dp", scatter_dimension=0, tiled=True),
        lax.psum_scatter(grad_up, "dp", scatter_dimension=0, tiled=True),
        lax.psum_scatter(grad_down, "dp", scatter_dimension=1, tiled=True),
    )
    return (
        outputs,
        input_grad,
        small_sums[0],
        matrix_sums[0],
        matrix_sums[1],
        matrix_sums[2],
        matrix_sums[3],
        matrix_sums[4],
        matrix_sums[5],
        small_sums[3],
        small_sums[4],
        small_sums[5],
        small_sums[6],
        small_sums[7],
        small_sums[2],
        matrix_sums[6],
        small_sums[1],
        matrix_sums[7],
        matrix_sums[8],
        matrix_sums[9],
    )


def solution(mesh):
    placed = (
        P("dp", None),
        P("dp", None),
        P(),
        P(None, "tensor"),
        P(None, "tensor"),
        P(None, "tensor"),
        P(None, "tensor"),
        P(None, "tensor"),
        P(None, "tensor"),
        P(None, "tensor"),
        P(None, "tensor"),
        P(None, "tensor"),
        P("tensor"),
        P("tensor"),
        P(),
        P("tensor", None),
        P(),
        P(None, "tensor"),
        P(None, "tensor"),
        P("tensor", None),
        P("dp", None),
    )
    return jax.shard_map(
        per_device,
        mesh=mesh,
        in_specs=placed,
        out_specs=(
            P("dp", None),
            P("dp", None),
            P(),
            P("dp", "tensor"),
            P("dp", "tensor"),
            P("dp", "tensor"),
            P("dp", "tensor"),
            P("dp", "tensor"),
            P("dp", "tensor"),
            P(None, "tensor"),
            P(None, "tensor"),
            P(None, "tensor"),
            P("tensor"),
            P("tensor"),
            P(),
            P("tensor", "dp"),
            P(),
            P("dp", "tensor"),
            P("dp", "tensor"),
            P("tensor", "dp"),
        ),
        check_vma=False,
    )
```

profile of v0, /device:TPU:24, one launch (start us, length us, event | category | flops | bytes accessed | tf_op | source)
XLA Modules:
  0.0 2335.8 jit_solution(12180955887018039735)
XLA Ops:
  35.4 223.4 %while.42 = (s32[]{:T(128)}, f32[2,128,256]{2,1,0:T(8,128)S(1)}, f32[12,2,64,256]{3,2,0,1:T(8,128)}, f32[12,2,128,256]{3,2,1,0:T(8,128)}, s32[12,2,64]{2,1,0:T(2...) while((s32[]{:T(128)}, f32[2,128,256]{2,1,0:T(8,128)S(1)}, ...), condition=%wide.region_5.7_spmd.clone, body=%wide.region_3.6_spmd.clone.sunk | while | flops 227254592 | bytes 3476217 | solution.py:87
  37.3 9.8 custom-call.25
  55.9 9.8 custom-call.25
  74.6 9.8 custom-call.25
  93.2 9.8 custom-call.25
  111.8 9.8 custom-call.25
  130.4 9.8 custom-call.25
  149.0 9.8 custom-call.25
  167.7 9.8 custom-call.25
  186.3 9.8 custom-call.25
  204.9 9.8 custom-call.25
  223.5 9.8 custom-call.25
  242.1 9.8 custom-call.25
  260.5 6.1 fusion.157
  275.1 6.3 fusion.257
  281.7 264.1 %all-reduce.42.cloned.1.call-done = f32[768,2048]{1,0:T(8,128)} async-done(((f32[768,2048]{1,0:T(8,128)}), f32[768,2048]{1,0:T(8,128)}) %all-reduce.42.cloned.1.call-update) | async-done | bytes 6291472 | tf_op jit(solution)/shard_map/psum | solution.py:233
  577.6 256.7 %all-reduce.44.cloned.1.call-done = f32[768,2048]{1,0:T(8,128)} async-done(((f32[768,2048]{1,0:T(8,128)}), f32[768,2048]{1,0:T(8,128)}) %all-reduce.44.cloned.1.call-update) | async-done | bytes 6291472 | tf_op jit(solution)/shard_map/psum | solution.py:252
  860.0 282.9 %while.43 = (s32[]{:T(128)}, f32[2,128,256]{2,1,0:T(8,128)S(1)}, f32[12,2,64,128]{3,2,0,1:T(8,128)}, f32[12,2,64,128]{3,2,0,1:T(8,128)S(1)}, f32[12,2,64,256]{3,...) while((s32[]{:T(128)}, f32[2,128,256]{2,1,0:T(8,128)S(1)}, ...), condition=%wide.region_24.26_spmd.clone, body=%wide.region_13.25_spmd.clone.sunk | while | flops 611922752 | bytes 10611043 | solution.py:87
  866.3 9.8 custom-call.26
  889.8 9.8 custom-call.26
  913.4 9.8 custom-call.26
  936.9 9.8 custom-call.26
  960.5 9.8 custom-call.26
  984.1 9.8 custom-call.26
  1007.6 9.8 custom-call.26
  1031.2 9.8 custom-call.26
  1054.8 9.8 custom-call.26
  1078.3 9.8 custom-call.26
  1101.9 9.8 custom-call.26
  1125.4 9.8 custom-call.26
  1192.8 14.5 add_add_fusion
  1216.1 7.1 fusion.266
  1223.3 7.1 fusion.265
  1230.4 7.1 fusion.264
  1237.6 6.8 fusion.153
  1244.7 6.0 fusion.263
  1250.8 5.9 fusion.201
  1264.8 20.6 psum.101
  1292.4 486.8 %all-reduce.46.cloned.1.call-done = (f32[768,2048]{1,0:T(8,128)}, f32[768,2048]{1,0:T(8,128)}) async-done(((f32[768,2048]{1,0:T(8,128)}, f32[768,2048]{1,0:T(8,128)}), (f32[768,2048]{1,0:T(8,128)}, f32[768,2048]{1,0:T(8,128)})) %all-reduce.46.cloned.1.call-update) | async-done | bytes 12582928 | tf_op jit(solution)/shard_map/psum | solution.py:242
  1783.8 55.0 %all-reduce.36 = (f32[2048]{0:T(1024)}, f32[4,256]{1,0:T(4,128)}, f32[4,256]{1,0:T(4,128)}, f32[4,512]{1,0:T(4,128)}, f32[2]{0:T(128)}, /*index=5*/f32[2]{0:T(128)}, f32[256]{0:T(256)}, f32[2048]{0:T(1024)}) all-reduce(f32[2048]{0:T(1024)S(1)} %get-tuple-element.716, ...), channel_id=1, replica_groups=mesh['dp'=16,'tensor'=8] {'dp'}, use_global_device_ids=true, to_apply=%region_30.32 | all-reduce | flops 8452 | bytes 67616 | tf_op jit(solution)/shard_map/psum | solution.py:281
  1838.8 14.2 fusion.123
  1853.0 57.4 %reduce-scatter.17.cloned.1.call-done = f32[128,256]{1,0:T(8,128)} async-done(((f32[2048,256]{1,0:T(8,128)}), f32[128,256]{1,0:T(8,128)}) %reduce-scatter.17.cloned.1.call-update) | async-done | bytes 131088 | tf_op jit(solution)/shard_map/reduce_scatter | solution.py:296
  1910.4 71.3 %reduce-scatter.27.cloned.1.call-done = f32[128,704]{0,1:T(8,128)} async-done(((f32[2048,704]{0,1:T(8,128)}), f32[128,704]{0,1:T(8,128)}) %reduce-scatter.27.cloned.1.call-update) | async-done | bytes 360464 | tf_op jit(solution)/shard_map/reduce_scatter | solution.py:303
  1981.7 71.3 %reduce-scatter.25.cloned.1.call-done = f32[128,704]{0,1:T(8,128)} async-done(((f32[2048,704]{0,1:T(8,128)}), f32[128,704]{0,1:T(8,128)}) %reduce-scatter.25.cloned.1.call-update) | async-done | bytes 360464 | tf_op jit(solution)/shard_map/reduce_scatter | solution.py:302
  2053.0 71.2 %reduce-scatter.29.cloned.1.call-done = f32[704,128]{1,0:T(8,128)} async-done(((f32[704,2048]{1,0:T(8,128)}), f32[704,128]{1,0:T(8,128)}) %reduce-scatter.29.cloned.1.call-update) | async-done | bytes 360464 | tf_op jit(solution)/shard_map/reduce_scatter | solution.py:304
  2124.2 68.3 %reduce-scatter.23.cloned.1.call-done = f32[512,128]{1,0:T(8,128)} async-done(((f32[512,2048]{1,0:T(8,128)}), f32[512,128]{1,0:T(8,128)}) %reduce-scatter.23.cloned.1.call-update) | async-done | bytes 262160 | tf_op jit(solution)/shard_map/reduce_scatter | solution.py:301
  2192.4 68.2 %reduce-scatter.21.cloned.1.call-done = f32[128,512]{1,0:T(8,128)} async-done(((f32[2048,512]{1,0:T(8,128)}), f32[128,512]{1,0:T(8,128)}) %reduce-scatter.21.cloned.1.call-update) | async-done | bytes 262160 | tf_op jit(solution)/shard_map/reduce_scatter | solution.py:298
  2260.7 68.4 %reduce-scatter.19.cloned.1.call-done = f32[128,512]{1,0:T(8,128)} async-done(((f32[2048,512]{1,0:T(8,128)}), f32[128,512]{1,0:T(8,128)}) %reduce-scatter.19.cloned.1.call-update) | async-done | bytes 262160 | tf_op jit(solution)/shard_map/reduce_scatter | solution.py:297
  (1044 shorter events, 440.1 us)
Async XLA Ops:
  7.2 552.7 %copy-start = (bf16[704,2048]{1,0:T(8,128)(2,1)S(1)}, bf16[704,2048]{1,0:T(8,128)(2,1)}, u32[]{:S(2)}) copy-start(bf16[704,2048]{1,0:T(8,128)(2,1)} %param.46) | copy-start | bytes 8650756
  7.2 5.8 copy-start.54
  7.2 5.8 copy-start.55
  7.2 6.0 copy-start.53
  7.2 6.0 copy-start.46
  7.2 538.6 %all-reduce.42.cloned.1.call-start = ((), (), s32[]{:S(2)}) async-start(), calls=%async_computation.10 | async-start | bytes 12582912 | tf_op jit(solution)/shard_map/psum | solution.py:233
  13.0 2.9 copy-start.48
  13.2 2.7 copy-start.50
  18.8 3.3 copy-start.3
  18.8 3.4 copy-start.43
  22.2 6.8 copy-start.20
  24.1 4.9 copy-start.22
  266.6 3.1 copy-start.52
  281.4 269.1 %copy-start.45 = (f32[2048]{0:T(1024)S(1)}, f32[2048]{0:T(1024)}, u32[]{:S(2)}) copy-start(f32[2048]{0:T(1024)} %param.43) | copy-start | bytes 24580
  281.4 552.9 %all-reduce.44.cloned.1.call-start = ((), (), s32[]{:S(2)}) async-start(), calls=%async_computation.11 | async-start | bytes 12582912 | tf_op jit(solution)/shard_map/psum | solution.py:252
  550.5 3.2 copy-start.5
  550.5 4.0 copy-start.57
  554.5 3.0 copy-start.35
  564.0 2.7 copy-start.59
  571.3 718.1 %reduce-scatter.31.cloned.1.call-start = ((), (), s32[]{:S(2)}) async-start(), calls=%async_computation.20 | async-start | bytes 1114112
  834.3 6.4 copy-start.13
  834.3 7.3 copy-start.31
  841.7 4.0 copy-start.36
  845.7 3.1 copy-start.6
  848.8 3.2 copy-start.7
  852.0 4.0 copy-start.12
  852.0 4.0 copy-start.19
  1146.9 3.9 copy-start.9
  1154.1 136.8 %reduce-scatter.33.cloned.1.call-start = ((), (), s32[]{:S(2)}) async-start(), calls=%async_computation.21 | async-start | bytes 1114112
  1155.8 4.6 copy-start.28
  1163.7 4.6 copy-start.33
  1163.7 4.6 copy-start.40
  1170.0 4.6 copy-start.24
  1184.5 3.6 copy-start.4
  1190.1 589.1 %all-reduce.46.cloned.1.call-start = ((), (), s32[]{:S(2)}) async-start(), calls=%async_computation.22 | async-start | bytes 25165824 | tf_op jit(solution)/shard_map/psum | solution.py:242
  1207.4 645.6 %reduce-scatter.15.cloned.1.call-start = ((), (), s32[]{:S(2)}) async-start(), calls=%async_computation.12 | async-start | bytes 2228224 | tf_op jit(solution)/shard_map/reduce_scatter | solution.py:295
  1211.7 698.6 %reduce-scatter.17.cloned.1.call-start = ((), (), s32[]{:S(2)}) async-start(), calls=%async_computation.13 | async-start | bytes 2228224 | tf_op jit(solution)/shard_map/reduce_scatter | solution.py:296
  1216.1 765.6 %reduce-scatter.27.cloned.1.call-start = ((), (), s32[]{:S(2)}) async-start(), calls=%async_computation.18 | async-start | bytes 6127616 | tf_op jit(solution)/shard_map/reduce_scatter | solution.py:303
  1223.2 829.8 %reduce-scatter.25.cloned.1.call-start = ((), (), s32[]{:S(2)}) async-start(), calls=%async_computation.17 | async-start | bytes 6127616 | tf_op jit(solution)/shard_map/reduce_scatter | solution.py:302
  1230.4 893.8 %reduce-scatter.29.cloned.1.call-start = ((), (), s32[]{:S(2)}) async-start(), calls=%async_computation.19 | async-start | bytes 6127616 | tf_op jit(solution)/shard_map/reduce_scatter | solution.py:304
  1237.6 954.8 %reduce-scatter.23.cloned.1.call-start = ((), (), s32[]{:S(2)}) async-start(), calls=%async_computation.16 | async-start | bytes 4456448 | tf_op jit(solution)/shard_map/reduce_scatter | solution.py:301
  1244.5 1016.2 %reduce-scatter.21.cloned.1.call-start = ((), (), s32[]{:S(2)}) async-start(), calls=%async_computation.15 | async-start | bytes 4456448 | tf_op jit(solution)/shard_map/reduce_scatter | solution.py:298
  1250.8 1078.3 %reduce-scatter.19.cloned.1.call-start = ((), (), s32[]{:S(2)}) async-start(), calls=%async_computation.14 | async-start | bytes 4456448 | tf_op jit(solution)/shard_map/reduce_scatter | solution.py:297
  1256.8 5.5 copy-start.18
  1285.4 3.1 copy-start.29
  1288.5 490.7 %copy-start.47 = (f32[2048]{0:T(1024)S(1)}, f32[2048]{0:T(1024)}, u32[]{:S(2)}) copy-start(f32[2048]{0:T(1024)} %param.29) | copy-start | bytes 24580
  1288.5 490.7 %copy-start.49 = (f32[768]{0:T(1024)S(1)}, f32[768]{0:T(1024)}, u32[]{:S(2)}) copy-start(f32[768]{0:T(1024)} %copy-done.48) | copy-start | bytes 9220
  1838.8 490.2 %copy-start.1 = (bf16[704,2048]{1,0:T(8,128)(2,1)S(1)}, bf16[704,2048]{1,0:T(8,128)(2,1)}, u32[]{:S(2)}) copy-start(bf16[704,2048]{1,0:T(8,128)(2,1)} %param.46) | copy-start | bytes 8650756
  (25 other events, 44.3 us)
Sparse Core Ops, SparseCore 0:
  281.5 264.2 all-reduce.41
  571.4 262.8 all-reduce.43
  1154.2 61.3 reduce-scatter.30
  1217.9 60.0 reduce-scatter.32
  1280.4 498.7 all-reduce.45
  1782.0 63.3 reduce-scatter.14
  1848.4 61.9 reduce-scatter.16
  1913.4 68.2 reduce-scatter.26
  1984.7 68.2 reduce-scatter.24
  2055.8 68.2 reduce-scatter.28
  2127.1 65.2 reduce-scatter.22
  2195.3 65.3 reduce-scatter.20
  2263.7 65.3 reduce-scatter.18
where the time goes:
time: 2350 us; the launch traced here: 2340 us
  waiting for transfers between devices  1480 us (63%)
  other arithmetic  344 us (15%)
  matrix products  317 us (13%)
  local copies, waits for them, and re-layouts  94.1 us (4%)
  blocking collectives  75.6 us (3%)
    psum x1, waiting for transfers between devices, per_device(): ffn_total = lax.psum(matmul(inner, w_down), 'tensor')  487 us
    psum x1, waiting for transfers between devices, per_device(): attn_total = lax.psum(matmul(mixed_low, w_out), 'tensor')  264 us
    psum x1, waiting for transfers between devices, per_device(): lax.psum(matmul(grad_gate_pre, w_up_gate.T) + matmul(grad_up_pre, w_up.T)...  257 us
    another operation x96, other arithmetic, block_step(): jax.scipy.linalg.solve_triangular(ident_mat + strict, target_value, lower...  240 us
    dot_general x28, matrix products, matmul(): return jnp.dot(left, right, preferred_element_type=jnp.float32)  129 us
    reduce_scatter x1, waiting for transfers between devices, per_device(): lax.psum_scatter(grad_up_gate, 'dp', scatter_dimension=0, tiled=True)  71.3 us
    reduce_scatter x1, waiting for transfers between devices, per_device(): lax.psum_scatter(grad_up, 'dp', scatter_dimension=0, tiled=True)  71.3 us
    reduce_scatter x1, waiting for transfers between devices, per_device(): lax.psum_scatter(grad_down, 'dp', scatter_dimension=1, tiled=True)  71.2 us
  transfers between devices with their start and end apart: 13, of which 10 were waited for; matrix products, arithmetic and copies ran while one was open for 6% of the time, Pallas kernels for 0%

commit v1 on v0

v1 whole, which is shorter than its diff:
```python
import functools
import jax, jax.numpy as jnp
from jax import lax
from jax.experimental import pallas as pl
from jax.experimental.pallas import tpu as pltpu
from jax.sharding import PartitionSpec as P

F32 = jnp.float32
BF16 = jnp.bfloat16
L = 128
PAD = 8
NN = (((1,), (0,)), ((), ()))
NT = (((1,), (1,)), ((), ()))
TN = (((0,), (0,)), ((), ()))


def split(x):
    hi = x.astype(BF16)
    return hi, (x - hi.astype(F32)).astype(BF16)


def mm1(a, b, dims):
    return lax.dot_general(a, b, dims, preferred_element_type=F32)


def mm3(a, b, dims=NN):
    return mm1(a[0], b[0], dims) + (mm1(a[0], b[1], dims) + mm1(a[1], b[0], dims))


def sigmoid(x):
    return 1.0 / (1.0 + jnp.exp(-x))


def rows(ref, b, n=L, lead=0):
    return ref[pl.ds(pl.multiple_of(b * L, L) + lead, n)]


def decay_tile(ba, rate, bias):
    lane = lax.broadcasted_iota(jnp.int32, ba.shape, 1)
    shifted = ba + bias
    soft = jnp.maximum(shifted, 0.0) + jnp.log1p(jnp.exp(-jnp.abs(shifted)))
    return jnp.where(lane < 2, sigmoid(ba), rate * soft)


def tri_sum(tile, dims):
    r = lax.broadcasted_iota(jnp.int32, (L, L), 0)
    c = lax.broadcasted_iota(jnp.int32, (L, L), 1)
    tri = (r >= c).astype(BF16)
    p0 = tile.astype(BF16)
    rest = tile - p0.astype(F32)
    p1 = rest.astype(BF16)
    p2 = (rest - p1.astype(F32)).astype(BF16)
    return mm1(tri, p0, dims) + (mm1(tri, p1, dims) + mm1(tri, p2, dims))


def block_decay(b, seg_ref, ba_ref, rate, bias):
    tile = decay_tile(rows(ba_ref, b), rate, bias)
    cum = tri_sum(tile, NN)
    lane = lax.broadcasted_iota(jnp.int32, (L, L), 1)
    both = jnp.where(lane < 2, tile, cum)
    flat = both.T
    seg_row = seg_ref[b, 0:1, :]
    seg_col = jnp.broadcast_to(seg_row, (L, L)).T
    prev = seg_ref[b, 1:2, 0:1]
    r = lax.broadcasted_iota(jnp.int32, (L, L), 0)
    keep = (seg_col == seg_row) & (r >= lane)
    strict_keep = r > lane
    carry_keep = seg_col[:, 0:1] == prev
    out = []
    for h in range(2):
        c_col = cum[:, 2 + h:3 + h]
        c_row = flat[2 + h:3 + h, :]
        beta_row = flat[h:h + 1, :]
        decay = jnp.where(keep, jnp.exp(jnp.where(keep, c_col - c_row, 0.0)), 0.0)
        carry = jnp.where(carry_keep, jnp.exp(c_col), 0.0)
        last_keep = seg_col[:, 0:1] == seg_row[:, L - 1:L]
        last_decay = jnp.where(last_keep, jnp.exp(jnp.where(last_keep, c_col[L - 1:L, :] - c_col, 0.0)), 0.0)
        beta_col = tile[:, h:h + 1]
        out.append((decay, carry, beta_row, beta_col, last_decay))
    return out, strict_keep, (tile, seg_col)


def conv_block(b, pre_ref, taps_ref, seg_ref, cols, segpad_ref):
    base = pl.multiple_of(b * L, L)
    z = pre_ref[pl.ds(base, L + PAD), cols]
    s = segpad_ref[pl.ds(base, L + PAD), 0:1]
    total = z[PAD:] * taps_ref[0:1, cols]
    for k in range(1, 4):
        same = (s[PAD - k:PAD - k + L] == s[PAD:]).astype(F32)
        total = total + z[PAD - k:PAD - k + L] * same * taps_ref[k:k + 1, cols]
    return total


def inverse_many(mats):
    r = lax.broadcasted_iota(jnp.int32, (L, L), 0)
    c = lax.broadcasted_iota(jnp.int32, (L, L), 1)
    eye = (r == c).astype(F32)
    xs = [eye - jnp.where((r // 2 == c // 2), a, 0.0) for a in mats]
    s = 2
    while s < L:
        pick = (r // (2 * s) == c // (2 * s)) & (r // s != c // s)
        sx = [split(x) for x in xs]
        sa = [split(jnp.where(pick, a, 0.0)) for a in mats]
        t = [mm3(x, a) for x, a in zip(sx, sa)]
        xs = [x - mm3(split(y), z) for x, y, z in zip(xs, t, sx)]
        s *= 2
    return xs


def fwd_kernel(blocks, group, seg_ref, qp_ref, kp_ref, vp_ref, gp_ref, ba_ref, cq_ref, ck_ref, cv_ref, rate_ref, bias_ref, gain_ref,
               low_ref, q_ref, k_ref, x_ref, u_ref, s_ref, o_ref,
               qpad, kpad, vpad, segpad, w_s, u0_s, kw_s):
    T = blocks * L
    rate, bias = rate_ref[0:1, :], bias_ref[0:1, :]
    for pad, src in ((qpad, qp_ref), (kpad, kp_ref), (vpad, vp_ref)):
        pad[0:PAD, :] = jnp.zeros((PAD, pad.shape[1]), F32)
        pad[PAD:PAD + T, :] = src[...]
    segpad[0:PAD, :] = jnp.full((PAD, L), -1.0, F32)
    for b in range(blocks):
        segpad[PAD + b * L:PAD + (b + 1) * L, :] = jnp.broadcast_to(seg_ref[b, 0:1, :], (L, L)).T

    def phase_a(g, _):
        a_mats, keepers = [], []
        for i in range(group):
            b = g * group + i
            base = pl.multiple_of(b * L, L)
            per_head, strict_keep, _u = block_decay(b, seg_ref, ba_ref, rate, bias)
            for h in range(2):
                decay, carry, beta_row, beta_col, last_decay = per_head[h]
                kc = slice(h * 128, h * 128 + 128)
                vc = slice(h * 256, h * 256 + 256)
                y = conv_block(b, qpad, cq_ref, seg_ref, kc, segpad)
                q = y * sigmoid(y)
                q = q * (lax.rsqrt(jnp.sum(q * q, axis=-1, keepdims=True) + 1e-06) * (128 ** -0.5))
                y = conv_block(b, kpad, ck_ref, seg_ref, kc, segpad)
                k = y * sigmoid(y)
                k = k * lax.rsqrt(jnp.sum(k * k, axis=-1, keepdims=True) + 1e-06)
                q_ref[pl.ds(base, L), kc] = q
                k_ref[pl.ds(base, L), kc] = k
                y = conv_block(b, vpad, cv_ref, seg_ref, vc, segpad)
                v = y * sigmoid(y)
                ks = split(k)
                kk = mm3(ks, ks, NT)
                a_mats.append(jnp.where(strict_keep, decay, 0.0) * kk * beta_row)
                kw_s[pl.ds(base, L), kc] = k * (last_decay * beta_col)
                keepers.append((b, base, h, kc, vc, v, k * carry))
        xs = inverse_many(a_mats)
        for x, (b, base, h, kc, vc, v, gk) in zip(xs, keepers):
            x_ref[pl.ds(base, L), kc] = x
            sx = split(x)
            u0_s[pl.ds(base, L), vc] = mm3(sx, split(v))
            w_s[pl.ds(base, L), kc] = mm3(sx, split(gk))
        return 0

    lax.fori_loop(0, blocks // group, phase_a, 0)

    def phase_b(b, state):
        base = pl.multiple_of(b * L, L)
        per_head, strict_keep, _u = block_decay(b, seg_ref, ba_ref, rate, bias)
        new = []
        for h in range(2):
            decay, carry, beta_row, beta_col, last_decay = per_head[h]
            kc = slice(h * 128, h * 128 + 128)
            vc = slice(h * 256, h * 256 + 256)
            s = state[h]
            s_ref[pl.ds(base, L), vc] = s
            ss = split(s)
            u = u0_s[pl.ds(base, L), vc] - mm3(split(w_s[pl.ds(base, L), kc]), ss)
            u_ref[pl.ds(base, L), vc] = u
            new.append(carry[L - 1:L, :] * s + mm3(split(kw_s[pl.ds(base, L), kc]), split(u), TN))
        return tuple(new)

    zero = jnp.zeros((128, 256), F32)
    lax.fori_loop(0, blocks, phase_b, (zero, zero))

    def phase_c(b, _):
        base = pl.multiple_of(b * L, L)
        per_head, strict_keep, _u = block_decay(b, seg_ref, ba_ref, rate, bias)
        for h in range(2):
            decay, carry, beta_row, beta_col, last_decay = per_head[h]
            kc = slice(h * 128, h * 128 + 128)
            vc = slice(h * 256, h * 256 + 256)
            q = q_ref[pl.ds(base, L), kc]
            qk = mm3(split(q), split(k_ref[pl.ds(base, L), kc]), NT)
            p = decay * qk * beta_row
            o = mm3(split(q * carry), split(s_ref[pl.ds(base, L), vc])) + mm3(split(p), split(u_ref[pl.ds(base, L), vc]))
            o_ref[pl.ds(base, L), vc] = o
            gp = gp_ref[pl.ds(base, L), vc]
            n = o * lax.rsqrt(jnp.mean(o * o, axis=-1, keepdims=True) + 1e-05)
            low_ref[pl.ds(base, L), vc] = (n * gain_ref[0:1, :] * (gp * sigmoid(gp))).astype(BF16)
        return 0

    lax.fori_loop(0, blocks, phase_c, 0)


VM = pl.BlockSpec(memory_space=pltpu.VMEM)


def mixer_fwd(seg3, qp, kp, vp, gp, ba, cq, ck, cv, rate, bias, gain, group=2):
    T = qp.shape[0]
    blocks = T // L
    sd = jax.ShapeDtypeStruct
    return pl.pallas_call(
        functools.partial(fwd_kernel, blocks, group),
        out_shape=(sd((T, 512), BF16), sd((T, 256), F32), sd((T, 256), F32), sd((T, 256), F32), sd((T, 512), F32),
                   sd((T, 512), F32), sd((T, 512), F32)),
        in_specs=[VM] * 12, out_specs=[VM] * 7,
        scratch_shapes=[pltpu.VMEM((T + PAD, 256), F32), pltpu.VMEM((T + PAD, 256), F32), pltpu.VMEM((T + PAD, 512), F32),
                        pltpu.VMEM((T + PAD, L), F32), pltpu.VMEM((T, 256), F32), pltpu.VMEM((T, 512), F32), pltpu.VMEM((T, 256), F32)],
        compiler_params=pltpu.CompilerParams(vmem_limit_bytes=56 * 2 ** 20),
        name="mixer_forward",
    )(seg3, qp, kp, vp, gp, ba, cq, ck, cv, rate, bias, gain)


def bwd_kernel(blocks, seg_ref, gm_ref, qp_ref, kp_ref, vp_ref, gp_ref, ba_ref, cq_ref, ck_ref, cv_ref, rate_ref, bias_ref, gain_ref,
               q_ref, k_ref, x_ref, u_ref, s_ref, o_ref,
               dqp_ref, dkp_ref, dvp_ref, dgp_ref, dba_ref, dtap_ref, dsmall_ref, dgain_ref,
               qpad, kpad, vpad, segpad, do_s, y0_s, z_s, r_s, y_s, ds_s, dq_s, dk_s, dv_s, acc_s):
    T = blocks * L
    rate, bias = rate_ref[0:1, :], bias_ref[0:1, :]
    for pad, src in ((qpad, qp_ref), (kpad, kp_ref), (vpad, vp_ref)):
        pad[0:PAD, :] = jnp.zeros((PAD, pad.shape[1]), F32)
        pad[PAD:PAD + T, :] = src[...]
    segpad[0:PAD, :] = jnp.full((PAD, L), -1.0, F32)
    segpad[PAD + T:, :] = jnp.full((PAD, L), -1.0, F32)
    for b in range(blocks):
        segpad[PAD + b * L:PAD + (b + 1) * L, :] = jnp.broadcast_to(seg_ref[b, 0:1, :], (L, L)).T
    dgain_ref[...] = jnp.zeros_like(dgain_ref)
    dsmall_ref[...] = jnp.zeros_like(dsmall_ref)
    dtap_ref[...] = jnp.zeros_like(dtap_ref)

    def phase_1(b, _):
        base = pl.multiple_of(b * L, L)
        per_head, strict_keep, _u = block_decay(b, seg_ref, ba_ref, rate, bias)
        for h in range(2):
            decay, carry, beta_row, beta_col, last_decay = per_head[h]
            kc = slice(h * 128, h * 128 + 128)
            vc = slice(h * 256, h * 256 + 256)
            o = o_ref[pl.ds(base, L), vc]
            gp = gp_ref[pl.ds(base, L), vc]
            gm = gm_ref[pl.ds(base, L), vc]
            gain = gain_ref[0:1, :]
            sg = sigmoid(gp)
            r = lax.rsqrt(jnp.mean(o * o, axis=-1, keepdims=True) + 1e-05)
            n = o * r
            act = gp * sg
            gn = gm * n
            dgain_ref[0:1, :] = dgain_ref[0:1, :] + jnp.sum(gn * act, axis=0, keepdims=True)
            dgp_ref[pl.ds(base, L), vc] = (gn * gain * (sg * (1.0 + gp * (1.0 - sg)))).astype(BF16)
            dn = gm * gain * act
            do = r * (dn - n * jnp.mean(dn * n, axis=-1, keepdims=True))
            do_s[pl.ds(base, L), vc] = do
            q, k = q_ref[pl.ds(base, L), kc], k_ref[pl.ds(base, L), kc]
            p = decay * mm3(split(q), split(k), NT) * beta_row
            sdo = split(do)
            sx = split(x_ref[pl.ds(base, L), kc])
            y0 = mm3(sx, split(mm3(split(p), sdo, TN)), TN)
            z = mm3(sx, split(k * (last_decay * beta_col)), TN)
            y0_s[pl.ds(base, L), vc] = y0
            z_s[pl.ds(base, L), kc] = z
            r_s[pl.ds(base, L), vc] = mm3(split(q * carry), sdo, TN)
        return 0

    lax.fori_loop(0, blocks, phase_1, 0)

    def phase_2(i, grads):
        b = blocks - 1 - i
        base = pl.multiple_of(b * L, L)
        per_head, strict_keep, _u = block_decay(b, seg_ref, ba_ref, rate, bias)
        new = []
        for h in range(2):
            decay, carry, beta_row, beta_col, last_decay = per_head[h]
            kc = slice(h * 128, h * 128 + 128)
            vc = slice(h * 256, h * 256 + 256)
            ds = grads[h]
            ds_s[pl.ds(base, L), vc] = ds
            y = y0_s[pl.ds(base, L), vc] + mm3(split(z_s[pl.ds(base, L), kc]), split(ds))
            y_s[pl.ds(base, L), vc] = y
            new.append(carry[L - 1:L, :] * ds + r_s[pl.ds(base, L), vc]
                       - mm3(split(k_ref[pl.ds(base, L), kc] * carry), split(y), TN))
        return tuple(new)

    zero = jnp.zeros((128, 256), F32)
    lax.fori_loop(0, blocks, phase_2, (zero, zero))

    def phase_3(b, _):
        base = pl.multiple_of(b * L, L)
        per_head, strict_keep, (tile, seg_col) = block_decay(b, seg_ref, ba_ref, rate, bias)
        lane = lax.broadcasted_iota(jnp.int32, (L, L), 1)
        rowi = lax.broadcasted_iota(jnp.int32, (L, L), 0)
        row_tile = jnp.zeros((L, L), F32)
        col_tile = jnp.zeros((L, L), F32)
        for h in range(2):
            decay, carry, beta_row, beta_col, last_decay = per_head[h]
            kc = slice(h * 128, h * 128 + 128)
            vc = slice(h * 256, h * 256 + 256)
            q, k = q_ref[pl.ds(base, L), kc], k_ref[pl.ds(base, L), kc]
            sq, sk = split(q), split(k)
            kk = mm3(sk, sk, NT)
            qk = mm3(sq, sk, NT)
            s, u = s_ref[pl.ds(base, L), vc], u_ref[pl.ds(base, L), vc]
            do, y, ds = do_s[pl.ds(base, L), vc], y_s[pl.ds(base, L), vc], ds_s[pl.ds(base, L), vc]
            ss, su, sdo, sy, sds = split(s), split(u), split(do), split(y), split(ds)
            do_st = mm3(sdo, ss, NT)
            y_st = mm3(sy, ss, NT)
            u_dst = mm3(su, sds, NT)
            dp = mm3(sdo, su, NT)
            da = -mm3(sy, su, NT)
            dcarry = jnp.sum(q * do_st - k * y_st, axis=-1, keepdims=True)
            dcarry_last = jnp.sum(jnp.sum(ds * s, axis=0, keepdims=True), axis=1, keepdims=True)
            dw = jnp.sum(u_dst * k, axis=-1, keepdims=True)
            dpd = dp * decay
            dad = jnp.where(strict_keep, da * decay, 0.0)
            dqk = dpd * beta_row
            dkk = dad * beta_row
            prod = dpd * qk + dad * kk
            dbeta_row = jnp.sum(prod, axis=0, keepdims=True)
            dec_grad = prod * beta_row
            dc_col = jnp.sum(dec_grad, axis=1, keepdims=True) + dcarry * carry
            dc_row = -jnp.sum(dec_grad, axis=0, keepdims=True)
            dlast = dw * beta_col * last_decay
            row1 = rowi[:, 0:1]
            dc_col = dc_col - dlast
            dc_col = dc_col + jnp.where(row1 == L - 1, jnp.sum(dlast, axis=0, keepdims=True) + dcarry_last * carry, 0.0)
            dbeta_col = dw * last_decay
            row_tile = row_tile + jnp.where(rowi == h, dbeta_row, 0.0) + jnp.where(rowi == 2 + h, dc_row, 0.0)
            col_tile = col_tile + jnp.where(lane == h, dbeta_col, 0.0) + jnp.where(lane == 2 + h, dc_col, 0.0)
            sdqk, sdkk = split(dqk), split(dkk + dkk.T)
            dq_s[pl.ds(base, L), kc] = carry * do_st + mm3(sdqk, sk)
            dk_s[pl.ds(base, L), kc] = (mm3(sdqk, sq, TN) + mm3(sdkk, sk) - carry * y_st
                                        + (last_decay * beta_col) * u_dst)
        grad = col_tile + row_tile.T
        dld = tri_sum(grad, TN)
        ba = rows(ba_ref, b)
        sig_alpha = sigmoid(ba + bias)
        dalpha = dld * rate * sig_alpha
        dpre = jnp.where(lane < 2, grad * tile * (1.0 - tile), jnp.where(lane < 4, dalpha, 0.0))
        dba_ref[pl.ds(base, L), :] = dpre.astype(BF16)
        dsmall_ref[0:1, :] = dsmall_ref[0:1, :] + jnp.sum(dpre, axis=0, keepdims=True)
        dsmall_ref[1:2, :] = dsmall_ref[1:2, :] + jnp.sum(dld * tile, axis=0, keepdims=True)
        return 0

    lax.fori_loop(0, blocks, phase_3, 0)

    def conv_back(pre, taps_ref, src, out_ref, cols, tap_cols, scale):
        acc_s[T:, cols] = jnp.zeros((PAD, 128), F32)

        def one(b, tap_grads):
            base = pl.multiple_of(b * L, L)
            y = conv_block(b, pre, taps_ref, None, cols, segpad)
            sg = sigmoid(y)
            act = y * sg
            d = src[pl.ds(base, L), cols]
            if scale is not None:
                r = lax.rsqrt(jnp.sum(act * act, axis=-1, keepdims=True) + 1e-06)
                d = (scale * r) * (d - act * (r * r * jnp.sum(d * act, axis=-1, keepdims=True)))
            dy = d * (sg * (1.0 + y * (1.0 - sg)))
            acc_s[pl.ds(base, L), cols] = dy
            z = pre[pl.ds(base, L + PAD), cols]
            s = segpad[pl.ds(base, L + PAD), 0:1]
            new = [tap_grads[0] + jnp.sum(dy * z[PAD:], axis=0, keepdims=True)]
            for t in range(1, 4):
                same = (s[PAD - t:PAD - t + L] == s[PAD:]).astype(F32)
                new.append(tap_grads[t] + jnp.sum(dy * (z[PAD - t:PAD - t + L] * same), axis=0, keepdims=True))
            return tuple(new)

        zero = jnp.zeros((1, 128), F32)
        res = lax.fori_loop(0, blocks, one, (zero,) * 4)
        for t in range(4):
            dtap_ref[t:t + 1, tap_cols] = res[t]

        def two(b, _):
            base = pl.multiple_of(b * L, L)
            dy = acc_s[pl.ds(base, L + PAD), cols]
            s = segpad[pl.ds(base + PAD, L + PAD), 0:1]
            total = dy[:L] * taps_ref[0:1, cols]
            for t in range(1, 4):
                same = (s[t:t + L] == s[:L]).astype(F32)
                total = total + dy[t:t + L] * same * taps_ref[t:t + 1, cols]
            out_ref[pl.ds(base, L), cols] = total.astype(BF16)
            return 0

        lax.fori_loop(0, blocks, two, 0)

    for h in range(2):
        c = slice(h * 128, h * 128 + 128)
        conv_back(qpad, cq_ref, dq_s, dqp_ref, c, slice(h * 128, h * 128 + 128), 128 ** -0.5)
        conv_back(kpad, ck_ref, dk_s, dkp_ref, c, slice(256 + h * 128, 256 + h * 128 + 128), 1.0)
    for j in range(4):
        c = slice(j * 128, j * 128 + 128)
        conv_back(vpad, cv_ref, y_s, dvp_ref, c, slice(512 + j * 128, 512 + j * 128 + 128), None)


def mixer_bwd(seg3, gm, qp, kp, vp, gp, ba, cq, ck, cv, rate, bias, gain, q, k, x, u, s, o):
    T = qp.shape[0]
    blocks = T // L
    sd = jax.ShapeDtypeStruct
    vm = lambda n, w: pltpu.VMEM((n, w), F32)
    return pl.pallas_call(
        functools.partial(bwd_kernel, blocks),
        out_shape=(sd((T, 256), BF16), sd((T, 256), BF16), sd((T, 512), BF16), sd((T, 512), BF16), sd((T, 128), BF16),
                   sd((8, 1024), F32), sd((8, 128), F32), sd((8, 256), F32)),
        in_specs=[VM] * 19, out_specs=[VM] * 8,
        scratch_shapes=[vm(T + PAD, 256), vm(T + PAD, 256), vm(T + PAD, 512), vm(T + 2 * PAD, L),
                        vm(T, 512), vm(T, 512), vm(T, 256), vm(T, 512), vm(T, 512), vm(T, 512), vm(T, 256), vm(T, 256), vm(8, 128), vm(T + PAD, 512)],
        compiler_params=pltpu.CompilerParams(vmem_limit_bytes=56 * 2 ** 20),
        name="mixer_backward",
    )(seg3, gm, qp, kp, vp, gp, ba, cq, ck, cv, rate, bias, gain, q, k, x, u, s, o)


MESH = pl.DeviceIdType.MESH
N_TENSOR = 8


def tensor_peers():
    d, t = lax.axis_index("dp"), lax.axis_index("tensor")
    return d, t, [lax.rem(t + j, N_TENSOR) for j in range(1, N_TENSOR)]


def greet(d, peers):
    barrier = pltpu.get_barrier_semaphore()
    for p in peers:
        pl.semaphore_signal(barrier, inc=1, device_id=(d, p), device_id_type=MESH)
    pl.semaphore_wait(barrier, len(peers))


def scatter_copies(d, peers, send, recv, ssem, rsem, own):
    return [
        pltpu.make_async_remote_copy(
            src_ref=send.at[pl.ds(pl.multiple_of(p * own, own), own)], dst_ref=recv.at[j],
            send_sem=ssem.at[j], recv_sem=rsem.at[j], device_id=(d, p), device_id_type=MESH)
        for j, p in enumerate(peers)]


def gather_copies(d, peers, shard, recv, ssem, rsem):
    return [
        pltpu.make_async_remote_copy(
            src_ref=shard, dst_ref=recv.at[j],
            send_sem=ssem.at[j], recv_sem=rsem.at[j], device_id=(d, p), device_id_type=MESH)
        for j, p in enumerate(peers)]


def summed(send, recv, t, own, r0, n):
    total = send[pl.ds(pl.multiple_of(t * own + r0, 8), n), :]
    for j in range(N_TENSOR - 1):
        total = total + recv[j, pl.ds(r0, n), :]
    return total


def gathered_out(t, shard, recv, out_ref, copies, own):
    out_ref[pl.ds(pl.multiple_of(t * own, own), own), :] = shard[...].astype(out_ref.dtype)
    for j in range(N_TENSOR - 1):
        copies[j].wait_recv()
        source = lax.rem(t + N_TENSOR - 1 - j, N_TENSOR)
        out_ref[pl.ds(pl.multiple_of(source * own, own), own), :] = recv[j].astype(out_ref.dtype)


def attn_kernel(low_ref, w_ref, x_ref, gain_ref, hid_ref, resid_ref,
                send, recv, shard, grecv, xown, csem, s1, r1, s2, r2):
    d, t, peers = tensor_peers()
    own = resid_ref.shape[0]
    mine = pltpu.make_async_copy(x_ref.at[pl.ds(pl.multiple_of(t * own, own), own)], xown, csem)
    mine.start()

    def partial(n, _):
        cols = pl.ds(pl.multiple_of(n * 256, 256), 256)
        send[:, cols] = mm1(low_ref[...], w_ref[:, cols], NN)
        return 0

    lax.fori_loop(0, send.shape[1] // 256, partial, 0)
    greet(d, peers)
    copies = scatter_copies(d, peers, send, recv, s1, r1, own)
    for c in copies:
        c.start()
    mine.wait()
    for c in copies:
        c.wait_recv()

    def finish(i, _):
        r0 = pl.multiple_of(i * 16, 16)
        resid = xown[pl.ds(r0, 16), :].astype(F32) + summed(send, recv, t, own, r0, 16)
        resid_ref[pl.ds(r0, 16), :] = resid
        n = resid * lax.rsqrt(jnp.mean(resid * resid, axis=-1, keepdims=True) + 1e-05)
        shard[pl.ds(r0, 16), :] = (n * gain_ref[0:1, :]).astype(BF16).astype(F32)
        return 0

    lax.fori_loop(0, own // 16, finish, 0)
    back = gather_copies(d, peers, shard, grecv, s2, r2)
    for c in back:
        c.start()
    gathered_out(t, shard, grecv, hid_ref, back, own)
    for c in copies + back:
        c.wait_send()


def dma_sems(*counts):
    return [pltpu.SemaphoreType.DMA((n,)) for n in counts]


ANY = pl.BlockSpec(memory_space=pl.ANY)


def attn_exchange(low, w_out, inputs, gain):
    T, D = inputs.shape
    own = T // N_TENSOR
    sd = jax.ShapeDtypeStruct
    return pl.pallas_call(
        attn_kernel,
        out_shape=(sd((T, D), BF16), sd((own, D), F32)),
        in_specs=[VM, VM, ANY, VM], out_specs=[VM, VM],
        scratch_shapes=[pltpu.VMEM((T, D), F32), pltpu.VMEM((7, own, D), F32), pltpu.VMEM((own, D), F32),
                        pltpu.VMEM((7, own, D), F32), pltpu.VMEM((own, D), BF16), pltpu.SemaphoreType.DMA(())] + dma_sems(7, 7, 7, 7),
        compiler_params=pltpu.CompilerParams(collective_id=1, has_side_effects=True, vmem_limit_bytes=56 * 2 ** 20),
        name="attn_exchange",
    )(low, w_out, inputs, gain)


def mid_kernel(gg_ref, gu_ref, wg_ref, wu_ref, ffn_ref, resid_in, og_ref, gain_ref,
               ga_ref, gres_ref, dgain_ref, out_ref,
               send, recv, shard, grecv, ogown, oshard, orecv, csem, s1, r1, s2, r2, s3, r3, s4, r4):
    d, t, peers = tensor_peers()
    own = gres_ref.shape[0]
    rows_t = pl.ds(pl.multiple_of(t * own, own), own)
    mine = pltpu.make_async_copy(og_ref.at[rows_t], ogown, csem.at[0])
    mine.start()
    ffn_own = pltpu.make_async_copy(ffn_ref.at[rows_t], oshard, csem.at[1])
    ffn_own.start()

    def partial(n, _):
        cols = pl.ds(pl.multiple_of(n * 256, 256), 256)
        send[:, cols] = mm1(gg_ref[...], wg_ref[cols, :], NT) + mm1(gu_ref[...], wu_ref[cols, :], NT)
        return 0

    lax.fori_loop(0, send.shape[1] // 256, partial, 0)
    greet(d, peers)
    copies = scatter_copies(d, peers, send, recv, s1, r1, own)
    copies2 = scatter_copies(d, peers, ffn_ref, orecv, s3, r3, own)
    for c in copies:
        c.start()
    for c in copies2:
        c.start()
    mine.wait()
    for c in copies:
        c.wait_recv()
    dgain_ref[...] = jnp.zeros_like(dgain_ref)

    def finish(i, _):
        r0 = pl.multiple_of(i * 16, 16)
        resid = resid_in[pl.ds(r0, 16), :]
        back = summed(send, recv, t, own, r0, 16)
        scale = lax.rsqrt(jnp.mean(resid * resid, axis=-1, keepdims=True) + 1e-05)
        n = resid * scale
        bn = back * n
        dgain_ref[...] = dgain_ref[...] + bn[0:8] + bn[8:16]
        b = back * gain_ref[0:1, :]
        g = ogown[pl.ds(r0, 16), :].astype(F32) + scale * (b - n * jnp.mean(b * n, axis=-1, keepdims=True))
        gres_ref[pl.ds(r0, 16), :] = g
        shard[pl.ds(r0, 16), :] = g.astype(BF16).astype(F32)
        return 0

    lax.fori_loop(0, own // 16, finish, 0)
    back = gather_copies(d, peers, shard, grecv, s2, r2)
    for c in back:
        c.start()
    for c in copies2:
        c.wait_recv()
    ffn_own.wait()

    def finish2(i, _):
        r0 = pl.multiple_of(i * 16, 16)
        total = oshard[pl.ds(r0, 16), :]
        for j in range(N_TENSOR - 1):
            total = total + orecv[j, pl.ds(r0, 16), :]
        oshard[pl.ds(r0, 16), :] = (resid_in[pl.ds(r0, 16), :] + total).astype(BF16).astype(F32)
        return 0

    lax.fori_loop(0, own // 16, finish2, 0)
    back2 = [
        pltpu.make_async_remote_copy(
            src_ref=oshard, dst_ref=out_ref.at[rows_t],
            send_sem=s4.at[j], recv_sem=r4.at[j], device_id=(d, p), device_id_type=MESH)
        for j, p in enumerate(peers)]
    for c in back2:
        c.start()
    own_out = pltpu.make_async_copy(oshard, out_ref.at[rows_t], csem.at[2])
    own_out.start()
    gathered_out(t, shard, grecv, ga_ref, back, own)
    for c in back2:
        c.wait_recv()
    own_out.wait()
    for c in copies + back + copies2 + back2:
        c.wait_send()


def mid_exchange(gg, gu, wg, wu, ffn, resid, og, gain):
    T, D = og.shape
    own = T // N_TENSOR
    sd = jax.ShapeDtypeStruct
    return pl.pallas_call(
        mid_kernel,
        out_shape=(sd((T, D), BF16), sd((own, D), F32), sd((8, D), F32), sd((T, D), F32)),
        in_specs=[VM, VM, VM, VM, ANY, VM, ANY, VM], out_specs=[VM, VM, VM, ANY],
        scratch_shapes=[pltpu.VMEM((T, D), F32), pltpu.VMEM((7, own, D), F32), pltpu.VMEM((own, D), F32),
                        pltpu.VMEM((7, own, D), F32), pltpu.VMEM((own, D), BF16), pltpu.VMEM((own, D), F32), pltpu.VMEM((7, own, D), F32),
                        pltpu.SemaphoreType.DMA((3,))] + dma_sems(7, 7, 7, 7, 7, 7, 7, 7),
        compiler_params=pltpu.CompilerParams(collective_id=2, has_side_effects=True, vmem_limit_bytes=58 * 2 ** 20),
        name="mid_exchange",
    )(gg, gu, wg, wu, ffn, resid, og, gain)


def in_kernel(part_ref, gres_ref, x_ref, gain_ref, ig_ref, dgain_ref,
              recv, shard, grecv, xown, pown, csem, s1, r1, s2, r2):
    d, t, peers = tensor_peers()
    own = gres_ref.shape[0]
    rows_t = pl.ds(pl.multiple_of(t * own, own), own)
    mine = pltpu.make_async_copy(x_ref.at[rows_t], xown, csem.at[0])
    mine.start()
    mine2 = pltpu.make_async_copy(part_ref.at[rows_t], pown, csem.at[1])
    mine2.start()
    greet(d, peers)
    copies = scatter_copies(d, peers, part_ref, recv, s1, r1, own)
    for c in copies:
        c.start()
    mine.wait()
    mine2.wait()
    for c in copies:
        c.wait_recv()
    dgain_ref[...] = jnp.zeros_like(dgain_ref)

    def finish(i, _):
        r0 = pl.multiple_of(i * 16, 16)
        x = xown[pl.ds(r0, 16), :].astype(F32)
        back = pown[pl.ds(r0, 16), :]
        for j in range(N_TENSOR - 1):
            back = back + recv[j, pl.ds(r0, 16), :]
        scale = lax.rsqrt(jnp.mean(x * x, axis=-1, keepdims=True) + 1e-05)
        n = x * scale
        bn = back * n
        dgain_ref[...] = dgain_ref[...] + bn[0:8] + bn[8:16]
        b = back * gain_ref[0:1, :]
        g = gres_ref[pl.ds(r0, 16), :] + scale * (b - n * jnp.mean(b * n, axis=-1, keepdims=True))
        shard[pl.ds(r0, 16), :] = g.astype(BF16).astype(F32)
        return 0

    lax.fori_loop(0, own // 16, finish, 0)
    back = gather_copies(d, peers, shard, grecv, s2, r2)
    for c in back:
        c.start()
    gathered_out(t, shard, grecv, ig_ref, back, own)
    for c in copies + back:
        c.wait_send()


def in_exchange(part, gres, inputs, gain):
    T, D = inputs.shape
    own = T // N_TENSOR
    sd = jax.ShapeDtypeStruct
    return pl.pallas_call(
        in_kernel,
        out_shape=(sd((T, D), BF16), sd((8, D), F32)),
        in_specs=[ANY, VM, ANY, VM], out_specs=[VM, VM],
        scratch_shapes=[pltpu.VMEM((7, own, D), F32), pltpu.VMEM((own, D), F32),
                        pltpu.VMEM((7, own, D), F32), pltpu.VMEM((own, D), BF16), pltpu.VMEM((own, D), F32), pltpu.SemaphoreType.DMA((2,))] + dma_sems(7, 7, 7, 7),
        compiler_params=pltpu.CompilerParams(collective_id=3, has_side_effects=True, vmem_limit_bytes=56 * 2 ** 20),
        name="in_exchange",
    )(part, gres, inputs, gain)


def matmul(left, right):
    return jnp.dot(left, right, preferred_element_type=F32)


def rows8(v):
    return jnp.broadcast_to(v[None, :], (8, v.shape[0]))


def per_device(inputs, segments, attn_gain, w_query, w_key, w_value, w_gate, w_beta, w_alpha, conv_query, conv_key, conv_value,
               decay_log, decay_bias, head_gain, w_out, ffn_gain, w_up_gate, w_up, w_down, out_grad):
    T, D = inputs.shape
    blocks = T // L
    tokens_in = inputs.astype(F32)
    scale_in = lax.rsqrt(jnp.mean(tokens_in * tokens_in, axis=-1, keepdims=True) + 1e-05)
    hidden_in = (tokens_in * scale_in * attn_gain).astype(BF16)
    w_ba = jnp.concatenate([w_beta, w_alpha, jnp.zeros((D, 124), BF16)], axis=1)
    qp, kp, vp, gp = (matmul(hidden_in, w) for w in (w_query, w_key, w_value, w_gate))
    ba = matmul(hidden_in, w_ba)
    rate = jnp.zeros((8, 128), F32).at[:, 2:4].set(-jnp.exp(decay_log))
    bias = jnp.zeros((8, 128), F32).at[:, 2:4].set(decay_bias)
    seg = segments.astype(F32).reshape(blocks, 1, L)
    prev = jnp.concatenate([seg[:1, :, :1], seg[:-1, :, L - 1:]], axis=0)
    seg3 = jnp.concatenate([seg, jnp.broadcast_to(prev, seg.shape), jnp.zeros((blocks, 6, L), F32)], axis=1)
    gain8 = rows8(head_gain)
    low, q, k, x, u, s, o = mixer_fwd(seg3, qp, kp, vp, gp, ba, conv_query, conv_key, conv_value, rate, bias, gain8)
    hidden_mid, resid = attn_exchange(low, w_out, inputs, rows8(ffn_gain))
    gate_pre = matmul(hidden_mid, w_up_gate)
    up_pre = matmul(hidden_mid, w_up)
    sig = jax.nn.sigmoid(gate_pre)
    act = gate_pre * sig
    inner = (act * up_pre).astype(BF16)
    ffn = matmul(inner, w_down)
    grad_inner = matmul(out_grad, w_down.T)
    grad_down = matmul(inner.T, out_grad)
    gg = (grad_inner * up_pre * sig * (1.0 + gate_pre * (1.0 - sig))).astype(BF16)
    gu = (grad_inner * act).astype(BF16)
    grad_up_gate = matmul(hidden_mid.T, gg)
    grad_up = matmul(hidden_mid.T, gu)
    grad_attn, grad_resid, ffn_gain_part, out32 = mid_exchange(gg, gu, w_up_gate, w_up, ffn, resid, out_grad, rows8(ffn_gain))
    outputs = out32.astype(BF16)
    grad_out = matmul(low.T, grad_attn)
    grad_mixed = matmul(grad_attn, w_out.T)
    gq, gk, gv, gt, gba, taps, small, hgain = mixer_bwd(
        seg3, grad_mixed, qp, kp, vp, gp, ba, conv_query, conv_key, conv_value, rate, bias, gain8, q, k, x, u, s, o)
    grad_query = matmul(hidden_in.T, gq)
    grad_key = matmul(hidden_in.T, gk)
    grad_value = matmul(hidden_in.T, gv)
    grad_gate = matmul(hidden_in.T, gt)
    grad_ba = matmul(hidden_in.T, gba)
    part = matmul(gq, w_query.T) + matmul(gk, w_key.T) + matmul(gv, w_value.T) + matmul(gt, w_gate.T) + matmul(gba, w_ba.T)
    input_grad, attn_gain_part = in_exchange(part, grad_resid, inputs, rows8(attn_gain))
    both = lax.psum((jnp.sum(attn_gain_part, axis=0), jnp.sum(ffn_gain_part, axis=0), hgain[0]), ("dp", "tensor"))
    sums = lax.psum((taps[:4], small[:2, 2:4]), "dp")

    def scatter(g, dim=0):
        return lax.psum_scatter(g, "dp", scatter_dimension=dim, tiled=True)

    return (outputs, input_grad, both[0], scatter(grad_query), scatter(grad_key), scatter(grad_value), scatter(grad_gate),
            scatter(grad_ba[:, 0:2]), scatter(grad_ba[:, 2:4]), sums[0][:, 0:256], sums[0][:, 256:512], sums[0][:, 512:1024],
            sums[1][1], sums[1][0], both[2], scatter(grad_out, 1), both[1], scatter(grad_up_gate), scatter(grad_up), scatter(grad_down, 1))


def solution(mesh):
    col, row, rep = P(None, "tensor"), P("tensor", None), P()
    tok, both, head = P("dp", None), P("dp", "tensor"), P("tensor")
    return jax.shard_map(
        per_device,
        mesh=mesh,
        in_specs=(tok, tok, rep, col, col, col, col, col, col, col, col, col, head, head, rep, row, rep, col, col, row, tok),
        out_specs=(tok, tok, rep, both, both, both, both, both, both, col, col, col, head, head, rep, P("tensor", "dp"), rep, both, both, P("tensor", "dp")),
        check_vma=False,
    )
```

time: 2350 us -> 1290 us (0.55)
  waiting for transfers between devices: 1480 us -> 288 us
  Pallas kernels: 0 us -> 693 us
  other arithmetic: 344 us -> 15.4 us
  matrix products: 317 us -> 104 us
  local copies, waits for them, and re-layouts: 94.1 us -> 34.5 us
  blocking collectives: 75.6 us -> 128 us
    psum x3 -> x0, waiting for transfers between devices: 1010 us -> none  [the longest x1 487 us: per_device(): ffn_total = lax.psum(matmul(inner, w_down), 'tensor')]
    pallas_call x0 -> x5, Pallas kernels: none -> 693 us  [the longest x1 287 us: mid_exchange(): pl.pallas_call(mid_kernel, out_shape=(sd((T, D), BF16), sd((own, D), F32)...]
    another operation x156 -> x2, other arithmetic: 252 us -> 1.97 us  [the longest x96 240 us: block_step(): jax.scipy.linalg.solve_triangular(ident_mat + strict, target_value, lower...]
    reduce_scatter x8, waiting for transfers between devices: 476 us -> 288 us  [scatter(): return lax.psum_scatter(g, 'dp', scatter_dimension=dim, tiled=True)]
    dot_general x304 -> x24, matrix products: 290 us -> 104 us  [matmul(): return jnp.dot(left, right, preferred_element_type=F32)]
    psum x2, blocking collectives: 75.6 us -> 128 us  [the longest x1 72 us: per_device(): lax.psum((jnp.sum(attn_gain_part, axis=0), jnp.sum(ffn_gain_part, axis=0)...]
    squeeze x96 -> x1, local copies, waits for them, and re-layouts: 44.9 us -> 0.52 us  [per_device(): sums[1][0]]
    reduce_sum x51 -> x3, other arithmetic: 39 us -> 3.46 us  [the longest x1 2.57 us: per_device(): jnp.mean(tokens_in * tokens_in, axis=-1, keepdims=True) + 1e-05]
  transfers between devices with their start and end apart: 13 -> 10, of which waited for: 10 -> 5; matrix products, arithmetic and copies ran while one was open for 6% -> 6% of each run, Pallas kernels for 0% -> 14%
where the time goes in v1:
time: 1290 us; the launch traced here: 1280 us
  Pallas kernels  693 us (54%)
  waiting for transfers between devices  288 us (22%)
  blocking collectives  128 us (10%)
  matrix products  104 us (8%)
  local copies, waits for them, and re-layouts  34.5 us (3%)
  other arithmetic  15.4 us (1%)
  between operations  15 us (1%)
    reduce_scatter x8, waiting for transfers between devices, scatter(): return lax.psum_scatter(g, 'dp', scatter_dimension=dim, tiled=True)  288 us
    pallas_call x1, Pallas kernels, mid_exchange(): pl.pallas_call(mid_kernel, out_shape=(sd((T, D), BF16), sd((own, D), F32)...  287 us
    pallas_call x1, Pallas kernels, in_exchange(): pl.pallas_call(in_kernel, out_shape=(sd((T, D), BF16), sd((8, D), F32)),...  176 us
    pallas_call x1, Pallas kernels, attn_exchange(): pl.pallas_call(attn_kernel, out_shape=(sd((T, D), BF16), sd((own, D), F32...  153 us
    dot_general x24, matrix products, matmul(): return jnp.dot(left, right, preferred_element_type=F32)  104 us
    psum x1, blocking collectives, per_device(): lax.psum((jnp.sum(attn_gain_part, axis=0), jnp.sum(ffn_gain_part, axis=0)...  72 us
    psum x1, blocking collectives, per_device(): sums = lax.psum((taps[:4], small[:2, 2:4]), 'dp')  55.6 us
    pallas_call x1, Pallas kernels, mixer_bwd(): pl.pallas_call(functools.partial(bwd_kernel, blocks), out_shape=(sd((T, 2...  49.9 us
  transfers between devices with their start and end apart: 10, of which 5 were waited for; matrix products, arithmetic and copies ran while one was open for 6% of the time, Pallas kernels for 14%

profile of v1, /device:TPU:24, one launch (start us, length us, event | category | flops | bytes accessed | tf_op | source)
XLA Modules:
  0.0 1278.1 jit_solution(7595200952908209379)
XLA Ops:
  9.3 1.3 broadcast_select_fusion
  10.9 2.6 fusion
  14.9 2.8 fusion.2
  17.7 1.9 fusion.12.kp_ref
  19.7 1.9 fusion.11.qp_ref
  21.6 2.9 fusion.14.gp_ref
  24.5 3.0 fusion.13.vp_ref
  27.5 4.6 copy.74.wg_ref
  32.1 4.6 copy.75.wu_ref
  38.4 3.8 fusion.5.ba_ref
  44.0 25.9 %mixer_forward.1 = (bf16[768,512]{1,0:T(8,128)(2,1)}, f32[768,256]{1,0:T(8,128)}, f32[768,256]{1,0:T(8,128)}, f32[768,256]{1,0:T(8,128)}, f32[768,512]{1,0:T(8,1...) custom-call(f32[6,8,128]{2,1,0:T(8,128)} %maximum_maximum_fusion.1.seg_ref, f32[768,256]{1,0:T(8,128)} %fusion.11.qp_ref, ...), custom_call_target="tpu_custom_call" | custom-call | tf_op jit(solution)/shard_map/mixer_forward/pallas_call | solution.py:203
  70.5 153.5 %attn_exchange.1 = (bf16[768,2048]{1,0:T(8,128)(2,1)}, f32[96,2048]{1,0:T(8,128)}) custom-call(bf16[768,512]{1,0:T(8,128)(2,1)} %get-tuple-element.67.low_ref, bf16[512,2048]{1,0:T(8,128)(2,1)} %w_ref.1, bf16[768,2048]{1,0:T(8,128)(2,1)} %x_ref.3, f32[8,2048]{1,0:T(8,128)} %broadcast_in_dim.19.gain_ref), custom_call_target="tpu_custom_call" | custom-call | tf_op jit(solution)/shard_map/attn_exchange/pallas_call | solution.py:507
  223.9 5.5 fusion.15
  229.5 2.6 fusion.10
  232.3 4.7 multiply_convert_fusion
  237.0 4.6 fusion.16.ffn_ref
  241.6 287.3 %mid_exchange.1 = (bf16[768,2048]{1,0:T(8,128)(2,1)}, f32[96,2048]{1,0:T(8,128)}, f32[8,2048]{1,0:T(8,128)}, f32[768,2048]{1,0:T(8,128)}) custom-call(bf16[768,704]{1,0:T(8,128)(2,1)} %get-tuple-element.96.gg_ref, bf16[768,704]{1,0:T(8,128)(2,1)} %get-tuple-element.97.gu_ref, bf16[2048,704]{1,0:T(8,128)(2,1)} %copy.74.wg_ref, ...), custom_call_target="tpu_custom_call" | custom-call | tf_op jit(solution)/shard_map/mid_exchange/pallas_call | solution.py:599
  528.9 4.9 fusion.17.gm_ref
  533.7 49.9 %mixer_backward.1 = (bf16[768,256]{1,0:T(8,128)(2,1)}, bf16[768,256]{1,0:T(8,128)(2,1)}, bf16[768,512]{1,0:T(8,128)(2,1)}, bf16[768,512]{1,0:T(8,128)(2,1)}, bf1...) custom-call(f32[6,8,128]{2,1,0:T(8,128)} %maximum_maximum_fusion.1.seg_ref, ...), custom_call_target="tpu_custom_call" | custom-call | tf_op jit(solution)/shard_map/mixer_backward/pallas_call | solution.py:399
  583.6 1.5 fusion.25
  585.2 1.4 copy.81
  586.7 1.4 copy.79
  588.1 4.3 fusion.21
  592.5 4.3 fusion.22
  596.9 5.7 fusion.26
  603.7 5.8 fusion.23
  610.7 5.7 fusion.24
  616.4 1.2 copy-done.19
  617.7 6.8 fusion.29
  624.5 1.2 copy-done.17
  625.7 6.8 fusion.28
  632.6 1.2 copy-done.16
  633.8 6.9 fusion.27
  640.8 5.0 convert_element_type.27
  647.3 55.6 %all-reduce.3 = (f32[4,1024]{1,0:T(4,128)S(1)}, f32[2,2]{1,0:T(2,128)S(1)}) all-reduce(f32[4,1024]{1,0:T(4,128)S(1)} %slice.72, f32[2,2]{1,0:T(2,128)S(1)} %slice.76), channel_id=1, replica_groups=mesh['dp'=16,'tensor'=8] {'dp'}, use_global_device_ids=true, to_apply=%region_10.0 | all-reduce | flops 4100 | bytes 32800 | tf_op jit(solution)/shard_map/psum | solution.py:721
  706.5 4.5 fusion.20
  711.0 4.5 fusion.19
  715.5 9.5 add_add_fusion.part_ref
  725.6 176.2 %in_exchange.1 = (bf16[768,2048]{1,0:T(8,128)(2,1)}, f32[8,2048]{1,0:T(8,128)}) custom-call(f32[768,2048]{1,0:T(8,128)} %add_add_fusion.part_ref, f32[96,2048]{1,0:T(8,128)} %get-tuple-element.83.gres_ref, bf16[768,2048]{1,0:T(8,128)(2,1)} %x_ref.3, f32[8,2048]{1,0:T(8,128)} %broadcast_in_dim.20.gain_ref), custom_call_target="tpu_custom_call" | custom-call | tf_op jit(solution)/shard_map/in_exchange/pallas_call | solution.py:658
  902.7 72.0 %all-reduce.2 = (f32[2048]{0:T(1024)}, f32[256]{0:T(256)}, f32[2048]{0:T(1024)}) all-reduce(f32[2048]{0:T(1024)S(1)} %reduce_sum.28, f32[256]{0:T(256)S(1)} %bitcast.58, f32[2048]{0:T(1024)S(1)} %reduce_sum.29), channel_id=1, replica_groups=mesh['dp'=16,'tensor'=8] {'dp','tensor'}, use_global_device_ids=true, to_apply=%region_3.0 | all-reduce | flops 4352 | bytes 34816 | tf_op jit(solution)/shard_map/psum | solution.py:720
  975.8 1.5 copy.82
  977.2 1.5 copy.80
  978.7 6.3 reduce-scatter.19.cloned.1.call-done
  985.0 68.1 %reduce-scatter.21.cloned.1.call-done = f32[128,512]{1,0:T(8,128)} async-done(((f32[2048,512]{1,0:T(8,128)}), f32[128,512]{1,0:T(8,128)}) %reduce-scatter.21.cloned.1.call-update) | async-done | bytes 262160 | tf_op jit(solution)/shard_map/reduce_scatter | solution.py:724
  1053.1 71.3 %reduce-scatter.29.cloned.1.call-done = f32[704,128]{1,0:T(8,128)} async-done(((f32[704,2048]{1,0:T(8,128)}), f32[704,128]{1,0:T(8,128)}) %reduce-scatter.29.cloned.1.call-update) | async-done | bytes 360464 | tf_op jit(solution)/shard_map/reduce_scatter | solution.py:724
  1124.4 71.2 %reduce-scatter.27.cloned.1.call-done = f32[128,704]{0,1:T(8,128)} async-done(((f32[2048,704]{0,1:T(8,128)}), f32[128,704]{0,1:T(8,128)}) %reduce-scatter.27.cloned.1.call-update) | async-done | bytes 360464 | tf_op jit(solution)/shard_map/reduce_scatter | solution.py:724
  1195.6 71.1 %reduce-scatter.25.cloned.1.call-done = f32[128,704]{0,1:T(8,128)} async-done(((f32[2048,704]{0,1:T(8,128)}), f32[128,704]{0,1:T(8,128)}) %reduce-scatter.25.cloned.1.call-update) | async-done | bytes 360464 | tf_op jit(solution)/shard_map/reduce_scatter | solution.py:724
  1266.7 4.1 copy.84
  (131 shorter events, 18.4 us)
Async XLA Ops:
  7.2 222.3 %copy-start = (bf16[704,2048]{1,0:T(8,128)(2,1)S(1)}, bf16[704,2048]{1,0:T(8,128)(2,1)}, u32[]{:S(2)}) copy-start(bf16[704,2048]{1,0:T(8,128)(2,1)} %param.44) | copy-start | bytes 8650756
  7.2 6.3 copy-start.32
  7.2 6.6 copy-start.33
  7.2 7.7 copy-start.31
  7.2 968.5 %reduce-scatter.33.cloned.1.call-start = ((), (), s32[]{:S(2)}) async-start(), calls=%async_computation.19 | async-start | bytes 1114112
  13.8 24.6 %copy-start.8 = (bf16[2048,2]{1,0:T(8,128)(2,1)}, bf16[2048,2]{1,0:T(8,128)(2,1)S(1)}, u32[]{:S(2)}) copy-start(bf16[2048,2]{1,0:T(8,128)(2,1)S(1)} %copy.65) | copy-start | bytes 24580
  14.9 2.8 copy-start.23
  17.6 6.9 copy-start.2
  17.7 2.0 copy-start.21
  19.7 1.9 copy-start.11
  21.6 2.9 copy-start.13
  36.7 6.6 copy-start.36
  42.2 27.7 %copy-start.34 = (f32[2048]{0:T(1024)S(1)}, f32[2048]{0:T(1024)}, u32[]{:S(2)}) copy-start(f32[2048]{0:T(1024)} %param.41) | copy-start | bytes 24580
  223.9 5.6 copy-start.4
  229.5 2.7 copy-start.6
  229.5 2.8 copy-start.37
  237.0 4.6 copy-start.18
  241.6 287.3 %copy-start.7 = (bf16[512,2048]{1,0:T(8,128)(2,1)S(1)}, bf16[512,2048]{1,0:T(8,128)(2,1)}, u32[]{:S(2)}) copy-start(bf16[512,2048]{1,0:T(8,128)(2,1)} %w_ref.1) | copy-start | bytes 6291460
  533.7 49.9 %copy-start.3 = (bf16[768,2048]{1,0:T(8,128)(2,1)S(1)}, bf16[768,2048]{1,0:T(8,128)(2,1)}, u32[]{:S(2)}) copy-start(bf16[768,2048]{1,0:T(8,128)(2,1)} %copy-done.2) | copy-start | bytes 9437188
  585.2 2.9 copy-start.20
  586.6 390.6 %reduce-scatter.31.cloned.1.call-start = ((), (), s32[]{:S(2)}) async-start(), calls=%async_computation.18 | async-start | bytes 1114112
  588.1 390.7 %reduce-scatter.15.cloned.1.call-start = ((), (), s32[]{:S(2)}) async-start(), calls=%async_computation.10 | async-start | bytes 2228224 | tf_op jit(solution)/shard_map/reduce_scatter | solution.py:724
  588.1 4.4 copy-start.29
  592.5 386.3 %reduce-scatter.17.cloned.1.call-start = ((), (), s32[]{:S(2)}) async-start(), calls=%async_computation.11 | async-start | bytes 2228224 | tf_op jit(solution)/shard_map/reduce_scatter | solution.py:724
  592.5 4.4 copy-start.5
  596.9 381.9 %reduce-scatter.23.cloned.1.call-start = ((), (), s32[]{:S(2)}) async-start(), calls=%async_computation.14 | async-start | bytes 4456448 | tf_op jit(solution)/shard_map/reduce_scatter | solution.py:724
  602.6 1.1 copy-start.25
  602.6 382.4 %reduce-scatter.19.cloned.1.call-start = ((), (), s32[]{:S(2)}) async-start(), calls=%async_computation.12 | async-start | bytes 4456448 | tf_op jit(solution)/shard_map/reduce_scatter | solution.py:724
  609.5 1.1 copy-start.27
  609.6 443.5 %reduce-scatter.21.cloned.1.call-start = ((), (), s32[]{:S(2)}) async-start(), calls=%async_computation.13 | async-start | bytes 4456448 | tf_op jit(solution)/shard_map/reduce_scatter | solution.py:724
  616.4 1.3 copy-start.19
  616.4 508.0 %reduce-scatter.29.cloned.1.call-start = ((), (), s32[]{:S(2)}) async-start(), calls=%async_computation.17 | async-start | bytes 6127616 | tf_op jit(solution)/shard_map/reduce_scatter | solution.py:724
  624.4 1.3 copy-start.17
  624.5 571.2 %reduce-scatter.27.cloned.1.call-start = ((), (), s32[]{:S(2)}) async-start(), calls=%async_computation.16 | async-start | bytes 6127616 | tf_op jit(solution)/shard_map/reduce_scatter | solution.py:724
  632.5 1.3 copy-start.16
  632.5 634.2 %reduce-scatter.25.cloned.1.call-start = ((), (), s32[]{:S(2)}) async-start(), calls=%async_computation.15 | async-start | bytes 6127616 | tf_op jit(solution)/shard_map/reduce_scatter | solution.py:724
  640.7 5.1 copy-start.30
  640.7 5.1 copy-start.35
  640.7 62.8 %copy-start.9 = (bf16[2048,2]{1,0:T(8,128)(2,1)S(1)}, bf16[2048,2]{1,0:T(8,128)(2,1)}, u32[]{:S(2)}) copy-start(bf16[2048,2]{1,0:T(8,128)(2,1)} %copy-done.8) | copy-start | bytes 24580
  640.7 62.8 %copy-start.10 = (bf16[2048,2]{1,0:T(8,128)(2,1)S(1)}, bf16[2048,2]{1,0:T(8,128)(2,1)}, u32[]{:S(2)}) copy-start(bf16[2048,2]{1,0:T(8,128)(2,1)} %copy.66) | copy-start | bytes 24580
  640.7 62.8 %copy-start.15 = (bf16[768,128]{1,0:T(8,128)(2,1)S(1)}, bf16[768,128]{1,0:T(8,128)(2,1)}, u32[]{:S(2)}) copy-start(bf16[768,128]{1,0:T(8,128)(2,1)} %get-tuple-element.82) | copy-start | bytes 589828
  703.5 1.2 copy-start.22
  704.8 1.6 copy-start.12
  704.8 1.8 copy-start.28
  706.5 4.5 copy-start.14
  706.5 4.5 copy-start.26
  711.0 4.5 copy-start.24
  1266.7 4.1 copy-start.1
Sparse Core Ops, SparseCore 0:
  586.8 64.0 reduce-scatter.32
  653.4 59.8 reduce-scatter.30
  716.2 63.6 reduce-scatter.14
  782.8 63.5 reduce-scatter.16
  849.2 66.8 reduce-scatter.22
  919.0 65.9 reduce-scatter.18
  988.0 65.0 reduce-scatter.20
  1056.1 68.2 reduce-scatter.28
  1127.4 68.1 reduce-scatter.26
  1198.5 68.1 reduce-scatter.24

commit v2 on v1

--- a/solution.py
+++ b/solution.py
@@ -409,261 +409,632 @@
 
 
 MESH = pl.DeviceIdType.MESH
-N_TENSOR = 8
-
-
-def tensor_peers():
-    d, t = lax.axis_index("dp"), lax.axis_index("tensor")
-    return d, t, [lax.rem(t + j, N_TENSOR) for j in range(1, N_TENSOR)]
-
-
-def greet(d, peers):
+NT_ = 8
+HALF = 1024
+
+
+class Ring:
+    def __init__(self):
+        self.d = lax.axis_index("dp")
+        self.t = lax.axis_index("tensor")
+        self.y = lax.rem(self.t, 2)
+        self.z = self.t // 2
+        self.right = (self.d, self.at(1) * 2 + self.y)
+        self.left = (self.d, self.at(3) * 2 + self.y)
+        self.flip = (self.d, self.z * 2 + 1 - self.y)
+
+    def at(self, k):
+        return lax.rem(self.z + k, 4)
+
+    def rows(self, k, other, own):
+        side = 1 - self.y if other else self.y
+        return pl.ds(pl.multiple_of((self.at(k) * 2 + side) * own, own), own)
+
+    def quarter(self, k, own):
+        return pl.ds(pl.multiple_of(self.at(k) * 2 * own, 2 * own), 2 * own)
+
+
+class Sends:
+    def __init__(self, ssem, rsem):
+        self.ssem, self.rsem, self.made = ssem, rsem, []
+
+    def make(self, i, src, dst, device):
+        return pltpu.make_async_remote_copy(src_ref=src, dst_ref=dst, send_sem=self.ssem.at[i], recv_sem=self.rsem.at[i],
+                                            device_id=device, device_id_type=MESH)
+
+    def go(self, i, src, dst, device):
+        c = self.make(i, src, dst, device)
+        c.start()
+        self.made.append(c)
+
+    def got(self, i, dst, device):
+        self.make(i, dst, dst, device).wait_recv()
+
+    def drain(self):
+        for c in self.made:
+            c.wait_send()
+
+
+def greet(devices):
     barrier = pltpu.get_barrier_semaphore()
-    for p in peers:
-        pl.semaphore_signal(barrier, inc=1, device_id=(d, p), device_id_type=MESH)
-    pl.semaphore_wait(barrier, len(peers))
-
-
-def scatter_copies(d, peers, send, recv, ssem, rsem, own):
-    return [
-        pltpu.make_async_remote_copy(
-            src_ref=send.at[pl.ds(pl.multiple_of(p * own, own), own)], dst_ref=recv.at[j],
-            send_sem=ssem.at[j], recv_sem=rsem.at[j], device_id=(d, p), device_id_type=MESH)
-        for j, p in enumerate(peers)]
-
-
-def gather_copies(d, peers, shard, recv, ssem, rsem):
-    return [
-        pltpu.make_async_remote_copy(
-            src_ref=shard, dst_ref=recv.at[j],
-            send_sem=ssem.at[j], recv_sem=rsem.at[j], device_id=(d, p), device_id_type=MESH)
-        for j, p in enumerate(peers)]
-
-
-def summed(send, recv, t, own, r0, n):
-    total = send[pl.ds(pl.multiple_of(t * own + r0, 8), n), :]
-    for j in range(N_TENSOR - 1):
-        total = total + recv[j, pl.ds(r0, n), :]
-    return total
-
-
-def gathered_out(t, shard, recv, out_ref, copies, own):
-    out_ref[pl.ds(pl.multiple_of(t * own, own), own), :] = shard[...].astype(out_ref.dtype)
-    for j in range(N_TENSOR - 1):
-        copies[j].wait_recv()
-        source = lax.rem(t + N_TENSOR - 1 - j, N_TENSOR)
-        out_ref[pl.ds(pl.multiple_of(source * own, own), own), :] = recv[j].astype(out_ref.dtype)
-
-
-def attn_kernel(low_ref, w_ref, x_ref, gain_ref, hid_ref, resid_ref,
-                send, recv, shard, grecv, xown, csem, s1, r1, s2, r2):
-    d, t, peers = tensor_peers()
+    for dev in devices:
+        pl.semaphore_signal(barrier, inc=1, device_id=dev, device_id_type=MESH)
+    pl.semaphore_wait(barrier, len(devices))
+
+
+ZA, ZB, YA, YB = (pl.ds(i * 512, 512) for i in range(4))
+ZZ, YY = pl.ds(0, HALF), pl.ds(HALF, HALF)
+LO, HI = pl.ds(0, 512), pl.ds(512, 512)
+
+
+def scatter_scratch(own):
+    return [pltpu.VMEM((4, own, 1024), F32), pltpu.VMEM((6, 2 * own, 512), F32), pltpu.VMEM((6, own, 512), F32),
+            pltpu.VMEM((own, 1024), F32), pltpu.VMEM((own, 1024), F32),
+            pltpu.SemaphoreType.DMA((17,)), pltpu.SemaphoreType.DMA((17,))]
+
+
+def add_rows(dst, src_of, n):
+    def one(i, _):
+        r = pl.multiple_of(i * 16, 16)
+        dst[pl.ds(r, 16), :] = dst[pl.ds(r, 16), :] + src_of(r)
+        return 0
+    lax.fori_loop(0, n // 16, one, 0)
+
+
+def sub(ref, rows, cols):
+    return lambda r: ref[pl.ds(pl.multiple_of(rows.start + r, 16), 16), cols]
+
+
+class Scatter:
+    def __init__(self, ring, part, scratch, own):
+        self.ring, self.part, self.own = ring, part, own
+        self.yb, self.zb, self.yr, self.zsend, self.zf, ssem, rsem = scratch
+        self.s = Sends(ssem, rsem)
+
+    def start(self):
+        g, s, p, own = self.ring, self.s, self.part, self.own
+        s.go(0, p.at[g.quarter(2, own), ZB], self.zb.at[0], g.right)
+        s.go(1, p.at[g.quarter(2, own), ZA], self.zb.at[1], g.left)
+        s.go(6, p.at[g.rows(2, True, own), YY], self.yb.at[2], g.flip)
+        s.go(2, p.at[g.quarter(1, own), ZA], self.zb.at[2], g.right)
+        s.go(3, p.at[g.quarter(3, own), ZB], self.zb.at[3], g.left)
+        s.go(7, p.at[g.rows(1, True, own), YY], self.yb.at[1], g.flip)
+        s.go(8, p.at[g.rows(3, True, own), YY], self.yb.at[3], g.flip)
+        s.go(9, p.at[g.rows(0, True, own), YY], self.yb.at[0], g.flip)
+
+    def middle(self):
+        g, s, p, own = self.ring, self.s, self.part, self.own
+        yb, zb, yr = self.yb, self.zb, self.yr
+        s.got(6, yb.at[2], g.flip)
+        add_rows(yb.at[2], sub(p, g.rows(2, False, own), YY), own)
+        s.go(10, yb.at[2, :, HI], yr.at[0], g.right)
+        s.go(11, yb.at[2, :, LO], yr.at[1], g.left)
+        s.got(0, zb.at[0], g.left)
+        add_rows(zb.at[0], sub(p, g.quarter(1, own), ZB), 2 * own)
+        s.go(4, zb.at[0], zb.at[4], g.right)
+        s.got(1, zb.at[1], g.right)
+        add_rows(zb.at[1], sub(p, g.quarter(3, own), ZA), 2 * own)
+        s.go(5, zb.at[1], zb.at[5], g.left)
+        s.got(7, yb.at[1], g.flip)
+        add_rows(yb.at[1], sub(p, g.rows(1, False, own), YY), own)
+        s.go(12, yb.at[1, :, LO], yr.at[2], g.right)
+        s.got(10, yr.at[0], g.left)
+        add_rows(yr.at[0], lambda r: yb[1, pl.ds(r, 16), HI], own)
+        s.go(14, yr.at[0], yr.at[4], g.right)
+        s.got(8, yb.at[3], g.flip)
+        add_rows(yb.at[3], sub(p, g.rows(3, False, own), YY), own)
+        s.go(13, yb.at[3, :, HI], yr.at[3], g.left)
+        s.got(11, yr.at[1], g.right)
+        add_rows(yr.at[1], lambda r: yb[3, pl.ds(r, 16), LO], own)
+        s.go(15, yr.at[1], yr.at[5], g.left)
+        s.got(2, zb.at[2], g.left)
+        s.got(3, zb.at[3], g.right)
+        s.got(4, zb.at[4], g.left)
+        s.got(5, zb.at[5], g.right)
+        base = g.rows(0, True, own).start
+        lead = (1 - g.y) * own
+
+        def one(i, _):
+            r = pl.multiple_of(i * 16, 16)
+            at = pl.ds(pl.multiple_of(lead + r, 16), 16)
+            mine = pl.ds(pl.multiple_of(base + r, 16), 16)
+            self.zsend[pl.ds(r, 16), LO] = p[mine, ZA] + (zb[2, at, :] + zb[5, at, :])
+            self.zsend[pl.ds(r, 16), HI] = p[mine, ZB] + (zb[3, at, :] + zb[4, at, :])
+            return 0
+
+        lax.fori_loop(0, own // 16, one, 0)
+        s.go(16, self.zsend, self.zf, g.flip)
+
+    def finish(self):
+        g, s = self.ring, self.s
+        s.got(9, self.yb.at[0], g.flip)
+        s.got(12, self.yr.at[2], g.left)
+        s.got(13, self.yr.at[3], g.right)
+        s.got(14, self.yr.at[4], g.left)
+        s.got(15, self.yr.at[5], g.right)
+        s.got(16, self.zf, g.flip)
+
+    def value(self, r):
+        g, p, own = self.ring, self.part, self.own
+        zb, yr = self.zb, self.yr
+        at = pl.ds(pl.multiple_of(g.y * own + r, 16), 16)
+        here = pl.ds(r, 16)
+        mine = pl.ds(pl.multiple_of(g.rows(0, False, own).start + r, 16), 16)
+        za = p[mine, ZA] + (zb[2, at, :] + zb[5, at, :]) + self.zf[here, LO]
+        zz = p[mine, ZB] + (zb[3, at, :] + zb[4, at, :]) + self.zf[here, HI]
+        ya = p[mine, YA] + self.yb[0, here, LO] + (yr[2, here, :] + yr[5, here, :])
+        yz = p[mine, YB] + self.yb[0, here, HI] + (yr[3, here, :] + yr[4, here, :])
+        return jnp.concatenate([za, zz, ya, yz], axis=1)
+
+
+def gather_sems():
+    return [pltpu.SemaphoreType.DMA((17,)), pltpu.SemaphoreType.DMA((17,))]
+
+
+class Gather:
+    def __init__(self, ring, whole, sems, own):
+        self.ring, self.whole, self.own = ring, whole, own
+        self.s = Sends(*sems)
+
+    def _go(self, i, rows, cols, device):
+        ref = self.whole.at[rows, cols]
+        self.s.go(i, ref, ref, device)
+
+    def _got(self, i, rows, cols, device):
+        self.s.got(i, self.whole.at[rows, cols], device)
+
+    def start(self):
+        g, own = self.ring, self.own
+        mine = g.rows(0, False, own)
+        self._go(0, mine, YY, g.right)
+        self._go(1, mine, YY, g.left)
+        self._go(2, mine, ZZ, g.flip)
+        self._go(3, mine, ZZ, g.right)
+        self._go(4, mine, ZZ, g.left)
+        self._go(5, mine, YY, g.flip)
+
+    def middle(self):
+        g, own = self.ring, self.own
+        lf, rt = g.rows(3, False, own), g.rows(1, False, own)
+        lo, ro = g.rows(3, True, own), g.rows(1, True, own)
+        far, faro, other = g.rows(2, False, own), g.rows(2, True, own), g.rows(0, True, own)
+        self._got(0, lf, YY, g.left)
+        self._go(6, lf, YB, g.right)
+        self._go(7, lf, YY, g.flip)
+        self._got(1, rt, YY, g.right)
+        self._go(8, rt, YA, g.left)
+        self._go(9, rt, YY, g.flip)
+        self._got(2, other, ZZ, g.flip)
+        self._go(10, other, ZZ, g.right)
+        self._go(11, other, ZZ, g.left)
+        self._got(6, far, YB, g.left)
+        self._got(8, far, YA, g.right)
+        self._go(12, far, YY, g.flip)
+        self._got(3, lf, ZZ, g.left)
+        self._go(13, lf, ZB, g.right)
+        self._got(4, rt, ZZ, g.right)
+        self._go(14, rt, ZA, g.left)
+        self._got(10, lo, ZZ, g.left)
+        self._go(15, lo, ZB, g.right)
+        self._got(11, ro, ZZ, g.right)
+        self._go(16, ro, ZA, g.left)
+
+    def finish(self):
+        g, own = self.ring, self.own
+        far, faro, other = g.rows(2, False, own), g.rows(2, True, own), g.rows(0, True, own)
+        self._got(5, other, YY, g.flip)
+        self._got(7, g.rows(3, True, own), YY, g.flip)
+        self._got(9, g.rows(1, True, own), YY, g.flip)
+        self._got(12, faro, YY, g.flip)
+        self._got(13, far, ZB, g.left)
+        self._got(14, far, ZA, g.right)
+        self._got(15, faro, ZB, g.left)
+        self._got(16, faro, ZA, g.right)
+
+
+class DpScatter:
+    ORDER = (2, 1, 3, 0)
+
+    def __init__(self, ring, scratch, compute):
+        d, t = ring.d, ring.t
+        self.c, self.x, self.y = lax.rem(d, 2), lax.rem(d // 2, 4), d // 8
+        self.pair = (d + 1 - 2 * self.c, t)
+        self.right = ((self.y * 4 + self.step(1)) * 2 + self.c, t)
+        self.left = ((self.y * 4 + self.step(3)) * 2 + self.c, t)
+        self.far = (((1 - self.y) * 4 + self.x) * 2 + self.c, t)
+        self.csend, self.crecv, self.xr, self.yr, ssem, rsem = scratch
+        self.s = Sends(ssem, rsem)
+        self.compute = compute
+
+    def step(self, k):
+        return lax.rem(self.x + k, 4)
+
+    def devices(self):
+        return [self.pair, self.right, self.left, self.far]
+
+    def cols(self, k, side, core):
+        return pl.ds(pl.multiple_of(((side * 4 + self.step(k)) * 2 + core) * 128, 128), 128)
+
+    def cores(self):
+        sent = []
+        for n, k in enumerate(self.ORDER):
+            slot = 2 * (n % 2)
+            if n >= 2:
+                for c in sent[2 * n - 4:2 * n - 2]:
+                    c.wait_send()
+
+            def put(rows, both):
+                self.csend[slot, rows, :] = both[:, :128]
+                self.csend[slot + 1, rows, :] = both[:, 128:]
+
+            self.compute(self.cols(k, 0, 1 - self.c), self.cols(k, 1, 1 - self.c), put)
+            for side in range(2):
+                c = self.s.make(2 * k + side, self.csend.at[slot + side], self.crecv.at[2 * k + side], self.pair)
+                c.start()
+                sent.append(c)
+        self.s.made += sent[4:]
+
+    def along(self):
+        s, acc, xr = self.s, self.crecv, self.xr
+        for k in self.ORDER:
+            for side in range(2):
+                s.got(2 * k + side, acc.at[2 * k + side], self.pair)
+
+            def put(rows, both):
+                acc[2 * k, rows, :] = acc[2 * k, rows, :] + both[:, :128]
+                acc[2 * k + 1, rows, :] = acc[2 * k + 1, rows, :] + both[:, 128:]
+
+            self.compute(self.cols(k, 0, self.c), self.cols(k, 1, self.c), put)
+            if k == 2:
+                s.go(8, acc.at[5], xr.at[0], self.right)
+                s.go(9, acc.at[4], xr.at[1], self.left)
+            if k == 1:
+                s.go(10, acc.at[2], xr.at[2], self.right)
+            if k == 3:
+                s.go(11, acc.at[7], xr.at[3], self.left)
+
+    def second(self):
+        s, acc, xr = self.s, self.crecv, self.xr
+        n = acc.shape[1]
+        s.got(8, xr.at[0], self.left)
+        add_rows(xr.at[0], lambda r: acc[3, pl.ds(r, 16), :], n)
+        s.go(12, xr.at[0], xr.at[4], self.right)
+        s.got(9, xr.at[1], self.right)
+        add_rows(xr.at[1], lambda r: acc[6, pl.ds(r, 16), :], n)
+        s.go(13, xr.at[1], xr.at[5], self.left)
+
+    def third(self):
+        s, acc, xr = self.s, self.crecv, self.xr
+        n = acc.shape[1]
+        s.got(10, xr.at[2], self.left)
+        s.got(13, xr.at[5], self.right)
+        add_rows(acc.at[0], lambda r: xr[2, pl.ds(r, 16), :] + xr[5, pl.ds(r, 16), :], n)
+        s.got(11, xr.at[3], self.right)
+        s.got(12, xr.at[4], self.left)
+        add_rows(acc.at[1], lambda r: xr[3, pl.ds(r, 16), :] + xr[4, pl.ds(r, 16), :], n)
+        s.go(14, acc.at[1 - self.y], self.yr, self.far)
+
+    def finish(self, out_ref):
+        self.s.got(14, self.yr, self.far)
+        n = self.yr.shape[0]
+
+        def one(i, _):
+            r = pl.ds(pl.multiple_of(i * 16, 16), 16)
+            out_ref[r, :] = self.crecv[self.y, r, :] + self.yr[r, :]
+            return 0
+
+        lax.fori_loop(0, n // 16, one, 0)
+        self.s.drain()
+
+
+def dp_scratch(n):
+    return [pltpu.VMEM((4, n, 128), F32), pltpu.VMEM((8, n, 128), F32), pltpu.VMEM((6, n, 128), F32), pltpu.VMEM((n, 128), F32),
+            pltpu.SemaphoreType.DMA((15,)), pltpu.SemaphoreType.DMA((15,))]
+
+
+def params(cid, mib):
+    return pltpu.CompilerParams(collective_id=cid, has_side_effects=True, vmem_limit_bytes=mib * 2 ** 20)
+
+
+def attn_kernel(low_ref, w_ref, x_ref, gain_ref, hid_ref, resid_ref, part, whole, xown, csem, *rest):
+    scr, gsem = rest[:7], rest[7:]
+    ring = Ring()
     own = resid_ref.shape[0]
-    mine = pltpu.make_async_copy(x_ref.at[pl.ds(pl.multiple_of(t * own, own), own)], xown, csem)
-    mine.start()
+    mine = ring.rows(0, False, own)
+    fetch = pltpu.make_async_copy(x_ref.at[mine], xown, csem)
+    fetch.start()
 
     def partial(n, _):
         cols = pl.ds(pl.multiple_of(n * 256, 256), 256)
-        send[:, cols] = mm1(low_ref[...], w_ref[:, cols], NN)
+        part[:, cols] = mm1(low_ref[...], w_ref[:, cols], NN)
         return 0
 
-    lax.fori_loop(0, send.shape[1] // 256, partial, 0)
-    greet(d, peers)
-    copies = scatter_copies(d, peers, send, recv, s1, r1, own)
-    for c in copies:
-        c.start()
-    mine.wait()
-    for c in copies:
-        c.wait_recv()
+    lax.fori_loop(0, part.shape[1] // 256, partial, 0)
+    greet([ring.right, ring.left, ring.flip])
+    sc = Scatter(ring, part, scr, own)
+    sc.start()
+    fetch.wait()
+    sc.middle()
+    sc.finish()
 
     def finish(i, _):
-        r0 = pl.multiple_of(i * 16, 16)
-        resid = xown[pl.ds(r0, 16), :].astype(F32) + summed(send, recv, t, own, r0, 16)
-        resid_ref[pl.ds(r0, 16), :] = resid
+        r = pl.multiple_of(i * 16, 16)
+        resid = xown[pl.ds(r, 16), :].astype(F32) + sc.value(r)
+        resid_ref[pl.ds(r, 16), :] = resid
         n = resid * lax.rsqrt(jnp.mean(resid * resid, axis=-1, keepdims=True) + 1e-05)
-        shard[pl.ds(r0, 16), :] = (n * gain_ref[0:1, :]).astype(BF16).astype(F32)
+        whole[pl.ds(pl.multiple_of(mine.start + r, 16), 16), :] = (n * gain_ref[0:1, :]).astype(BF16).astype(F32)
         return 0
 
     lax.fori_loop(0, own // 16, finish, 0)
-    back = gather_copies(d, peers, shard, grecv, s2, r2)
-    for c in back:
-        c.start()
-    gathered_out(t, shard, grecv, hid_ref, back, own)
-    for c in copies + back:
-        c.wait_send()
-
-
-def dma_sems(*counts):
-    return [pltpu.SemaphoreType.DMA((n,)) for n in counts]
-
-
+    ga = Gather(ring, whole, gsem, own)
+    ga.start()
+    ga.middle()
+    ga.finish()
+
+    def cast(i, _):
+        r = pl.ds(pl.multiple_of(i * 32, 32), 32)
+        hid_ref[r, :] = whole[r, :].astype(BF16)
+        return 0
+
+    lax.fori_loop(0, whole.shape[0] // 32, cast, 0)
+    sc.s.drain()
+    ga.s.drain()
+
+
+VM = pl.BlockSpec(memory_space=pltpu.VMEM)
 ANY = pl.BlockSpec(memory_space=pl.ANY)
 
 
 def attn_exchange(low, w_out, inputs, gain):
     T, D = inputs.shape
-    own = T // N_TENSOR
+    own = T // NT_
     sd = jax.ShapeDtypeStruct
     return pl.pallas_call(
         attn_kernel,
         out_shape=(sd((T, D), BF16), sd((own, D), F32)),
         in_specs=[VM, VM, ANY, VM], out_specs=[VM, VM],
-        scratch_shapes=[pltpu.VMEM((T, D), F32), pltpu.VMEM((7, own, D), F32), pltpu.VMEM((own, D), F32),
-                        pltpu.VMEM((7, own, D), F32), pltpu.VMEM((own, D), BF16), pltpu.SemaphoreType.DMA(())] + dma_sems(7, 7, 7, 7),
-        compiler_params=pltpu.CompilerParams(collective_id=1, has_side_effects=True, vmem_limit_bytes=56 * 2 ** 20),
+        scratch_shapes=[pltpu.VMEM((T, D), F32), pltpu.VMEM((T, D), F32), pltpu.VMEM((own, D), BF16),
+                        pltpu.SemaphoreType.DMA(())] + scatter_scratch(own) + gather_sems(),
+        compiler_params=params(1, 56),
         name="attn_exchange",
     )(low, w_out, inputs, gain)
 
 
-def mid_kernel(gg_ref, gu_ref, wg_ref, wu_ref, ffn_ref, resid_in, og_ref, gain_ref,
-               ga_ref, gres_ref, dgain_ref, out_ref,
-               send, recv, shard, grecv, ogown, oshard, orecv, csem, s1, r1, s2, r2, s3, r3, s4, r4):
-    d, t, peers = tensor_peers()
+def mid_kernel(gg_ref, gu_ref, inner_ref, wg_ref, wu_ref, hid_ref, og_ref, resid_in, gain_ref,
+               whole, gres_ref, dgain_ref, grads_ref,
+               part, shard, left, csem, *rest):
+    scr, gsem, dscr = rest[:7], rest[7:9], rest[9:]
+    ring = Ring()
     own = gres_ref.shape[0]
-    rows_t = pl.ds(pl.multiple_of(t * own, own), own)
-    mine = pltpu.make_async_copy(og_ref.at[rows_t], ogown, csem.at[0])
-    mine.start()
-    ffn_own = pltpu.make_async_copy(ffn_ref.at[rows_t], oshard, csem.at[1])
-    ffn_own.start()
-
-    def partial(n, _):
-        cols = pl.ds(pl.multiple_of(n * 256, 256), 256)
-        send[:, cols] = mm1(gg_ref[...], wg_ref[cols, :], NT) + mm1(gu_ref[...], wu_ref[cols, :], NT)
+    n = gg_ref.shape[1]
+    mine = ring.rows(0, False, own)
+
+    def partial(i, _):
+        cols = pl.ds(pl.multiple_of(i * 256, 256), 256)
+        part[:, cols] = mm1(gg_ref[...], wg_ref[:, cols], NN) + mm1(gu_ref[...], wu_ref[:, cols], NN)
         return 0
 
-    lax.fori_loop(0, send.shape[1] // 256, partial, 0)
-    greet(d, peers)
-    copies = scatter_copies(d, peers, send, recv, s1, r1, own)
-    copies2 = scatter_copies(d, peers, ffn_ref, orecv, s3, r3, own)
-    for c in copies:
-        c.start()
-    for c in copies2:
-        c.start()
-    mine.wait()
-    for c in copies:
-        c.wait_recv()
+    lax.fori_loop(0, part.shape[1] // 256, partial, 0)
+
+    def compute(a, b, put):
+        hid = jnp.concatenate([hid_ref[:, a], hid_ref[:, b]], axis=1)
+        put(slice(0, n), mm1(left[0:n, :], hid, NN))
+        put(slice(n, 2 * n), mm1(left[n:2 * n, :], hid, NN))
+        put(slice(2 * n, 3 * n), mm1(left[2 * n:, :], jnp.concatenate([og_ref[:, a], og_ref[:, b]], axis=1), NN))
+
+    dp = DpScatter(ring, dscr, compute)
+    greet([ring.right, ring.left, ring.flip] + dp.devices())
+    sc = Scatter(ring, part, scr, own)
+    sc.start()
+    left[0:n, :] = gg_ref[...].T
+    left[n:2 * n, :] = gu_ref[...].T
+    left[2 * n:, :] = inner_ref[...].T
+    dp.cores()
+    sc.middle()
+    dp.along()
+    sc.finish()
     dgain_ref[...] = jnp.zeros_like(dgain_ref)
 
     def finish(i, _):
-        r0 = pl.multiple_of(i * 16, 16)
-        resid = resid_in[pl.ds(r0, 16), :]
-        back = summed(send, recv, t, own, r0, 16)
+        r = pl.multiple_of(i * 16, 16)
+        resid = resid_in[pl.ds(r, 16), :]
+        back = sc.value(r)
         scale = lax.rsqrt(jnp.mean(resid * resid, axis=-1, keepdims=True) + 1e-05)
-        n = resid * scale
-        bn = back * n
+        nn = resid * scale
+        bn = back * nn
         dgain_ref[...] = dgain_ref[...] + bn[0:8] + bn[8:16]
         b = back * gain_ref[0:1, :]
-        g = ogown[pl.ds(r0, 16), :].astype(F32) + scale * (b - n * jnp.mean(b * n, axis=-1, keepdims=True))
-        gres_ref[pl.ds(r0, 16), :] = g
-        shard[pl.ds(r0, 16), :] = g.astype(BF16).astype(F32)
+        g = og_ref[pl.ds(pl.multiple_of(mine.start + r, 16), 16), :].astype(F32) + scale * (b - nn * jnp.mean(b * nn, axis=-1, keepdims=True))
+        gres_ref[pl.ds(r, 16), :] = g
+        shard[pl.ds(r, 16), :] = g.astype(BF16).astype(F32)
         return 0
 
     lax.fori_loop(0, own // 16, finish, 0)
-    back = gather_copies(d, peers, shard, grecv, s2, r2)
-    for c in back:
-        c.start()
-    for c in copies2:
-        c.wait_recv()
-    ffn_own.wait()
-
-    def finish2(i, _):
-        r0 = pl.multiple_of(i * 16, 16)
-        total = oshard[pl.ds(r0, 16), :]
-        for j in range(N_TENSOR - 1):
-            total = total + orecv[j, pl.ds(r0, 16), :]
-        oshard[pl.ds(r0, 16), :] = (resid_in[pl.ds(r0, 16), :] + total).astype(BF16).astype(F32)
-        return 0
-
-    lax.fori_loop(0, own // 16, finish2, 0)
-    back2 = [
-        pltpu.make_async_remote_copy(
-            src_ref=oshard, dst_ref=out_ref.at[rows_t],
-            send_sem=s4.at[j], recv_sem=r4.at[j], device_id=(d, p), device_id_type=MESH)
-        for j, p in enumerate(peers)]
-    for c in back2:
-        c.start()
-    own_out = pltpu.make_async_copy(oshard, out_ref.at[rows_t], csem.at[2])
-    own_out.start()
-    gathered_out(t, shard, grecv, ga_ref, back, own)
-    for c in back2:
-        c.wait_recv()
-    own_out.wait()
-    for c in copies + back + copies2 + back2:
-        c.wait_send()
-
-
-def mid_exchange(gg, gu, wg, wu, ffn, resid, og, gain):
+    place = pltpu.make_async_copy(shard, whole.at[mine], csem)
+    place.start()
+    place.wait()
+    ga = Gather(ring, whole, gsem, own)
+    ga.start()
+    dp.second()
+    ga.middle()
+    dp.third()
+    ga.finish()
+    dp.finish(grads_ref)
+    sc.s.drain()
+    ga.s.drain()
+
+
+def mid_exchange(gg, gu, inner, wg, wu, hid, og, resid, gain):
     T, D = og.shape
-    own = T // N_TENSOR
+    own = T // NT_
+    n = 3 * gg.shape[1]
     sd = jax.ShapeDtypeStruct
     return pl.pallas_call(
         mid_kernel,
-        out_shape=(sd((T, D), BF16), sd((own, D), F32), sd((8, D), F32), sd((T, D), F32)),
-        in_specs=[VM, VM, VM, VM, ANY, VM, ANY, VM], out_specs=[VM, VM, VM, ANY],
-        scratch_shapes=[pltpu.VMEM((T, D), F32), pltpu.VMEM((7, own, D), F32), pltpu.VMEM((own, D), F32),
-                        pltpu.VMEM((7, own, D), F32), pltpu.VMEM((own, D), BF16), pltpu.VMEM((own, D), F32), pltpu.VMEM((7, own, D), F32),
-                        pltpu.SemaphoreType.DMA((3,))] + dma_sems(7, 7, 7, 7, 7, 7, 7, 7),
-        compiler_params=pltpu.CompilerParams(collective_id=2, has_side_effects=True, vmem_limit_bytes=58 * 2 ** 20),
+        out_shape=(sd((T, D), F32), sd((own, D), F32), sd((8, D), F32), sd((n, 128), F32)),
+        in_specs=[VM] * 9, out_specs=[ANY, VM, VM, VM],
+        scratch_shapes=[pltpu.VMEM((T, D), F32), pltpu.VMEM((own, D), F32), pltpu.VMEM((n, T), BF16),
+                        pltpu.SemaphoreType.DMA(())] + scatter_scratch(own) + gather_sems() + dp_scratch(n),
+        compiler_params=params(2, 60),
         name="mid_exchange",
-    )(gg, gu, wg, wu, ffn, resid, og, gain)
-
-
-def in_kernel(part_ref, gres_ref, x_ref, gain_ref, ig_ref, dgain_ref,
-              recv, shard, grecv, xown, pown, csem, s1, r1, s2, r2):
-    d, t, peers = tensor_peers()
+    )(gg, gu, inner, wg, wu, hid, og, resid, gain)
+
+
+SMALL = 40
+TAPS = 40
+
+
+def in_kernel(gq, gk, gv, gt, gba, low_ref, wq, wk, wv, wt, wba, hid_ref, ga_ref, gres_ref, x_ref, gain_ref, gains_ref, taps_ref,
+              whole, grads_ref, gains_out, taps_out,
+              part, shard, left, xown, g_own, g_recv, s_own, s_recv, csem, ssem, srsem, *rest):
+    scr, gsem, dscr = rest[:7], rest[7:9], rest[9:]
+    ring = Ring()
     own = gres_ref.shape[0]
-    rows_t = pl.ds(pl.multiple_of(t * own, own), own)
-    mine = pltpu.make_async_copy(x_ref.at[rows_t], xown, csem.at[0])
-    mine.start()
-    mine2 = pltpu.make_async_copy(part_ref.at[rows_t], pown, csem.at[1])
-    mine2.start()
-    greet(d, peers)
-    copies = scatter_copies(d, peers, part_ref, recv, s1, r1, own)
-    for c in copies:
-        c.start()
-    mine.wait()
-    mine2.wait()
-    for c in copies:
-        c.wait_recv()
-    dgain_ref[...] = jnp.zeros_like(dgain_ref)
-
-    def finish(i, _):
-        r0 = pl.multiple_of(i * 16, 16)
-        x = xown[pl.ds(r0, 16), :].astype(F32)
-        back = pown[pl.ds(r0, 16), :]
-        for j in range(N_TENSOR - 1):
-            back = back + recv[j, pl.ds(r0, 16), :]
+    mine = ring.rows(0, False, own)
+    fetch = pltpu.make_async_copy(x_ref.at[mine], xown, csem)
+    fetch.start()
+
+    def partial(i, _):
+        rows_w = pl.ds(pl.multiple_of(i * 256, 256), 256)
+        total = mm1(gq[...], wq[rows_w, :], NT) + mm1(gk[...], wk[rows_w, :], NT)
+        total = total + mm1(gv[...], wv[rows_w, :], NT) + mm1(gt[...], wt[rows_w, :], NT)
+        part[:, rows_w] = total + mm1(gba[...], wba[rows_w, :], NT)
+        return 0
+
+    lax.fori_loop(0, part.shape[1] // 256, partial, 0)
+
+    def compute(a, b, put):
+        hid = jnp.concatenate([hid_ref[:, a], hid_ref[:, b]], axis=1)
+        put(slice(0, 768), mm1(left[0:768, :], hid, NN))
+        put(slice(768, 1552), mm1(left[768:1552, :], hid, NN))
+        put(slice(1552, 2064), mm1(left[1552:, :], jnp.concatenate([ga_ref[:, a], ga_ref[:, b]], axis=1), NN))
+
+    dp = DpScatter(ring, dscr, compute)
+    t_peers = [(ring.d, lax.rem(ring.t + j, NT_)) for j in range(1, NT_)]
+    d_peers = [(lax.rem(ring.d + j, 16), ring.t) for j in range(1, 16)]
+    greet(t_peers + d_peers)
+    sc = Scatter(ring, part, scr, own)
+    sc.start()
+    left[0:256, :] = gq[...].T
+    left[256:512, :] = gk[...].T
+    left[512:1024, :] = gv[...].T
+    left[1024:1536, :] = gt[...].T
+    left[1536:1552, :] = gba[...].T[0:16]
+    left[1552:, :] = low_ref[...].T
+    dp.cores()
+    sc.middle()
+    dp.along()
+    fetch.wait()
+    sc.finish()
+    g_own[...] = gains_ref[...]
+
+    def finish(i, total):
+        r = pl.multiple_of(i * 16, 16)
+        x = xown[pl.ds(r, 16), :].astype(F32)
+        back = sc.value(r)
         scale = lax.rsqrt(jnp.mean(x * x, axis=-1, keepdims=True) + 1e-05)
-        n = x * scale
-        bn = back * n
-        dgain_ref[...] = dgain_ref[...] + bn[0:8] + bn[8:16]
+        nn = x * scale
+        total = total + jnp.sum(back * nn, axis=0, keepdims=True)
         b = back * gain_ref[0:1, :]
-        g = gres_ref[pl.ds(r0, 16), :] + scale * (b - n * jnp.mean(b * n, axis=-1, keepdims=True))
-        shard[pl.ds(r0, 16), :] = g.astype(BF16).astype(F32)
-        return 0
-
-    lax.fori_loop(0, own // 16, finish, 0)
-    back = gather_copies(d, peers, shard, grecv, s2, r2)
-    for c in back:
-        c.start()
-    gathered_out(t, shard, grecv, ig_ref, back, own)
-    for c in copies + back:
-        c.wait_send()
-
-
-def in_exchange(part, gres, inputs, gain):
+        g = gres_ref[pl.ds(r, 16), :] + scale * (b - nn * jnp.mean(b * nn, axis=-1, keepdims=True))
+        shard[pl.ds(r, 16), :] = g.astype(BF16).astype(F32)
+        return total
+
+    total = lax.fori_loop(0, own // 16, finish, jnp.zeros((1, x_ref.shape[1]), F32))
+    for j in range(16):
+        g_own[j:j + 1, :] = total[:, j * 128:(j + 1) * 128]
+    place = pltpu.make_async_copy(shard, whole.at[mine], csem)
+    place.start()
+    place.wait()
+    small = Sends(ssem, srsem)
+    for j, dev in enumerate(t_peers):
+        small.go(j, g_own, g_recv.at[j], dev)
+    ga = Gather(ring, whole, gsem, own)
+    ga.start()
+    dp.second()
+    for j, dev in enumerate(t_peers):
+        small.got(j, g_recv.at[j], dev)
+    gains = g_own[...]
+    for j in range(NT_ - 1):
+        gains = gains + g_recv[j]
+    s_own[0:SMALL, :] = gains
+    s_own[SMALL:, :] = taps_ref[...]
+    for j, dev in enumerate(d_peers):
+        small.go(7 + j, s_own, s_recv.at[j], dev)
+    ga.middle()
+    dp.third()
+    for j, dev in enumerate(d_peers):
+        small.got(7 + j, s_recv.at[j], dev)
+    both = s_own[...]
+    for j in range(15):
+        both = both + s_recv[j]
+    gains_out[...] = both[:SMALL]
+    taps_out[...] = both[SMALL:]
+    ga.finish()
+    dp.finish(grads_ref)
+    small.drain()
+    sc.s.drain()
+    ga.s.drain()
+
+
+def in_exchange(grads, low, weights, hid, ga, gres, inputs, gain, gains, taps):
     T, D = inputs.shape
-    own = T // N_TENSOR
+    own = T // NT_
+    n = 2064
     sd = jax.ShapeDtypeStruct
+    vm = lambda *s: pltpu.VMEM(s, F32)
     return pl.pallas_call(
         in_kernel,
-        out_shape=(sd((T, D), BF16), sd((8, D), F32)),
-        in_specs=[ANY, VM, ANY, VM], out_specs=[VM, VM],
-        scratch_shapes=[pltpu.VMEM((7, own, D), F32), pltpu.VMEM((own, D), F32),
-                        pltpu.VMEM((7, own, D), F32), pltpu.VMEM((own, D), BF16), pltpu.VMEM((own, D), F32), pltpu.SemaphoreType.DMA((2,))] + dma_sems(7, 7, 7, 7),
-        compiler_params=pltpu.CompilerParams(collective_id=3, has_side_effects=True, vmem_limit_bytes=56 * 2 ** 20),
+        out_shape=(sd((T, D), F32), sd((n, 128), F32), sd((SMALL, 128), F32), sd((TAPS, 128), F32)),
+        in_specs=[VM] * 14 + [ANY] + [VM] * 3, out_specs=[ANY, VM, VM, VM],
+        scratch_shapes=[vm(T, D), vm(own, D), pltpu.VMEM((n, T), BF16), pltpu.VMEM((own, D), BF16),
+                        vm(SMALL, 128), vm(7, SMALL, 128), vm(SMALL + TAPS, 128), vm(15, SMALL + TAPS, 128),
+                        pltpu.SemaphoreType.DMA(()), pltpu.SemaphoreType.DMA((22,)), pltpu.SemaphoreType.DMA((22,))]
+        + scatter_scratch(own) + gather_sems() + dp_scratch(n),
+        compiler_params=params(3, 60),
         name="in_exchange",
-    )(part, gres, inputs, gain)
+    )(*grads, low, *weights, hid, ga, gres, inputs, gain, gains, taps)
+
+
+def out_kernel(part, resid_in, whole, shard, csem, *rest):
+    scr, gsem = rest[:7], rest[7:]
+    ring = Ring()
+    own = resid_in.shape[0]
+    mine = ring.rows(0, False, own)
+    greet([ring.right, ring.left, ring.flip])
+    sc = Scatter(ring, part, scr, own)
+    sc.start()
+    sc.middle()
+    sc.finish()
+
+    def finish(i, _):
+        r = pl.multiple_of(i * 16, 16)
+        shard[pl.ds(r, 16), :] = (resid_in[pl.ds(r, 16), :] + sc.value(r)).astype(BF16).astype(F32)
+        return 0
+
+    lax.fori_loop(0, own // 16, finish, 0)
+    place = pltpu.make_async_copy(shard, whole.at[mine], csem)
+    place.start()
+    place.wait()
+    ga = Gather(ring, whole, gsem, own)
+    ga.start()
+    ga.middle()
+    ga.finish()
+    sc.s.drain()
+    ga.s.drain()
+
+
+def out_exchange(part, resid):
+    T, D = part.shape
+    own = T // NT_
+    return pl.pallas_call(
+        out_kernel,
+        out_shape=jax.ShapeDtypeStruct((T, D), F32),
+        in_specs=[VM, VM], out_specs=ANY,
+        scratch_shapes=[pltpu.VMEM((own, D), F32), pltpu.SemaphoreType.DMA(())] + scatter_scratch(own) + gather_sems(),
+        compiler_params=params(4, 56),
+        name="out_exchange",
+    )(part, resid)
 
 
 def matmul(left, right):
@@ -699,33 +1070,28 @@
     inner = (act * up_pre).astype(BF16)
     ffn = matmul(inner, w_down)
     grad_inner = matmul(out_grad, w_down.T)
-    grad_down = matmul(inner.T, out_grad)
     gg = (grad_inner * up_pre * sig * (1.0 + gate_pre * (1.0 - sig))).astype(BF16)
     gu = (grad_inner * act).astype(BF16)
-    grad_up_gate = matmul(hidden_mid.T, gg)
-    grad_up = matmul(hidden_mid.T, gu)
-    grad_attn, grad_resid, ffn_gain_part, out32 = mid_exchange(gg, gu, w_up_gate, w_up, ffn, resid, out_grad, rows8(ffn_gain))
-    outputs = out32.astype(BF16)
-    grad_out = matmul(low.T, grad_attn)
+    grad_attn, grad_resid, ffn_gain_part, grads_mid = mid_exchange(
+        gg, gu, inner, w_up_gate.T, w_up.T, hidden_mid, out_grad, resid, rows8(ffn_gain))
+    grad_attn = grad_attn.astype(BF16)
+    outputs = out_exchange(ffn, resid).astype(BF16)
     grad_mixed = matmul(grad_attn, w_out.T)
     gq, gk, gv, gt, gba, taps, small, hgain = mixer_bwd(
         seg3, grad_mixed, qp, kp, vp, gp, ba, conv_query, conv_key, conv_value, rate, bias, gain8, q, k, x, u, s, o)
-    grad_query = matmul(hidden_in.T, gq)
-    grad_key = matmul(hidden_in.T, gk)
-    grad_value = matmul(hidden_in.T, gv)
-    grad_gate = matmul(hidden_in.T, gt)
-    grad_ba = matmul(hidden_in.T, gba)
-    part = matmul(gq, w_query.T) + matmul(gk, w_key.T) + matmul(gv, w_value.T) + matmul(gt, w_gate.T) + matmul(gba, w_ba.T)
-    input_grad, attn_gain_part = in_exchange(part, grad_resid, inputs, rows8(attn_gain))
-    both = lax.psum((jnp.sum(attn_gain_part, axis=0), jnp.sum(ffn_gain_part, axis=0), hgain[0]), ("dp", "tensor"))
-    sums = lax.psum((taps[:4], small[:2, 2:4]), "dp")
-
-    def scatter(g, dim=0):
-        return lax.psum_scatter(g, "dp", scatter_dimension=dim, tiled=True)
-
-    return (outputs, input_grad, both[0], scatter(grad_query), scatter(grad_key), scatter(grad_value), scatter(grad_gate),
-            scatter(grad_ba[:, 0:2]), scatter(grad_ba[:, 2:4]), sums[0][:, 0:256], sums[0][:, 256:512], sums[0][:, 512:1024],
-            sums[1][1], sums[1][0], both[2], scatter(grad_out, 1), both[1], scatter(grad_up_gate), scatter(grad_up), scatter(grad_down, 1))
+    gains_in = jnp.concatenate([jnp.zeros((16, 128), F32), jnp.sum(ffn_gain_part, axis=0).reshape(16, 128), hgain[0].reshape(2, 128),
+                                jnp.zeros((SMALL - 34, 128), F32)], axis=0)
+    taps_in = jnp.concatenate([taps[:4].reshape(32, 128), small], axis=0)
+    ig, grads_in, gains, taps_sum = in_exchange(
+        (gq, gk, gv, gt, gba), low, (w_query, w_key, w_value, w_gate, w_ba), hidden_in, grad_attn, grad_resid, inputs,
+        rows8(attn_gain), gains_in, taps_in)
+    input_grad = ig.astype(BF16)
+    n = w_up.shape[1]
+    ct = taps_sum[:32].reshape(4, 1024)
+    return (outputs, input_grad, gains[:16].reshape(D), grads_in[0:256].T, grads_in[256:512].T, grads_in[512:1024].T, grads_in[1024:1536].T,
+            grads_in[1536:1538].T, grads_in[1538:1540].T, ct[:, 0:256], ct[:, 256:512], ct[:, 512:],
+            taps_sum[33, 2:4], taps_sum[32, 2:4], gains[32:34].reshape(256), grads_in[1552:], gains[16:32].reshape(D),
+            grads_mid[0:n].T, grads_mid[n:2 * n].T, grads_mid[2 * n:])
 
 
 def solution(mesh):

time: 1290 us -> 651 us (0.50)
  waiting for transfers between devices: 288 us -> 0 us
  Pallas kernels: 693 us -> 562 us
  blocking collectives: 128 us -> 0 us
  matrix products: 104 us -> 34.5 us
  local copies, waits for them, and re-layouts: 34.5 us -> 18.6 us
  between operations: 15 us -> 1.22 us
    reduce_scatter x8 -> x0, waiting for transfers between devices: 288 us -> none  [scatter(): return lax.psum_scatter(g, 'dp', scatter_dimension=dim, tiled=True)]
    psum x2 -> x0, blocking collectives: 128 us -> none  [the longest x1 72 us: per_device(): lax.psum((jnp.sum(attn_gain_part, axis=0), jnp.sum(ffn_gain_part, axis=0)...]
    pallas_call x2 -> x3, Pallas kernels: 463 us -> 386 us  [the longest x1 154 us: in_exchange(): pl.pallas_call(in_kernel, out_shape=(sd((T, D), F32), sd((n, 128), F32),...]
    dot_general x24 -> x10, matrix products: 104 us -> 34.5 us  [matmul(): return jnp.dot(left, right, preferred_element_type=F32)]
    pallas_call x1, Pallas kernels: 153 us -> 101 us  [attn_exchange(): pl.pallas_call(attn_kernel, out_shape=(sd((T, D), BF16), sd((own, D), F32...]
    unnamed x85 -> x56, local copies, waits for them, and re-layouts: 27.2 us -> 4.67 us
  transfers between devices with their start and end apart: 10 -> 0, of which waited for: 5 -> 0; matrix products, arithmetic and copies ran while one was open for 6% -> 0% of each run, Pallas kernels for 14% -> 0%
where the time goes in v2:
time: 651 us; the launch traced here: 642 us
  Pallas kernels  562 us (86%)
  matrix products  34.5 us (5%)
  other arithmetic  26 us (4%)
  local copies, waits for them, and re-layouts  18.6 us (3%)
    pallas_call x1, Pallas kernels, in_exchange(): pl.pallas_call(in_kernel, out_shape=(sd((T, D), F32), sd((n, 128), F32),...  154 us
    pallas_call x1, Pallas kernels, mid_exchange(): pl.pallas_call(mid_kernel, out_shape=(sd((T, D), F32), sd((own, D), F32),...  139 us
    pallas_call x1, Pallas kernels, attn_exchange(): pl.pallas_call(attn_kernel, out_shape=(sd((T, D), BF16), sd((own, D), F32...  101 us
    pallas_call x1, Pallas kernels, out_exchange(): pl.pallas_call(out_kernel, out_shape=jax.ShapeDtypeStruct((T, D), F32), i...  92.9 us
    pallas_call x1, Pallas kernels, mixer_bwd(): pl.pallas_call(functools.partial(bwd_kernel, blocks), out_shape=(sd((T, 2...  49.8 us
    dot_general x10, matrix products, matmul(): return jnp.dot(left, right, preferred_element_type=F32)  34.5 us
    pallas_call x1, Pallas kernels, mixer_fwd(): pl.pallas_call(functools.partial(fwd_kernel, blocks, group), out_shape=(s...  25.5 us

profile of v2, /device:TPU:24, one launch (start us, length us, event | category | flops | bytes accessed | tf_op | source)
XLA Modules:
  0.0 642.0 jit_solution(3869532107028040758)
XLA Ops:
  0.7 0.8 convert_bitcast_fusion
  2.2 1.0 maximum_bitcast_fusion
  3.3 0.7 maximum_maximum_fusion.1.seg_ref
  4.0 2.6 fusion
  6.7 2.5 fusion.2.hid_ref
  9.4 1.1 copy.85
  10.6 1.4 maximum_maximum_fusion.wba
  12.0 3.8 fusion.11.ba_ref
  15.8 3.0 fusion.10.gp_ref
  18.8 2.9 fusion.9.vp_ref
  21.7 1.9 fusion.7.qp_ref
  23.6 1.9 fusion.8.kp_ref
  25.5 1.1 compare_reduce_fusion
  26.6 0.7 broadcast_select_fusion
  27.3 0.6 scatter.15.rate_ref
  28.0 0.6 scatter.17.bias_ref
  28.6 0.6 broadcast_in_dim.22.gain_ref
  29.2 25.5 %mixer_forward.1 = (bf16[768,512]{1,0:T(8,128)(2,1)}, f32[768,256]{1,0:T(8,128)}, f32[768,256]{1,0:T(8,128)}, f32[768,256]{1,0:T(8,128)}, f32[768,512]{1,0:T(8,1...) custom-call(f32[6,8,128]{2,1,0:T(8,128)} %maximum_maximum_fusion.1.seg_ref, f32[768,256]{1,0:T(8,128)} %fusion.7.qp_ref, ...), custom_call_target="tpu_custom_call" | custom-call | tf_op jit(solution)/shard_map/mixer_forward/pallas_call | solution.py:203
  54.7 0.6 broadcast_in_dim.23.gain_ref
  55.3 100.8 %attn_exchange.1 = (bf16[768,2048]{1,0:T(8,128)(2,1)}, f32[96,2048]{1,0:T(8,128)}) custom-call(bf16[768,512]{1,0:T(8,128)(2,1)} %get-tuple-element.69.low_ref, bf16[512,2048]{1,0:T(8,128)(2,1)} %w_ref.1, bf16[768,2048]{1,0:T(8,128)(2,1)} %x_ref.3, f32[8,2048]{1,0:T(8,128)} %broadcast_in_dim.23.gain_ref), custom_call_target="tpu_custom_call" | custom-call | tf_op jit(solution)/shard_map/attn_exchange/pallas_call | solution.py:792
  156.2 4.7 fusion.12
  160.9 2.6 fusion.13
  163.6 4.8 multiply_convert_fusion
  168.4 138.7 %mid_exchange.1 = (f32[768,2048]{1,0:T(8,128)}, f32[96,2048]{1,0:T(8,128)}, f32[8,2048]{1,0:T(8,128)}, f32[2112,128]{1,0:T(8,128)}) custom-call(bf16[768,704]{1,0:T(8,128)(2,1)} %get-tuple-element.175.gg_ref, bf16[768,704]{1,0:T(8,128)(2,1)} %get-tuple-element.174.gu_ref, bf16[768,704]{1,0:T(8,128)(2,1)} %get-tuple-element.176.inner_ref, ...), custom_call_target="tpu_custom_call" | custom-call | tf_op jit(solution)/shard_map/mid_exchange/pallas_call | solution.py:872
  307.1 3.4 convert_element_type.34.ga_ref
  310.6 3.0 fusion.15.gm_ref
  313.6 49.8 %mixer_backward.1 = (bf16[768,256]{1,0:T(8,128)(2,1)}, bf16[768,256]{1,0:T(8,128)(2,1)}, bf16[768,512]{1,0:T(8,128)(2,1)}, bf16[768,512]{1,0:T(8,128)(2,1)}, bf1...) custom-call(f32[6,8,128]{2,1,0:T(8,128)} %maximum_maximum_fusion.1.seg_ref, ...), custom_call_target="tpu_custom_call" | custom-call | tf_op jit(solution)/shard_map/mixer_backward/pallas_call | solution.py:399
  363.4 0.8 slice.104
  364.2 1.3 pad_maximum_fusion.taps_ref
  365.5 0.7 slice.103
  366.3 0.7 maximum_maximum_fusion.2.gains_ref
  367.0 0.6 broadcast_in_dim.24.gain_ref
  367.6 154.0 %in_exchange.1 = (f32[768,2048]{1,0:T(8,128)}, f32[2064,128]{1,0:T(8,128)}, f32[40,128]{1,0:T(8,128)}, f32[40,128]{1,0:T(8,128)}) custom-call(bf16[768,256]{1,0:T(8,128)(2,1)} %get-tuple-element.79.gq, bf16[768,256]{1,0:T(8,128)(2,1)} %get-tuple-element.80.gk, bf16[768,512]{1,0:T(8,128)(2,1)} %get-tuple-element.81.gv, ...), custom_call_target="tpu_custom_call" | custom-call | tf_op jit(solution)/shard_map/in_exchange/pallas_call | solution.py:986
  521.7 5.0 convert_element_type.35
  526.7 0.8 fusion.5
  527.5 0.8 copy.100
  528.3 0.8 copy.99
  529.1 1.0 slice_bitcast_fusion.4
  530.1 0.8 copy.97
  530.9 0.8 copy.98
  531.6 0.6 fusion.6
  532.2 0.6 slice.128
  532.8 0.6 slice_bitcast_fusion.6
  533.5 1.3 slice_bitcast_fusion.9
  535.9 2.2 fusion.4
  538.1 5.8 fusion.14.part
  543.9 92.9 %out_exchange.1 = f32[768,2048]{1,0:T(8,128)} custom-call(f32[768,2048]{1,0:T(8,128)} %fusion.14.part, f32[96,2048]{1,0:T(8,128)} %get-tuple-element.71.resid_in), custom_call_target="tpu_custom_call" | custom-call | tf_op jit(solution)/shard_map/out_exchange/pallas_call | solution.py:1030
  636.8 4.9 convert_element_type.31
  (71 shorter events, 2.8 us)
Async XLA Ops:
  0.7 162.9 %copy-start = (bf16[704,2048]{1,0:T(8,128)(2,1)S(1)}, bf16[704,2048]{1,0:T(8,128)(2,1)}, u32[]{:S(2)}) copy-start(bf16[704,2048]{1,0:T(8,128)(2,1)} %param.44) | copy-start | bytes 8650756
  0.7 5.9 copy-start.16
  1.7 4.9 copy-start.1
  6.6 2.5 copy-start.19
  6.6 2.8 copy-start.20
  11.9 6.9 %copy-start.4 = (bf16[2048,128]{1,0:T(8,128)(2,1)}, bf16[2048,128]{1,0:T(8,128)(2,1)S(1)}, u32[]{:S(2)}) copy-start(bf16[2048,128]{1,0:T(8,128)(2,1)S(1)} %maximum_maximum_fusion.wba) | copy-start | bytes 1572868
  11.9 3.9 copy-start.2
  12.0 3.9 copy-start.11
  15.8 3.0 copy-start.10
  18.8 3.0 copy-start.12
  21.7 1.9 copy-start.13
  23.6 3.0 copy-start.23
  23.6 3.0 copy-start.24
  23.6 5.0 copy-start.22
  25.5 29.2 %copy-start.21 = (f32[2048]{0:T(1024)S(1)}, f32[2048]{0:T(1024)}, u32[]{:S(2)}) copy-start(f32[2048]{0:T(1024)} %param.41) | copy-start | bytes 24580
  55.3 100.8 %copy-start.7 = (bf16[2048,704]{0,1:T(8,128)(2,1)S(1)}, bf16[2048,704]{0,1:T(8,128)(2,1)}, u32[]{:S(2)}) copy-start(bf16[2048,704]{0,1:T(8,128)(2,1)} %param.42) | copy-start | bytes 8650756
  156.2 4.7 copy-start.6
  156.2 4.7 copy-start.8
  160.9 2.7 copy-start.5
  307.1 3.4 copy-start.9
  310.6 3.0 copy-start.3
  313.6 52.6 %copy-start.15 = (f32[8,2048]{1,0:T(8,128)S(1)}, f32[8,2048]{1,0:T(8,128)}, u32[]{:S(2)}) copy-start(f32[8,2048]{1,0:T(8,128)} %get-tuple-element.85) | copy-start | bytes 196612
  521.7 5.0 copy-start.14
  526.7 4.9 copy-start.18
  526.7 6.2 copy-start.17

commit v3 on v1

--- a/solution.py
+++ b/solution.py
@@ -212,11 +212,405 @@
     )(seg3, qp, kp, vp, gp, ba, cq, ck, cv, rate, bias, gain)
 
 
-def bwd_kernel(blocks, seg_ref, gm_ref, qp_ref, kp_ref, vp_ref, gp_ref, ba_ref, cq_ref, ck_ref, cv_ref, rate_ref, bias_ref, gain_ref,
+MESH = pl.DeviceIdType.MESH
+NT_ = 8
+ZH, YH = 512, 512
+
+
+def run(steps, count=None):
+    if count is None:
+        for _ in steps:
+            pass
+    else:
+        for _ in range(count):
+            next(steps)
+
+
+class Ring:
+    def __init__(self):
+        self.d = lax.axis_index("dp")
+        self.t = lax.axis_index("tensor")
+        self.y = lax.rem(self.t, 2)
+        self.z = self.t // 2
+        self.right = (self.d, self.at(1) * 2 + self.y)
+        self.left = (self.d, self.at(3) * 2 + self.y)
+        self.flip = (self.d, self.z * 2 + 1 - self.y)
+
+    def at(self, k):
+        return lax.rem(self.z + k, 4)
+
+    def rows(self, k, other, own):
+        side = 1 - self.y if other else self.y
+        return pl.ds(pl.multiple_of((self.at(k) * 2 + side) * own, own), own)
+
+    def quarter(self, k, own):
+        return pl.ds(pl.multiple_of(self.at(k) * 2 * own, 2 * own), 2 * own)
+
+
+class Sends:
+    def __init__(self, ssem, rsem):
+        self.ssem, self.rsem, self.made = ssem, rsem, []
+
+    def make(self, i, src, dst, device):
+        return pltpu.make_async_remote_copy(src_ref=src, dst_ref=dst, send_sem=self.ssem.at[i], recv_sem=self.rsem.at[i],
+                                            device_id=device, device_id_type=MESH)
+
+    def go(self, i, src, dst, device):
+        c = self.make(i, src, dst, device)
+        c.start()
+        self.made.append(c)
+
+    def got(self, i, dst, device):
+        self.make(i, dst, dst, device).wait_recv()
+
+    def drain(self):
+        for c in self.made:
+            c.wait_send()
+
+
+def greet(devices):
+    barrier = pltpu.get_barrier_semaphore()
+    for dev in devices:
+        pl.semaphore_signal(barrier, inc=1, device_id=dev, device_id_type=MESH)
+    pl.semaphore_wait(barrier, len(devices))
+
+
+ZA, ZB, ZZ = pl.ds(0, ZH), pl.ds(ZH, ZH), pl.ds(0, 2 * ZH)
+YA, YB, YY = pl.ds(2 * ZH, YH), pl.ds(2 * ZH + YH, YH), pl.ds(2 * ZH, 2 * YH)
+GZH, GYH = 640, 384
+GZA, GZB, GZZ = pl.ds(0, GZH), pl.ds(GZH, GZH), pl.ds(0, 2 * GZH)
+GYA, GYB, GYY = pl.ds(2 * GZH, GYH), pl.ds(2 * GZH + GYH, GYH), pl.ds(2 * GZH, 2 * GYH)
+ZLO, ZHI, YLO, YHI = pl.ds(0, ZH), pl.ds(ZH, ZH), pl.ds(0, YH), pl.ds(YH, YH)
+
+
+def scatter_scratch(own):
+    return [pltpu.VMEM((4, own, 2 * YH), F32), pltpu.VMEM((6, 2 * own, ZH), F32), pltpu.VMEM((6, own, YH), F32),
+            pltpu.VMEM((own, 2 * ZH), F32), pltpu.VMEM((own, 2 * ZH), F32),
+            pltpu.SemaphoreType.DMA((17,)), pltpu.SemaphoreType.DMA((17,))]
+
+
+def add_rows(dst, src_of, n):
+    def one(i, _):
+        r = pl.multiple_of(i * 16, 16)
+        dst[pl.ds(r, 16), :] = dst[pl.ds(r, 16), :] + src_of(r)
+        return 0
+    lax.fori_loop(0, n // 16, one, 0)
+
+
+def sub(ref, rows, cols):
+    return lambda r: ref[pl.ds(pl.multiple_of(rows.start + r, 16), 16), cols]
+
+
+class Scatter:
+    def __init__(self, ring, part, scratch, own):
+        self.ring, self.part, self.own = ring, part, own
+        self.yb, self.zb, self.yr, self.zsend, self.zf, ssem, rsem = scratch
+        self.s = Sends(ssem, rsem)
+
+    ORDER = (2, 1, 3, 0)
+
+    def start(self, k):
+        g, s, p, own = self.ring, self.s, self.part, self.own
+        if k == 2:
+            s.go(0, p.at[g.quarter(2, own), ZB], self.zb.at[0], g.right)
+            s.go(1, p.at[g.quarter(2, own), ZA], self.zb.at[1], g.left)
+        if k == 1:
+            s.go(2, p.at[g.quarter(1, own), ZA], self.zb.at[2], g.right)
+        if k == 3:
+            s.go(3, p.at[g.quarter(3, own), ZB], self.zb.at[3], g.left)
+        s.go({2: 6, 1: 7, 3: 8, 0: 9}[k], p.at[g.rows(k, True, own), YY], self.yb.at[k], g.flip)
+
+    def middle(self):
+        g, s, p, own = self.ring, self.s, self.part, self.own
+        yb, zb, yr = self.yb, self.zb, self.yr
+        s.got(6, yb.at[2], g.flip)
+        add_rows(yb.at[2], sub(p, g.rows(2, False, own), YY), own)
+        s.go(10, yb.at[2, :, YHI], yr.at[0], g.right)
+        s.go(11, yb.at[2, :, YLO], yr.at[1], g.left)
+        yield
+        s.got(0, zb.at[0], g.left)
+        add_rows(zb.at[0], sub(p, g.quarter(1, own), ZB), 2 * own)
+        s.go(4, zb.at[0], zb.at[4], g.right)
+        s.got(1, zb.at[1], g.right)
+        add_rows(zb.at[1], sub(p, g.quarter(3, own), ZA), 2 * own)
+        s.go(5, zb.at[1], zb.at[5], g.left)
+        yield
+        s.got(7, yb.at[1], g.flip)
+        add_rows(yb.at[1], sub(p, g.rows(1, False, own), YY), own)
+        s.go(12, yb.at[1, :, YLO], yr.at[2], g.right)
+        s.got(10, yr.at[0], g.left)
+        add_rows(yr.at[0], lambda r: yb[1, pl.ds(r, 16), YHI], own)
+        s.go(14, yr.at[0], yr.at[4], g.right)
+        yield
+        s.got(8, yb.at[3], g.flip)
+        add_rows(yb.at[3], sub(p, g.rows(3, False, own), YY), own)
+        s.go(13, yb.at[3, :, YHI], yr.at[3], g.left)
+        s.got(11, yr.at[1], g.right)
+        add_rows(yr.at[1], lambda r: yb[3, pl.ds(r, 16), YLO], own)
+        s.go(15, yr.at[1], yr.at[5], g.left)
+        yield
+        s.got(2, zb.at[2], g.left)
+        s.got(3, zb.at[3], g.right)
+        s.got(4, zb.at[4], g.left)
+        s.got(5, zb.at[5], g.right)
+        base = g.rows(0, True, own).start
+        lead = (1 - g.y) * own
+
+        def one(i, _):
+            r = pl.multiple_of(i * 16, 16)
+            at = pl.ds(pl.multiple_of(lead + r, 16), 16)
+            mine = pl.ds(pl.multiple_of(base + r, 16), 16)
+            self.zsend[pl.ds(r, 16), ZLO] = p[mine, ZA] + (zb[2, at, :] + zb[5, at, :])
+            self.zsend[pl.ds(r, 16), ZHI] = p[mine, ZB] + (zb[3, at, :] + zb[4, at, :])
+            return 0
+
+        lax.fori_loop(0, own // 16, one, 0)
+        s.go(16, self.zsend, self.zf, g.flip)
+        yield
+
+    def finish(self):
+        g, s = self.ring, self.s
+        s.got(9, self.yb.at[0], g.flip)
+        s.got(12, self.yr.at[2], g.left)
+        s.got(13, self.yr.at[3], g.right)
+        s.got(14, self.yr.at[4], g.left)
+        s.got(15, self.yr.at[5], g.right)
+        s.got(16, self.zf, g.flip)
+
+    def value(self, r):
+        g, p, own = self.ring, self.part, self.own
+        zb, yr = self.zb, self.yr
+        at = pl.ds(pl.multiple_of(g.y * own + r, 16), 16)
+        here = pl.ds(r, 16)
+        mine = pl.ds(pl.multiple_of(g.rows(0, False, own).start + r, 16), 16)
+        za = p[mine, ZA] + (zb[2, at, :] + zb[5, at, :]) + self.zf[here, ZLO]
+        zz = p[mine, ZB] + (zb[3, at, :] + zb[4, at, :]) + self.zf[here, ZHI]
+        ya = p[mine, YA] + self.yb[0, here, YLO] + (yr[2, here, :] + yr[5, here, :])
+        yz = p[mine, YB] + self.yb[0, here, YHI] + (yr[3, here, :] + yr[4, here, :])
+        return jnp.concatenate([za, zz, ya, yz], axis=1)
+
+
+def gather_sems():
+    return [pltpu.SemaphoreType.DMA((17,)), pltpu.SemaphoreType.DMA((17,))]
+
+
+class Gather:
+    def __init__(self, ring, whole, sems, own):
+        self.ring, self.whole, self.own = ring, whole, own
+        self.s = Sends(*sems)
+
+    def _go(self, i, rows, cols, device):
+        ref = self.whole.at[rows, cols]
+        self.s.go(i, ref, ref, device)
+
+    def _got(self, i, rows, cols, device):
+        self.s.got(i, self.whole.at[rows, cols], device)
+
+    def start(self):
+        g, own = self.ring, self.own
+        mine = g.rows(0, False, own)
+        self._go(0, mine, GYY, g.right)
+        self._go(1, mine, GYY, g.left)
+        self._go(2, mine, GZZ, g.flip)
+        self._go(3, mine, GZZ, g.right)
+        self._go(4, mine, GZZ, g.left)
+        self._go(5, mine, GYY, g.flip)
+
+    def middle(self):
+        g, own = self.ring, self.own
+        lf, rt = g.rows(3, False, own), g.rows(1, False, own)
+        lo, ro = g.rows(3, True, own), g.rows(1, True, own)
+        far, faro, other = g.rows(2, False, own), g.rows(2, True, own), g.rows(0, True, own)
+        self._got(0, lf, GYY, g.left)
+        self._go(6, lf, GYB, g.right)
+        self._go(7, lf, GYY, g.flip)
+        self._got(1, rt, GYY, g.right)
+        self._go(8, rt, GYA, g.left)
+        self._go(9, rt, GYY, g.flip)
+        self._got(2, other, GZZ, g.flip)
+        self._go(10, other, GZZ, g.right)
+        self._go(11, other, GZZ, g.left)
+        yield
+        self._got(6, far, GYB, g.left)
+        self._got(8, far, GYA, g.right)
+        self._go(12, far, GYY, g.flip)
+        yield
+        self._got(3, lf, GZZ, g.left)
+        self._go(13, lf, GZB, g.right)
+        self._got(4, rt, GZZ, g.right)
+        self._go(14, rt, GZA, g.left)
+        yield
+        self._got(10, lo, GZZ, g.left)
+        self._go(15, lo, GZB, g.right)
+        self._got(11, ro, GZZ, g.right)
+        self._go(16, ro, GZA, g.left)
+        yield
+
+    def finish(self):
+        g, own = self.ring, self.own
+        far, faro, other = g.rows(2, False, own), g.rows(2, True, own), g.rows(0, True, own)
+        self._got(5, other, GYY, g.flip)
+        self._got(7, g.rows(3, True, own), GYY, g.flip)
+        self._got(9, g.rows(1, True, own), GYY, g.flip)
+        self._got(12, faro, GYY, g.flip)
+        self._got(13, far, GZB, g.left)
+        self._got(14, far, GZA, g.right)
+        self._got(15, faro, GZB, g.left)
+        self._got(16, faro, GZA, g.right)
+
+
+class DpScatter:
+    ORDER = (2, 1, 3, 0)
+
+    def __init__(self, ring, scratch, compute):
+        d, t = ring.d, ring.t
+        self.c, self.x, self.y = lax.rem(d, 2), lax.rem(d // 2, 4), d // 8
+        self.pair = (d + 1 - 2 * self.c, t)
+        self.right = ((self.y * 4 + self.step(1)) * 2 + self.c, t)
+        self.left = ((self.y * 4 + self.step(3)) * 2 + self.c, t)
+        self.far = (((1 - self.y) * 4 + self.x) * 2 + self.c, t)
+        self.csend, self.crecv, self.xr, self.yr, ssem, rsem = scratch
+        self.s = Sends(ssem, rsem)
+        self.compute = compute
+
+    def step(self, k):
+        return lax.rem(self.x + k, 4)
+
+    def devices(self):
+        return [self.pair, self.right, self.left, self.far]
+
+    def cols(self, k, side, core):
+        return pl.ds(pl.multiple_of(((side * 4 + self.step(k)) * 2 + core) * 128, 128), 128)
+
+    def cores(self):
+        slots, sent = self.csend.shape[0], []
+        for n, k in enumerate(self.ORDER):
+            slot = 2 * n % slots
+            for c in sent[:2] if 2 * n >= slots else []:
+                c.wait_send()
+            sent = sent[2:] if 2 * n >= slots else sent
+
+            def put(rows, both):
+                self.csend[slot, rows, :] = both[:, :128]
+                self.csend[slot + 1, rows, :] = both[:, 128:]
+
+            self.compute(self.cols(k, 0, 1 - self.c), self.cols(k, 1, 1 - self.c), put)
+            for side in range(2):
+                c = self.s.make(2 * k + side, self.csend.at[slot + side], self.crecv.at[2 * k + side], self.pair)
+                c.start()
+                sent.append(c)
+            yield
+        self.s.made += sent
+
+    def along(self):
+        s, acc, xr = self.s, self.crecv, self.xr
+        for k in self.ORDER:
+            for side in range(2):
+                s.got(2 * k + side, acc.at[2 * k + side], self.pair)
+
+            def put(rows, both):
+                acc[2 * k, rows, :] = acc[2 * k, rows, :] + both[:, :128]
+                acc[2 * k + 1, rows, :] = acc[2 * k + 1, rows, :] + both[:, 128:]
+
+            self.compute(self.cols(k, 0, self.c), self.cols(k, 1, self.c), put)
+            if k == 2:
+                s.go(8, acc.at[5], xr.at[0], self.right)
+                s.go(9, acc.at[4], xr.at[1], self.left)
+            if k == 1:
+                s.go(10, acc.at[2], xr.at[2], self.right)
+            if k == 3:
+                s.go(11, acc.at[7], xr.at[3], self.left)
+            yield
+
+    def second(self):
+        s, acc, xr = self.s, self.crecv, self.xr
+        n = acc.shape[1]
+        s.got(8, xr.at[0], self.left)
+        add_rows(xr.at[0], lambda r: acc[3, pl.ds(r, 16), :], n)
+        s.go(12, xr.at[0], xr.at[4], self.right)
+        s.got(9, xr.at[1], self.right)
+        add_rows(xr.at[1], lambda r: acc[6, pl.ds(r, 16), :], n)
+        s.go(13, xr.at[1], xr.at[5], self.left)
+
+    def third(self):
+        s, acc, xr = self.s, self.crecv, self.xr
+        n = acc.shape[1]
+        s.got(10, xr.at[2], self.left)
+        s.got(13, xr.at[5], self.right)
+        add_rows(acc.at[0], lambda r: xr[2, pl.ds(r, 16), :] + xr[5, pl.ds(r, 16), :], n)
+        s.got(11, xr.at[3], self.right)
+        s.got(12, xr.at[4], self.left)
+        add_rows(acc.at[1], lambda r: xr[3, pl.ds(r, 16), :] + xr[4, pl.ds(r, 16), :], n)
+        s.go(14, acc.at[1 - self.y], self.yr, self.far)
+
+    def finish(self, out_ref):
+        self.s.got(14, self.yr, self.far)
+        n = self.yr.shape[0]
+
+        def one(i, _):
+            r = pl.ds(pl.multiple_of(i * 16, 16), 16)
+            out_ref[r, :] = self.crecv[self.y, r, :] + self.yr[r, :]
+            return 0
+
+        lax.fori_loop(0, n // 16, one, 0)
+        self.s.drain()
+
+
+def together(sc, dp):
+    steps, cores, along = sc.middle(), dp.cores(), dp.along()
+    run(cores, 2)
+    run(steps, 2)
+    run(along, 1)
+    run(cores)
+    run(steps, 1)
+    run(along, 2)
+    run(steps, 1)
+    run(along)
+    run(steps)
+
+
+def dp_scratch(n, slots=8):
+    return [pltpu.VMEM((slots, n, 128), F32), pltpu.VMEM((8, n, 128), F32), pltpu.VMEM((6, n, 128), F32), pltpu.VMEM((n, 128), F32),
+            pltpu.SemaphoreType.DMA((15,)), pltpu.SemaphoreType.DMA((15,))]
+
+
+def params(cid, mib):
+    return pltpu.CompilerParams(collective_id=cid, has_side_effects=True, vmem_limit_bytes=mib * 2 ** 20)
+
+
+VM = pl.BlockSpec(memory_space=pltpu.VMEM)
+ANY = pl.BlockSpec(memory_space=pl.ANY)
+
+
+def bwd_kernel(blocks, seg_ref, ga_ref, wout_ref, low_ref, ffn_ref, resid_ref, qp_ref, kp_ref, vp_ref, gp_ref, ba_ref, cq_ref, ck_ref, cv_ref, rate_ref, bias_ref, gain_ref,
                q_ref, k_ref, x_ref, u_ref, s_ref, o_ref,
-               dqp_ref, dkp_ref, dvp_ref, dgp_ref, dba_ref, dtap_ref, dsmall_ref, dgain_ref,
-               qpad, kpad, vpad, segpad, do_s, y0_s, z_s, r_s, y_s, ds_s, dq_s, dk_s, dv_s, acc_s):
+               dqp_ref, dkp_ref, dvp_ref, dgp_ref, dba_ref, dtap_ref, dsmall_ref, dgain_ref, oshard_ref, grads_ref,
+               qpad, kpad, vpad, segpad, gm_ref, do_s, y_s, z_s, ds_s, dq_s, dk_s, left, *rest):
     T = blocks * L
+    scr, dscr = rest[:7], rest[7:]
+    own = resid_ref.shape[0]
+    ring = Ring()
+
+    def compute(a, b, put):
+        put(slice(0, 512), mm1(left[...], jnp.concatenate([ga_ref[:, a], ga_ref[:, b]], axis=1), NN))
+
+    dp = DpScatter(ring, dscr, compute)
+    greet([ring.right, ring.left, ring.flip] + dp.devices())
+    sc = Scatter(ring, ffn_ref, scr, own)
+    for k in sc.ORDER:
+        sc.start(k)
+    left[...] = low_ref[...].T
+    steps, cores, along = sc.middle(), dp.cores(), dp.along()
+    run(cores)
+
+    def mixed_back(i, _):
+        r = pl.ds(pl.multiple_of(i * 256, 256), 256)
+        gm_ref[r, :] = mm1(ga_ref[r, :], wout_ref[...], NT)
+        return 0
+
+    lax.fori_loop(0, T // 256, mixed_back, 0)
+    run(along)
+    run(steps, 1)
     rate, bias = rate_ref[0:1, :], bias_ref[0:1, :]
     for pad, src in ((qpad, qp_ref), (kpad, kp_ref), (vpad, vp_ref)):
         pad[0:PAD, :] = jnp.zeros((PAD, pad.shape[1]), F32)
@@ -256,12 +650,16 @@
             sx = split(x_ref[pl.ds(base, L), kc])
             y0 = mm3(sx, split(mm3(split(p), sdo, TN)), TN)
             z = mm3(sx, split(k * (last_decay * beta_col)), TN)
-            y0_s[pl.ds(base, L), vc] = y0
+            y_s[pl.ds(base, L), vc] = y0
             z_s[pl.ds(base, L), kc] = z
-            r_s[pl.ds(base, L), vc] = mm3(split(q * carry), sdo, TN)
+            ds_s[pl.ds(base, L), vc] = mm3(split(q * carry), sdo, TN)
         return 0
 
-    lax.fori_loop(0, blocks, phase_1, 0)
+    lax.fori_loop(0, blocks // 2, phase_1, 0)
+    run(steps, 1)
+    lax.fori_loop(blocks // 2, blocks, phase_1, 0)
+    run(steps, 1)
+    dp.second()
 
     def phase_2(i, grads):
         b = blocks - 1 - i
@@ -273,15 +671,18 @@
             kc = slice(h * 128, h * 128 + 128)
             vc = slice(h * 256, h * 256 + 256)
             ds = grads[h]
+            kept = ds_s[pl.ds(base, L), vc]
             ds_s[pl.ds(base, L), vc] = ds
-            y = y0_s[pl.ds(base, L), vc] + mm3(split(z_s[pl.ds(base, L), kc]), split(ds))
+            y = y_s[pl.ds(base, L), vc] + mm3(split(z_s[pl.ds(base, L), kc]), split(ds))
             y_s[pl.ds(base, L), vc] = y
-            new.append(carry[L - 1:L, :] * ds + r_s[pl.ds(base, L), vc]
+            new.append(carry[L - 1:L, :] * ds + kept
                        - mm3(split(k_ref[pl.ds(base, L), kc] * carry), split(y), TN))
         return tuple(new)
 
     zero = jnp.zeros((128, 256), F32)
     lax.fori_loop(0, blocks, phase_2, (zero, zero))
+    run(steps)
+    dp.third()
 
     def phase_3(b, _):
         base = pl.multiple_of(b * L, L)
@@ -341,9 +742,19 @@
         return 0
 
     lax.fori_loop(0, blocks, phase_3, 0)
+    sc.finish()
+
+    def finish(i, _):
+        r = pl.ds(pl.multiple_of(i * 16, 16), 16)
+        oshard_ref[r, :] = (resid_ref[r, :] + sc.value(pl.multiple_of(i * 16, 16))).astype(BF16).astype(F32)
+        return 0
+
+    lax.fori_loop(0, own // 16, finish, 0)
+    dp.finish(grads_ref)
+    sc.s.drain()
 
     def conv_back(pre, taps_ref, src, out_ref, cols, tap_cols, scale):
-        acc_s[T:, cols] = jnp.zeros((PAD, 128), F32)
+        do_s[T:, cols] = jnp.zeros((PAD, 128), F32)
 
         def one(b, tap_grads):
             base = pl.multiple_of(b * L, L)
@@ -355,7 +766,7 @@
                 r = lax.rsqrt(jnp.sum(act * act, axis=-1, keepdims=True) + 1e-06)
                 d = (scale * r) * (d - act * (r * r * jnp.sum(d * act, axis=-1, keepdims=True)))
             dy = d * (sg * (1.0 + y * (1.0 - sg)))
-            acc_s[pl.ds(base, L), cols] = dy
+            do_s[pl.ds(base, L), cols] = dy
             z = pre[pl.ds(base, L + PAD), cols]
             s = segpad[pl.ds(base, L + PAD), 0:1]
             new = [tap_grads[0] + jnp.sum(dy * z[PAD:], axis=0, keepdims=True)]
@@ -371,7 +782,7 @@
 
         def two(b, _):
             base = pl.multiple_of(b * L, L)
-            dy = acc_s[pl.ds(base, L + PAD), cols]
+            dy = do_s[pl.ds(base, L + PAD), cols]
             s = segpad[pl.ds(base + PAD, L + PAD), 0:1]
             total = dy[:L] * taps_ref[0:1, cols]
             for t in range(1, 4):
@@ -391,279 +802,331 @@
         conv_back(vpad, cv_ref, y_s, dvp_ref, c, slice(512 + j * 128, 512 + j * 128 + 128), None)
 
 
-def mixer_bwd(seg3, gm, qp, kp, vp, gp, ba, cq, ck, cv, rate, bias, gain, q, k, x, u, s, o):
+def mixer_bwd(seg3, ga, wout, low, ffn, resid, qp, kp, vp, gp, ba, cq, ck, cv, rate, bias, gain, q, k, x, u, s, o):
     T = qp.shape[0]
     blocks = T // L
+    own, D = resid.shape
+    n = low.shape[1]
     sd = jax.ShapeDtypeStruct
-    vm = lambda n, w: pltpu.VMEM((n, w), F32)
+    vm = lambda r, w: pltpu.VMEM((r, w), F32)
     return pl.pallas_call(
         functools.partial(bwd_kernel, blocks),
         out_shape=(sd((T, 256), BF16), sd((T, 256), BF16), sd((T, 512), BF16), sd((T, 512), BF16), sd((T, 128), BF16),
-                   sd((8, 1024), F32), sd((8, 128), F32), sd((8, 256), F32)),
-        in_specs=[VM] * 19, out_specs=[VM] * 8,
-        scratch_shapes=[vm(T + PAD, 256), vm(T + PAD, 256), vm(T + PAD, 512), vm(T + 2 * PAD, L),
-                        vm(T, 512), vm(T, 512), vm(T, 256), vm(T, 512), vm(T, 512), vm(T, 512), vm(T, 256), vm(T, 256), vm(8, 128), vm(T + PAD, 512)],
-        compiler_params=pltpu.CompilerParams(vmem_limit_bytes=56 * 2 ** 20),
+                   sd((8, 1024), F32), sd((8, 128), F32), sd((8, 256), F32), sd((own, D), F32), sd((n, 128), F32)),
+        in_specs=[VM] * 23, out_specs=[VM] * 10,
+        scratch_shapes=[vm(T + PAD, 256), vm(T + PAD, 256), vm(T + PAD, 512), vm(T + 2 * PAD, L), vm(T, 512),
+                        vm(T + PAD, 512), vm(T, 512), vm(T, 256), vm(T, 512), vm(T, 256), vm(T, 256), pltpu.VMEM((n, T), BF16)]
+        + scatter_scratch(own) + dp_scratch(n),
+        compiler_params=params(4, 60),
         name="mixer_backward",
-    )(seg3, gm, qp, kp, vp, gp, ba, cq, ck, cv, rate, bias, gain, q, k, x, u, s, o)
-
-
-MESH = pl.DeviceIdType.MESH
-N_TENSOR = 8
-
-
-def tensor_peers():
-    d, t = lax.axis_index("dp"), lax.axis_index("tensor")
-    return d, t, [lax.rem(t + j, N_TENSOR) for j in range(1, N_TENSOR)]
-
-
-def greet(d, peers):
-    barrier = pltpu.get_barrier_semaphore()
-    for p in peers:
-        pl.semaphore_signal(barrier, inc=1, device_id=(d, p), device_id_type=MESH)
-    pl.semaphore_wait(barrier, len(peers))
-
-
-def scatter_copies(d, peers, send, recv, ssem, rsem, own):
-    return [
-        pltpu.make_async_remote_copy(
-            src_ref=send.at[pl.ds(pl.multiple_of(p * own, own), own)], dst_ref=recv.at[j],
-            send_sem=ssem.at[j], recv_sem=rsem.at[j], device_id=(d, p), device_id_type=MESH)
-        for j, p in enumerate(peers)]
-
-
-def gather_copies(d, peers, shard, recv, ssem, rsem):
-    return [
-        pltpu.make_async_remote_copy(
-            src_ref=shard, dst_ref=recv.at[j],
-            send_sem=ssem.at[j], recv_sem=rsem.at[j], device_id=(d, p), device_id_type=MESH)
-        for j, p in enumerate(peers)]
-
-
-def summed(send, recv, t, own, r0, n):
-    total = send[pl.ds(pl.multiple_of(t * own + r0, 8), n), :]
-    for j in range(N_TENSOR - 1):
-        total = total + recv[j, pl.ds(r0, n), :]
-    return total
-
-
-def gathered_out(t, shard, recv, out_ref, copies, own):
-    out_ref[pl.ds(pl.multiple_of(t * own, own), own), :] = shard[...].astype(out_ref.dtype)
-    for j in range(N_TENSOR - 1):
-        copies[j].wait_recv()
-        source = lax.rem(t + N_TENSOR - 1 - j, N_TENSOR)
-        out_ref[pl.ds(pl.multiple_of(source * own, own), own), :] = recv[j].astype(out_ref.dtype)
-
-
-def attn_kernel(low_ref, w_ref, x_ref, gain_ref, hid_ref, resid_ref,
-                send, recv, shard, grecv, xown, csem, s1, r1, s2, r2):
-    d, t, peers = tensor_peers()
+    )(seg3, ga, wout, low, ffn, resid, qp, kp, vp, gp, ba, cq, ck, cv, rate, bias, gain, q, k, x, u, s, o)
+
+
+def attn_kernel(low_ref, w_ref, x_ref, gain_ref, hid_ref, resid_ref, part, whole, xown, csem, *rest):
+    scr, gsem = rest[:7], rest[7:]
+    ring = Ring()
     own = resid_ref.shape[0]
-    mine = pltpu.make_async_copy(x_ref.at[pl.ds(pl.multiple_of(t * own, own), own)], xown, csem)
-    mine.start()
-
-    def partial(n, _):
-        cols = pl.ds(pl.multiple_of(n * 256, 256), 256)
-        send[:, cols] = mm1(low_ref[...], w_ref[:, cols], NN)
+    mine = ring.rows(0, False, own)
+    fetch = pltpu.make_async_copy(x_ref.at[mine], xown, csem)
+    fetch.start()
+
+    greet([ring.right, ring.left, ring.flip])
+    sc = Scatter(ring, part, scr, own)
+    for k in sc.ORDER:
+        quarter = ring.quarter(k, own)
+
+        def partial(n, _):
+            cols = pl.ds(pl.multiple_of(n * 512, 512), 512)
+            part[quarter, cols] = mm1(low_ref[quarter, :], w_ref[:, cols], NN)
+            return 0
+
+        lax.fori_loop(0, part.shape[1] // 512, partial, 0)
+        sc.start(k)
+    fetch.wait()
+    run(sc.middle())
+    sc.finish()
+
+    def finish(i, _):
+        r = pl.multiple_of(i * 16, 16)
+        resid = xown[pl.ds(r, 16), :].astype(F32) + sc.value(r)
+        resid_ref[pl.ds(r, 16), :] = resid
+        n = resid * lax.rsqrt(jnp.mean(resid * resid, axis=-1, keepdims=True) + 1e-05)
+        whole[pl.ds(pl.multiple_of(mine.start + r, 16), 16), :] = (n * gain_ref[0:1, :]).astype(BF16).astype(F32)
         return 0
 
-    lax.fori_loop(0, send.shape[1] // 256, partial, 0)
-    greet(d, peers)
-    copies = scatter_copies(d, peers, send, recv, s1, r1, own)
-    for c in copies:
-        c.start()
-    mine.wait()
-    for c in copies:
-        c.wait_recv()
-
-    def finish(i, _):
-        r0 = pl.multiple_of(i * 16, 16)
-        resid = xown[pl.ds(r0, 16), :].astype(F32) + summed(send, recv, t, own, r0, 16)
-        resid_ref[pl.ds(r0, 16), :] = resid
-        n = resid * lax.rsqrt(jnp.mean(resid * resid, axis=-1, keepdims=True) + 1e-05)
-        shard[pl.ds(r0, 16), :] = (n * gain_ref[0:1, :]).astype(BF16).astype(F32)
+    lax.fori_loop(0, own // 16, finish, 0)
+    ga = Gather(ring, whole, gsem, own)
+    ga.start()
+    run(ga.middle())
+    ga.finish()
+
+    def cast(i, _):
+        r = pl.ds(pl.multiple_of(i * 32, 32), 32)
+        hid_ref[r, :] = whole[r, :].astype(BF16)
         return 0
 
-    lax.fori_loop(0, own // 16, finish, 0)
-    back = gather_copies(d, peers, shard, grecv, s2, r2)
-    for c in back:
-        c.start()
-    gathered_out(t, shard, grecv, hid_ref, back, own)
-    for c in copies + back:
-        c.wait_send()
-
-
-def dma_sems(*counts):
-    return [pltpu.SemaphoreType.DMA((n,)) for n in counts]
-
-
-ANY = pl.BlockSpec(memory_space=pl.ANY)
+    lax.fori_loop(0, whole.shape[0] // 32, cast, 0)
+    sc.s.drain()
+    ga.s.drain()
 
 
 def attn_exchange(low, w_out, inputs, gain):
     T, D = inputs.shape
-    own = T // N_TENSOR
+    own = T // NT_
     sd = jax.ShapeDtypeStruct
     return pl.pallas_call(
         attn_kernel,
         out_shape=(sd((T, D), BF16), sd((own, D), F32)),
         in_specs=[VM, VM, ANY, VM], out_specs=[VM, VM],
-        scratch_shapes=[pltpu.VMEM((T, D), F32), pltpu.VMEM((7, own, D), F32), pltpu.VMEM((own, D), F32),
-                        pltpu.VMEM((7, own, D), F32), pltpu.VMEM((own, D), BF16), pltpu.SemaphoreType.DMA(())] + dma_sems(7, 7, 7, 7),
-        compiler_params=pltpu.CompilerParams(collective_id=1, has_side_effects=True, vmem_limit_bytes=56 * 2 ** 20),
+        scratch_shapes=[pltpu.VMEM((T, D), F32), pltpu.VMEM((T, D), F32), pltpu.VMEM((own, D), BF16),
+                        pltpu.SemaphoreType.DMA(())] + scatter_scratch(own) + gather_sems(),
+        compiler_params=params(1, 56),
         name="attn_exchange",
     )(low, w_out, inputs, gain)
 
 
-def mid_kernel(gg_ref, gu_ref, wg_ref, wu_ref, ffn_ref, resid_in, og_ref, gain_ref,
-               ga_ref, gres_ref, dgain_ref, out_ref,
-               send, recv, shard, grecv, ogown, oshard, orecv, csem, s1, r1, s2, r2, s3, r3, s4, r4):
-    d, t, peers = tensor_peers()
+def mid_kernel(wg_ref, wu_ref, wd_any, hid_ref, og_any, resid_any, gain_ref,
+               ga_ref, inner_ref, ffn_any, gres_ref, dgain_ref, grads_ref,
+               part, whole, left, gg_ref, gu_ref, wd_ref, og_ref, resid_in, csem, *rest):
+    scr, gsem, dscr = rest[:7], rest[7:9], rest[9:]
+    fetches = [pltpu.make_async_copy(src, dst, csem.at[i]) for i, (src, dst) in enumerate(
+        ((wd_any, wd_ref), (og_any, og_ref), (resid_any, resid_in)))]
+    for f in fetches:
+        f.start()
+    ring = Ring()
     own = gres_ref.shape[0]
-    rows_t = pl.ds(pl.multiple_of(t * own, own), own)
-    mine = pltpu.make_async_copy(og_ref.at[rows_t], ogown, csem.at[0])
-    mine.start()
-    ffn_own = pltpu.make_async_copy(ffn_ref.at[rows_t], oshard, csem.at[1])
-    ffn_own.start()
-
-    def partial(n, _):
-        cols = pl.ds(pl.multiple_of(n * 256, 256), 256)
-        send[:, cols] = mm1(gg_ref[...], wg_ref[cols, :], NT) + mm1(gu_ref[...], wu_ref[cols, :], NT)
-        return 0
-
-    lax.fori_loop(0, send.shape[1] // 256, partial, 0)
-    greet(d, peers)
-    copies = scatter_copies(d, peers, send, recv, s1, r1, own)
-    copies2 = scatter_copies(d, peers, ffn_ref, orecv, s3, r3, own)
-    for c in copies:
-        c.start()
-    for c in copies2:
-        c.start()
-    mine.wait()
-    for c in copies:
-        c.wait_recv()
+    n = gg_ref.shape[1]
+    mine = ring.rows(0, False, own)
+
+    def compute(a, b, put):
+        hid = jnp.concatenate([hid_ref[:, a], hid_ref[:, b]], axis=1)
+        put(slice(0, n), mm1(left[0:n, :], hid, NN))
+        put(slice(n, 2 * n), mm1(left[n:2 * n, :], hid, NN))
+
+    dp = DpScatter(ring, dscr, compute)
+    greet([ring.right, ring.left, ring.flip] + dp.devices())
+    sc = Scatter(ring, part, scr, own)
+    for k in sc.ORDER:
+        quarter = ring.quarter(k, own)
+        hid = hid_ref[quarter, :]
+        gate = mm1(hid, wg_ref[...], NT)
+        up = mm1(hid, wu_ref[...], NT)
+        sig = sigmoid(gate)
+        act = gate * sig
+        inner_ref[quarter, :] = (act * up).astype(BF16)
+        if k == 2:
+            fetches[0].wait()
+            fetches[1].wait()
+        back = mm1(og_ref[quarter, :], wd_ref[...], NT)
+        gg_ref[quarter, :] = (back * up * sig * (1.0 + gate * (1.0 - sig))).astype(BF16)
+        gu_ref[quarter, :] = (back * act).astype(BF16)
+
+        def partial(i, _):
+            cols = pl.ds(pl.multiple_of(i * 512, 512), 512)
+            part[quarter, cols] = mm1(gg_ref[quarter, :], wg_ref[:, cols], NN) + mm1(gu_ref[quarter, :], wu_ref[:, cols], NN)
+            return 0
+
+        lax.fori_loop(0, part.shape[1] // 512, partial, 0)
+        sc.start(k)
+    left[0:n, :] = gg_ref[...].T
+    left[n:2 * n, :] = gu_ref[...].T
+    together(sc, dp)
+    fetches[2].wait()
+    sc.finish()
     dgain_ref[...] = jnp.zeros_like(dgain_ref)
 
     def finish(i, _):
-        r0 = pl.multiple_of(i * 16, 16)
-        resid = resid_in[pl.ds(r0, 16), :]
-        back = summed(send, recv, t, own, r0, 16)
+        r = pl.multiple_of(i * 16, 16)
+        resid = resid_in[pl.ds(r, 16), :]
+        back = sc.value(r)
         scale = lax.rsqrt(jnp.mean(resid * resid, axis=-1, keepdims=True) + 1e-05)
-        n = resid * scale
-        bn = back * n
+        nn = resid * scale
+        bn = back * nn
         dgain_ref[...] = dgain_ref[...] + bn[0:8] + bn[8:16]
         b = back * gain_ref[0:1, :]
-        g = ogown[pl.ds(r0, 16), :].astype(F32) + scale * (b - n * jnp.mean(b * n, axis=-1, keepdims=True))
-        gres_ref[pl.ds(r0, 16), :] = g
-        shard[pl.ds(r0, 16), :] = g.astype(BF16).astype(F32)
+        g = og_ref[pl.ds(pl.multiple_of(mine.start + r, 16), 16), :].astype(F32) + scale * (b - nn * jnp.mean(b * nn, axis=-1, keepdims=True))
+        gres_ref[pl.ds(r, 16), :] = g
+        whole[pl.ds(pl.multiple_of(mine.start + r, 16), 16), :] = g.astype(BF16).astype(F32)
         return 0
 
     lax.fori_loop(0, own // 16, finish, 0)
-    back = gather_copies(d, peers, shard, grecv, s2, r2)
-    for c in back:
-        c.start()
-    for c in copies2:
-        c.wait_recv()
-    ffn_own.wait()
-
-    def finish2(i, _):
-        r0 = pl.multiple_of(i * 16, 16)
-        total = oshard[pl.ds(r0, 16), :]
-        for j in range(N_TENSOR - 1):
-            total = total + orecv[j, pl.ds(r0, 16), :]
-        oshard[pl.ds(r0, 16), :] = (resid_in[pl.ds(r0, 16), :] + total).astype(BF16).astype(F32)
+    ga = Gather(ring, whole, gsem, own)
+    ga.start()
+    sc.s.drain()
+    steps = ga.middle()
+    run(steps, 1)
+    dp.second()
+    run(steps, 1)
+
+    def down(i, _):
+        cols = pl.ds(pl.multiple_of(i * 256, 256), 256)
+        part[:, cols] = mm1(inner_ref[...], wd_ref[:, cols], NN)
         return 0
 
-    lax.fori_loop(0, own // 16, finish2, 0)
-    back2 = [
-        pltpu.make_async_remote_copy(
-            src_ref=oshard, dst_ref=out_ref.at[rows_t],
-            send_sem=s4.at[j], recv_sem=r4.at[j], device_id=(d, p), device_id_type=MESH)
-        for j, p in enumerate(peers)]
-    for c in back2:
-        c.start()
-    own_out = pltpu.make_async_copy(oshard, out_ref.at[rows_t], csem.at[2])
-    own_out.start()
-    gathered_out(t, shard, grecv, ga_ref, back, own)
-    for c in back2:
-        c.wait_recv()
-    own_out.wait()
-    for c in copies + back + copies2 + back2:
-        c.wait_send()
-
-
-def mid_exchange(gg, gu, wg, wu, ffn, resid, og, gain):
+    lax.fori_loop(0, part.shape[1] // 256, down, 0)
+    leave = pltpu.make_async_copy(part, ffn_any, csem.at[3])
+    leave.start()
+    run(steps)
+    dp.third()
+    ga.finish()
+
+    def cast(i, _):
+        r = pl.ds(pl.multiple_of(i * 32, 32), 32)
+        ga_ref[r, :] = whole[r, :].astype(BF16)
+        return 0
+
+    lax.fori_loop(0, whole.shape[0] // 32, cast, 0)
+    dp.finish(grads_ref)
+    leave.wait()
+    ga.s.drain()
+
+
+def mid_exchange(wg, wu, wd, hid, og, resid, gain):
     T, D = og.shape
-    own = T // N_TENSOR
+    own = T // NT_
+    m = wg.shape[0]
     sd = jax.ShapeDtypeStruct
     return pl.pallas_call(
         mid_kernel,
-        out_shape=(sd((T, D), BF16), sd((own, D), F32), sd((8, D), F32), sd((T, D), F32)),
-        in_specs=[VM, VM, VM, VM, ANY, VM, ANY, VM], out_specs=[VM, VM, VM, ANY],
-        scratch_shapes=[pltpu.VMEM((T, D), F32), pltpu.VMEM((7, own, D), F32), pltpu.VMEM((own, D), F32),
-                        pltpu.VMEM((7, own, D), F32), pltpu.VMEM((own, D), BF16), pltpu.VMEM((own, D), F32), pltpu.VMEM((7, own, D), F32),
-                        pltpu.SemaphoreType.DMA((3,))] + dma_sems(7, 7, 7, 7, 7, 7, 7, 7),
-        compiler_params=pltpu.CompilerParams(collective_id=2, has_side_effects=True, vmem_limit_bytes=58 * 2 ** 20),
+        out_shape=(sd((T, D), BF16), sd((T, m), BF16), sd((T, D), F32), sd((own, D), F32), sd((8, D), F32), sd((2 * m, 128), F32)),
+        in_specs=[VM, VM, ANY, VM, ANY, ANY, VM], out_specs=[VM, VM, ANY, VM, VM, VM],
+        scratch_shapes=[pltpu.VMEM((T, D), F32), pltpu.VMEM((T, D), F32), pltpu.VMEM((2 * m, T), BF16),
+                        pltpu.VMEM((T, m), BF16), pltpu.VMEM((T, m), BF16), pltpu.VMEM((m, D), BF16), pltpu.VMEM((T, D), BF16),
+                        pltpu.VMEM((own, D), F32), pltpu.SemaphoreType.DMA((4,))]
+        + scatter_scratch(own) + gather_sems() + dp_scratch(2 * m, 4),
+        compiler_params=params(2, 62),
         name="mid_exchange",
-    )(gg, gu, wg, wu, ffn, resid, og, gain)
-
-
-def in_kernel(part_ref, gres_ref, x_ref, gain_ref, ig_ref, dgain_ref,
-              recv, shard, grecv, xown, pown, csem, s1, r1, s2, r2):
-    d, t, peers = tensor_peers()
+    )(wg, wu, wd, hid, og, resid, gain)
+
+
+SMALL = 40
+TAPS = 40
+
+
+def in_kernel(gq, gk, gv, gt, gba, inner_ref, wq, wk, wv, wt, wba, hid_ref, og_ref, gres_ref, x_ref, gain_ref, gains_ref, taps_ref, oshard_ref,
+              whole, out_whole, grads_ref, gains_out, taps_out,
+              part, shard, left, xown, g_own, g_recv, s_own, s_recv, csem, ssem, srsem, *rest):
+    scr, gsem, osem, dscr = rest[:7], rest[7:9], rest[9:11], rest[11:]
+    ring = Ring()
     own = gres_ref.shape[0]
-    rows_t = pl.ds(pl.multiple_of(t * own, own), own)
-    mine = pltpu.make_async_copy(x_ref.at[rows_t], xown, csem.at[0])
-    mine.start()
-    mine2 = pltpu.make_async_copy(part_ref.at[rows_t], pown, csem.at[1])
-    mine2.start()
-    greet(d, peers)
-    copies = scatter_copies(d, peers, part_ref, recv, s1, r1, own)
-    for c in copies:
-        c.start()
-    mine.wait()
-    mine2.wait()
-    for c in copies:
-        c.wait_recv()
-    dgain_ref[...] = jnp.zeros_like(dgain_ref)
-
-    def finish(i, _):
-        r0 = pl.multiple_of(i * 16, 16)
-        x = xown[pl.ds(r0, 16), :].astype(F32)
-        back = pown[pl.ds(r0, 16), :]
-        for j in range(N_TENSOR - 1):
-            back = back + recv[j, pl.ds(r0, 16), :]
+    mine = ring.rows(0, False, own)
+    fetch = pltpu.make_async_copy(x_ref.at[mine], xown, csem.at[0])
+    fetch.start()
+    place_out = pltpu.make_async_copy(oshard_ref, out_whole.at[mine], csem.at[1])
+    place_out.start()
+    t_peers = [(ring.d, lax.rem(ring.t + j, NT_)) for j in range(1, NT_)]
+    d_peers = [(lax.rem(ring.d + j, 16), ring.t) for j in range(1, 16)]
+    greet(t_peers + d_peers)
+    place_out.wait()
+    go = Gather(ring, out_whole, osem, own)
+    go.start()
+
+    sc = Scatter(ring, part, scr, own)
+    for k in sc.ORDER:
+        quarter = ring.quarter(k, own)
+
+        def partial(i, _):
+            rows_w = pl.ds(pl.multiple_of(i * 512, 512), 512)
+            total = mm1(gq[quarter, :], wq[rows_w, :], NT) + mm1(gk[quarter, :], wk[rows_w, :], NT)
+            total = total + mm1(gv[quarter, :], wv[rows_w, :], NT) + mm1(gt[quarter, :], wt[rows_w, :], NT)
+            part[quarter, rows_w] = total + mm1(gba[quarter, :], wba[rows_w, :], NT)
+            return 0
+
+        lax.fori_loop(0, part.shape[1] // 512, partial, 0)
+        sc.start(k)
+
+    def compute(a, b, put):
+        hid = jnp.concatenate([hid_ref[:, a], hid_ref[:, b]], axis=1)
+        put(slice(0, 768), mm1(left[0:768, :], hid, NN))
+        put(slice(768, 1552), mm1(left[768:1552, :], hid, NN))
+        put(slice(1552, 2256), mm1(left[1552:, :], jnp.concatenate([og_ref[:, a], og_ref[:, b]], axis=1), NN))
+
+    dp = DpScatter(ring, dscr, compute)
+    left[0:256, :] = gq[...].T
+    left[256:512, :] = gk[...].T
+    left[512:1024, :] = gv[...].T
+    left[1024:1536, :] = gt[...].T
+    left[1536:1552, :] = gba[...].T[0:16]
+    left[1552:, :] = inner_ref[...].T
+    outs = go.middle()
+    run(outs, 1)
+    together(sc, dp)
+    run(outs, 2)
+    fetch.wait()
+    sc.finish()
+    g_own[...] = gains_ref[...]
+
+    def finish(i, total):
+        r = pl.multiple_of(i * 16, 16)
+        x = xown[pl.ds(r, 16), :].astype(F32)
+        back = sc.value(r)
         scale = lax.rsqrt(jnp.mean(x * x, axis=-1, keepdims=True) + 1e-05)
-        n = x * scale
-        bn = back * n
-        dgain_ref[...] = dgain_ref[...] + bn[0:8] + bn[8:16]
+        nn = x * scale
+        total = total + jnp.sum(back * nn, axis=0, keepdims=True)
         b = back * gain_ref[0:1, :]
-        g = gres_ref[pl.ds(r0, 16), :] + scale * (b - n * jnp.mean(b * n, axis=-1, keepdims=True))
-        shard[pl.ds(r0, 16), :] = g.astype(BF16).astype(F32)
-        return 0
-
-    lax.fori_loop(0, own // 16, finish, 0)
-    back = gather_copies(d, peers, shard, grecv, s2, r2)
-    for c in back:
-        c.start()
-    gathered_out(t, shard, grecv, ig_ref, back, own)
-    for c in copies + back:
-        c.wait_send()
-
-
-def in_exchange(part, gres, inputs, gain):
+        g = gres_ref[pl.ds(r, 16), :] + scale * (b - nn * jnp.mean(b * nn, axis=-1, keepdims=True))
+        shard[pl.ds(r, 16), :] = g.astype(BF16).astype(F32)
+        return total
+
+    total = lax.fori_loop(0, own // 16, finish, jnp.zeros((1, x_ref.shape[1]), F32))
+    for j in range(16):
+        g_own[j:j + 1, :] = total[:, j * 128:(j + 1) * 128]
+    place = pltpu.make_async_copy(shard, whole.at[mine], csem.at[2])
+    place.start()
+    place.wait()
+    small = Sends(ssem, srsem)
+    for j, dev in enumerate(t_peers):
+        small.go(j, g_own, g_recv.at[j], dev)
+    ga = Gather(ring, whole, gsem, own)
+    ga.start()
+    run(outs)
+    dp.second()
+    steps = ga.middle()
+    run(steps, 1)
+    for j, dev in enumerate(t_peers):
+        small.got(j, g_recv.at[j], dev)
+    gains = g_own[...]
+    for j in range(NT_ - 1):
+        gains = gains + g_recv[j]
+    s_own[0:SMALL, :] = gains
+    s_own[SMALL:, :] = taps_ref[...]
+    for j, dev in enumerate(d_peers):
+        small.go(7 + j, s_own, s_recv.at[j], dev)
+    run(steps)
+    dp.third()
+    for j, dev in enumerate(d_peers):
+        small.got(7 + j, s_recv.at[j], dev)
+    both = s_own[...]
+    for j in range(15):
+        both = both + s_recv[j]
+    gains_out[...] = both[:SMALL]
+    taps_out[...] = both[SMALL:]
+    go.finish()
+    ga.finish()
+    dp.finish(grads_ref)
+    small.drain()
+    go.s.drain()
+    sc.s.drain()
+    ga.s.drain()
+
+
+def in_exchange(grads, inner, weights, hid, og, gres, inputs, gain, gains, taps, oshard):
     T, D = inputs.shape
-    own = T // N_TENSOR
+    own = T // NT_
+    n = 1552 + inner.shape[1]
     sd = jax.ShapeDtypeStruct
+    vm = lambda *s: pltpu.VMEM(s, F32)
     return pl.pallas_call(
         in_kernel,
-        out_shape=(sd((T, D), BF16), sd((8, D), F32)),
-        in_specs=[ANY, VM, ANY, VM], out_specs=[VM, VM],
-        scratch_shapes=[pltpu.VMEM((7, own, D), F32), pltpu.VMEM((own, D), F32),
-                        pltpu.VMEM((7, own, D), F32), pltpu.VMEM((own, D), BF16), pltpu.VMEM((own, D), F32), pltpu.SemaphoreType.DMA((2,))] + dma_sems(7, 7, 7, 7),
-        compiler_params=pltpu.CompilerParams(collective_id=3, has_side_effects=True, vmem_limit_bytes=56 * 2 ** 20),
+        out_shape=(sd((T, D), F32), sd((T, D), F32), sd((n, 128), F32), sd((SMALL, 128), F32), sd((TAPS, 128), F32)),
+        in_specs=[VM] * 14 + [ANY] + [VM] * 4, out_specs=[ANY, ANY, VM, VM, VM],
+        scratch_shapes=[vm(T, D), vm(own, D), pltpu.VMEM((n, T), BF16), pltpu.VMEM((own, D), BF16),
+                        vm(SMALL, 128), vm(7, SMALL, 128), vm(SMALL + TAPS, 128), vm(15, SMALL + TAPS, 128),
+                        pltpu.SemaphoreType.DMA((3,)), pltpu.SemaphoreType.DMA((22,)), pltpu.SemaphoreType.DMA((22,))]
+        + scatter_scratch(own) + gather_sems() + gather_sems() + dp_scratch(n, 4),
+        compiler_params=params(3, 60),
         name="in_exchange",
-    )(part, gres, inputs, gain)
+    )(*grads, inner, *weights, hid, og, gres, inputs, gain, gains, taps, oshard)
 
 
 def matmul(left, right):
@@ -692,40 +1155,24 @@
     gain8 = rows8(head_gain)
     low, q, k, x, u, s, o = mixer_fwd(seg3, qp, kp, vp, gp, ba, conv_query, conv_key, conv_value, rate, bias, gain8)
     hidden_mid, resid = attn_exchange(low, w_out, inputs, rows8(ffn_gain))
-    gate_pre = matmul(hidden_mid, w_up_gate)
-    up_pre = matmul(hidden_mid, w_up)
-    sig = jax.nn.sigmoid(gate_pre)
-    act = gate_pre * sig
-    inner = (act * up_pre).astype(BF16)
-    ffn = matmul(inner, w_down)
-    grad_inner = matmul(out_grad, w_down.T)
-    grad_down = matmul(inner.T, out_grad)
-    gg = (grad_inner * up_pre * sig * (1.0 + gate_pre * (1.0 - sig))).astype(BF16)
-    gu = (grad_inner * act).astype(BF16)
-    grad_up_gate = matmul(hidden_mid.T, gg)
-    grad_up = matmul(hidden_mid.T, gu)
-    grad_attn, grad_resid, ffn_gain_part, out32 = mid_exchange(gg, gu, w_up_gate, w_up, ffn, resid, out_grad, rows8(ffn_gain))
+    grad_attn, inner, ffn, grad_resid, ffn_gain_part, grads_mid = mid_exchange(
+        w_up_gate.T, w_up.T, w_down, hidden_mid, out_grad, resid, rows8(ffn_gain))
+    gq, gk, gv, gt, gba, taps, small, hgain, oshard, grads_out = mixer_bwd(
+        seg3, grad_attn, w_out, low, ffn, resid, qp, kp, vp, gp, ba, conv_query, conv_key, conv_value, rate, bias, gain8, q, k, x, u, s, o)
+    gains_in = jnp.concatenate([jnp.zeros((16, 128), F32), jnp.sum(ffn_gain_part, axis=0).reshape(16, 128), hgain[0].reshape(2, 128),
+                                jnp.zeros((SMALL - 34, 128), F32)], axis=0)
+    taps_in = jnp.concatenate([taps[:4].reshape(32, 128), small], axis=0)
+    ig, out32, grads_in, gains, taps_sum = in_exchange(
+        (gq, gk, gv, gt, gba), inner, (w_query, w_key, w_value, w_gate, w_ba), hidden_in, out_grad, grad_resid, inputs,
+        rows8(attn_gain), gains_in, taps_in, oshard)
+    input_grad = ig.astype(BF16)
     outputs = out32.astype(BF16)
-    grad_out = matmul(low.T, grad_attn)
-    grad_mixed = matmul(grad_attn, w_out.T)
-    gq, gk, gv, gt, gba, taps, small, hgain = mixer_bwd(
-        seg3, grad_mixed, qp, kp, vp, gp, ba, conv_query, conv_key, conv_value, rate, bias, gain8, q, k, x, u, s, o)
-    grad_query = matmul(hidden_in.T, gq)
-    grad_key = matmul(hidden_in.T, gk)
-    grad_value = matmul(hidden_in.T, gv)
-    grad_gate = matmul(hidden_in.T, gt)
-    grad_ba = matmul(hidden_in.T, gba)
-    part = matmul(gq, w_query.T) + matmul(gk, w_key.T) + matmul(gv, w_value.T) + matmul(gt, w_gate.T) + matmul(gba, w_ba.T)
-    input_grad, attn_gain_part = in_exchange(part, grad_resid, inputs, rows8(attn_gain))
-    both = lax.psum((jnp.sum(attn_gain_part, axis=0), jnp.sum(ffn_gain_part, axis=0), hgain[0]), ("dp", "tensor"))
-    sums = lax.psum((taps[:4], small[:2, 2:4]), "dp")
-
-    def scatter(g, dim=0):
-        return lax.psum_scatter(g, "dp", scatter_dimension=dim, tiled=True)
-
-    return (outputs, input_grad, both[0], scatter(grad_query), scatter(grad_key), scatter(grad_value), scatter(grad_gate),
-            scatter(grad_ba[:, 0:2]), scatter(grad_ba[:, 2:4]), sums[0][:, 0:256], sums[0][:, 256:512], sums[0][:, 512:1024],
-            sums[1][1], sums[1][0], both[2], scatter(grad_out, 1), both[1], scatter(grad_up_gate), scatter(grad_up), scatter(grad_down, 1))
+    n = w_up.shape[1]
+    ct = taps_sum[:32].reshape(4, 1024)
+    return (outputs, input_grad, gains[:16].reshape(D), grads_in[0:256].T, grads_in[256:512].T, grads_in[512:1024].T, grads_in[1024:1536].T,
+            grads_in[1536:1538].T, grads_in[1538:1540].T, ct[:, 0:256], ct[:, 256:512], ct[:, 512:],
+            taps_sum[33, 2:4], taps_sum[32, 2:4], gains[32:34].reshape(256), grads_out, gains[16:32].reshape(D),
+            grads_mid[0:n].T, grads_mid[n:2 * n].T, grads_in[1552:])
 
 
 def solution(mesh):

time: 1290 us -> 533 us (0.41)
  waiting for transfers between devices: 288 us -> 0 us
  Pallas kernels: 693 us -> 475 us
  blocking collectives: 128 us -> 0 us
  matrix products: 104 us -> 13.7 us
  local copies, waits for them, and re-layouts: 34.5 us -> 15.5 us
  between operations: 15 us -> 1.31 us
    reduce_scatter x8 -> x0, waiting for transfers between devices: 288 us -> none  [scatter(): return lax.psum_scatter(g, 'dp', scatter_dimension=dim, tiled=True)]
    pallas_call x2, Pallas kernels: 463 us -> 273 us  [the longest x1 163 us: in_exchange(): pl.pallas_call(in_kernel, out_shape=(sd((T, D), F32), sd((T, D), F32), sd...]
    psum x2 -> x0, blocking collectives: 128 us -> none  [the longest x1 72 us: per_device(): lax.psum((jnp.sum(attn_gain_part, axis=0), jnp.sum(ffn_gain_part, axis=0)...]
    dot_general x24 -> x5, matrix products: 104 us -> 13.7 us  [matmul(): return jnp.dot(left, right, preferred_element_type=F32)]
    pallas_call x1, Pallas kernels: 153 us -> 97.6 us  [attn_exchange(): pl.pallas_call(attn_kernel, out_shape=(sd((T, D), BF16), sd((own, D), F32...]
    pallas_call x1, Pallas kernels: 49.9 us -> 79 us  [mixer_bwd(): pl.pallas_call(functools.partial(bwd_kernel, blocks), out_shape=(sd((T, 2...]
    unnamed x85 -> x49, local copies, waits for them, and re-layouts: 27.2 us -> 4.6 us
  transfers between devices with their start and end apart: 10 -> 0, of which waited for: 5 -> 0; matrix products, arithmetic and copies ran while one was open for 6% -> 0% of each run, Pallas kernels for 14% -> 0%
where the time goes in v3:
time: 533 us; the launch traced here: 524 us
  Pallas kernels  475 us (89%)
  other arithmetic  18.5 us (3%)
  local copies, waits for them, and re-layouts  15.5 us (3%)
  matrix products  13.7 us (3%)
    pallas_call x1, Pallas kernels, in_exchange(): pl.pallas_call(in_kernel, out_shape=(sd((T, D), F32), sd((T, D), F32), sd...  163 us
    pallas_call x1, Pallas kernels, mid_exchange(): pl.pallas_call(mid_kernel, out_shape=(sd((T, D), BF16), sd((T, m), BF16),...  110 us
    pallas_call x1, Pallas kernels, attn_exchange(): pl.pallas_call(attn_kernel, out_shape=(sd((T, D), BF16), sd((own, D), F32...  97.6 us
    pallas_call x1, Pallas kernels, mixer_bwd(): pl.pallas_call(functools.partial(bwd_kernel, blocks), out_shape=(sd((T, 2...  79 us
    pallas_call x1, Pallas kernels, mixer_fwd(): pl.pallas_call(functools.partial(fwd_kernel, blocks, group), out_shape=(s...  25.5 us
    dot_general x5, matrix products, matmul(): return jnp.dot(left, right, preferred_element_type=F32)  13.7 us

profile of v3, /device:TPU:24, one launch (start us, length us, event | category | flops | bytes accessed | tf_op | source)
XLA Modules:
  0.0 524.2 jit_solution(7288945176714870884)
XLA Ops:
  0.7 0.8 convert_bitcast_fusion
  1.6 0.1 copy.54
  1.7 0.5 slice.120
  2.2 0.7 maximum_bitcast_fusion
  3.0 0.1 pad.17.clone
  3.1 0.7 maximum_maximum_fusion.1.seg_ref
  3.8 2.6 fusion
  6.4 2.4 fusion.2.hid_ref
  8.8 0.3 copy.55
  9.2 0.3 copy.56
  9.5 0.1 pad.14.clone
  9.6 0.3 maximum_maximum_fusion.wba
  9.9 4.0 fusion.8.ba_ref
  13.9 2.9 fusion.6.vp_ref
  16.8 3.0 fusion.7.gp_ref
  19.9 1.9 fusion.4.qp_ref
  21.8 1.9 fusion.5.kp_ref
  23.7 1.1 compare_reduce_fusion
  24.7 0.7 broadcast_select_fusion
  25.5 0.6 scatter.15.rate_ref
  26.1 0.6 scatter.17.bias_ref
  26.7 0.6 broadcast_in_dim.22.gain_ref
  27.3 25.5 %mixer_forward.1 = (bf16[768,512]{1,0:T(8,128)(2,1)}, f32[768,256]{1,0:T(8,128)}, f32[768,256]{1,0:T(8,128)}, f32[768,256]{1,0:T(8,128)}, f32[768,512]{1,0:T(8,1...) custom-call(f32[6,8,128]{2,1,0:T(8,128)} %maximum_maximum_fusion.1.seg_ref, f32[768,256]{1,0:T(8,128)} %fusion.4.qp_ref, ...), custom_call_target="tpu_custom_call" | custom-call | tf_op jit(solution)/shard_map/mixer_forward/pallas_call | solution.py:203
  52.8 0.6 broadcast_in_dim.23.gain_ref
  53.5 97.6 %attn_exchange.1 = (bf16[768,2048]{1,0:T(8,128)(2,1)}, f32[96,2048]{1,0:T(8,128)}) custom-call(bf16[768,512]{1,0:T(8,128)(2,1)} %get-tuple-element.74.low_ref, bf16[512,2048]{1,0:T(8,128)(2,1)} %wout_ref.1, bf16[768,2048]{1,0:T(8,128)(2,1)} %x_ref.3, f32[8,2048]{1,0:T(8,128)} %broadcast_in_dim.23.gain_ref), custom_call_target="tpu_custom_call" | custom-call | tf_op jit(solution)/shard_map/attn_exchange/pallas_call | solution.py:877
  151.1 109.7 %mid_exchange.1 = (bf16[768,2048]{1,0:T(8,128)(2,1)}, bf16[768,704]{1,0:T(8,128)(2,1)}, f32[768,2048]{1,0:T(8,128)}, f32[96,2048]{1,0:T(8,128)}, f32[8,2048]{1,0:T(8,128)}, /*index=5*/f32[1408,128]{1,0:T(8,128)}) custom-call(bf16[704,2048]{1,0:T(8,128)(2,1)} %bitcast.45, bf16[704,2048]{1,0:T(8,128)(2,1)} %bitcast.46, bf16[704,2048]{1,0:T(8,128)(2,1)} %wd_any.1, ...), custom_call_target="tpu_custom_call" | custom-call | tf_op jit(solution)/shard_map/mid_exchange/pallas_call | solution.py:989
  260.7 79.0 %mixer_backward.1 = (bf16[768,256]{1,0:T(8,128)(2,1)}, bf16[768,256]{1,0:T(8,128)(2,1)}, bf16[768,512]{1,0:T(8,128)(2,1)}, bf16[768,512]{1,0:T(8,128)(2,1)}, bf1...) custom-call(f32[6,8,128]{2,1,0:T(8,128)} %maximum_maximum_fusion.1.s, ...), custom_call_target="tpu_custom_call" | custom-call | tf_op jit(solution)/shard_map/mixer_backward/pallas_call | solution.py:812
  339.7 0.8 slice.101
  340.5 1.3 pad_maximum_fusion.taps_ref
  341.8 0.7 slice.100
  342.6 0.7 maximum_maximum_fusion.2.gains_ref
  343.3 0.6 broadcast_in_dim.24.gain_ref
  343.9 163.4 %in_exchange.1 = (f32[768,2048]{1,0:T(8,128)}, f32[768,2048]{1,0:T(8,128)}, f32[2256,128]{1,0:T(8,128)}, f32[40,128]{1,0:T(8,128)}, f32[40,128]{1,0:T(8,128)}) custom-call(bf16[768,256]{1,0:T(8,128)(2,1)} %get-tuple-element.85.gq, bf16[768,256]{1,0:T(8,128)(2,1)} %get-tuple-element.86.gk, bf16[768,512]{1,0:T(8,128)(2,1)} %get-tuple-element.87.gv, ...), custom_call_target="tpu_custom_call" | custom-call | tf_op jit(solution)/shard_map/in_exchange/pallas_call | solution.py:1119
  507.4 5.1 convert_element_type.18
  512.5 2.1 convert_element_type.19
  514.7 0.8 copy.59
  515.5 0.8 copy.60
  516.4 0.8 copy.57
  517.1 0.8 copy.58
  517.9 0.8 slice.119
  518.7 0.6 fusion.3
  519.3 0.6 slice.124
  519.9 0.6 slice_bitcast_fusion.6
  520.5 0.6 slice_bitcast_fusion.9
  521.0 0.6 slice_bitcast_fusion.11
  521.6 0.6 slice_bitcast_fusion.8
  522.2 0.9 slice_bitcast_fusion
  523.1 0.7 copy.62
  (58 shorter events, 0.6 us)
Async XLA Ops:
  0.7 5.7 %copy-start = (bf16[768,2048]{1,0:T(8,128)(2,1)S(1)}, bf16[768,2048]{1,0:T(8,128)(2,1)}, u32[]{:S(2)}) copy-start(bf16[768,2048]{1,0:T(8,128)(2,1)} %x_ref.3) | copy-start | bytes 9437188
  0.7 5.7 %copy-start.12 = (f32[2048]{0:T(1024)S(1)}, f32[2048]{0:T(1024)}, u32[]{:S(2)}) copy-start(f32[2048]{0:T(1024)} %param.27) | copy-start | bytes 24580
  6.4 2.5 copy-start.15
  6.4 2.8 copy-start.16
  9.6 4.3 copy-start.1
  9.6 4.3 copy-start.4
  9.9 6.9 %copy-start.3 = (bf16[2048,128]{1,0:T(8,128)(2,1)}, bf16[2048,128]{1,0:T(8,128)(2,1)S(1)}, u32[]{:S(2)}) copy-start(bf16[2048,128]{1,0:T(8,128)(2,1)S(1)} %maximum_maximum_fusion.wba) | copy-start | bytes 1572868
  13.9 2.9 copy-start.5
  16.8 3.0 copy-start.7
  19.9 1.9 copy-start.8
  21.8 3.0 copy-start.19
  21.8 3.0 copy-start.20
  21.8 5.0 copy-start.18
  23.7 29.2 %copy-start.17 = (f32[2048]{0:T(1024)S(1)}, f32[2048]{0:T(1024)}, u32[]{:S(2)}) copy-start(f32[2048]{0:T(1024)} %param.41) | copy-start | bytes 24580
  260.7 81.8 %copy-start.11 = (f32[8,2048]{1,0:T(8,128)S(1)}, f32[8,2048]{1,0:T(8,128)}, u32[]{:S(2)}) copy-start(f32[8,2048]{1,0:T(8,128)} %get-tuple-element.92) | copy-start | bytes 196612
  507.4 5.1 copy-start.2
  512.5 2.2 copy-start.6
  514.6 4.0 copy-start.14
  514.6 5.3 %copy-start.13 = (f32[40,128]{1,0:T(8,128)S(1)}, f32[40,128]{1,0:T(8,128)}, u32[]{:S(2)}) copy-start(f32[40,128]{1,0:T(8,128)} %get-tuple-element.99) | copy-start | bytes 61444
  514.6 7.6 %copy-start.9 = (f32[1408,128]{1,0:T(8,128)S(1)}, f32[1408,128]{1,0:T(8,128)}, u32[]{:S(2)}) copy-start(f32[1408,128]{1,0:T(8,128)} %get-tuple-element.103) | copy-start | bytes 2162692
  514.6 8.5 %copy-start.10 = (f32[512,128]{1,0:T(8,128)S(1)}, f32[512,128]{1,0:T(8,128)}, u32[]{:S(2)}) copy-start(f32[512,128]{1,0:T(8,128)} %get-tuple-element.215) | copy-start | bytes 786436

commit v4 on v3

--- a/solution.py
+++ b/solution.py
@@ -24,11 +24,17 @@
 
 
 def mm3(a, b, dims=NN):
-    return mm1(a[0], b[0], dims) + (mm1(a[0], b[1], dims) + mm1(a[1], b[0], dims))
+    (ia,), (ib,) = dims[0]
+    if a[0].shape[ia] > 128:
+        return mm1(a[0], b[0], dims) + (mm1(a[0], b[1], dims) + mm1(a[1], b[0], dims))
+    return mm1(jnp.concatenate(a, axis=ia), jnp.concatenate([b[0], b[0]], axis=ib), dims) + mm1(a[0], b[1], dims)
 
 
 def sigmoid(x):
-    return 1.0 / (1.0 + jnp.exp(-x))
+    d = 1.0 + jnp.exp(-jnp.maximum(x, -80.0))
+    r = pl.reciprocal(d, approx=True)
+    r = r * (2.0 - d * r)
+    return r * (2.0 - d * r)
 
 
 def rows(ref, b, n=L, lead=0):
@@ -80,138 +86,6 @@
     return out, strict_keep, (tile, seg_col)
 
 
-def conv_block(b, pre_ref, taps_ref, seg_ref, cols, segpad_ref):
-    base = pl.multiple_of(b * L, L)
-    z = pre_ref[pl.ds(base, L + PAD), cols]
-    s = segpad_ref[pl.ds(base, L + PAD), 0:1]
-    total = z[PAD:] * taps_ref[0:1, cols]
-    for k in range(1, 4):
-        same = (s[PAD - k:PAD - k + L] == s[PAD:]).astype(F32)
-        total = total + z[PAD - k:PAD - k + L] * same * taps_ref[k:k + 1, cols]
-    return total
-
-
-def inverse_many(mats):
-    r = lax.broadcasted_iota(jnp.int32, (L, L), 0)
-    c = lax.broadcasted_iota(jnp.int32, (L, L), 1)
-    eye = (r == c).astype(F32)
-    xs = [eye - jnp.where((r // 2 == c // 2), a, 0.0) for a in mats]
-    s = 2
-    while s < L:
-        pick = (r // (2 * s) == c // (2 * s)) & (r // s != c // s)
-        sx = [split(x) for x in xs]
-        sa = [split(jnp.where(pick, a, 0.0)) for a in mats]
-        t = [mm3(x, a) for x, a in zip(sx, sa)]
-        xs = [x - mm3(split(y), z) for x, y, z in zip(xs, t, sx)]
-        s *= 2
-    return xs
-
-
-def fwd_kernel(blocks, group, seg_ref, qp_ref, kp_ref, vp_ref, gp_ref, ba_ref, cq_ref, ck_ref, cv_ref, rate_ref, bias_ref, gain_ref,
-               low_ref, q_ref, k_ref, x_ref, u_ref, s_ref, o_ref,
-               qpad, kpad, vpad, segpad, w_s, u0_s, kw_s):
-    T = blocks * L
-    rate, bias = rate_ref[0:1, :], bias_ref[0:1, :]
-    for pad, src in ((qpad, qp_ref), (kpad, kp_ref), (vpad, vp_ref)):
-        pad[0:PAD, :] = jnp.zeros((PAD, pad.shape[1]), F32)
-        pad[PAD:PAD + T, :] = src[...]
-    segpad[0:PAD, :] = jnp.full((PAD, L), -1.0, F32)
-    for b in range(blocks):
-        segpad[PAD + b * L:PAD + (b + 1) * L, :] = jnp.broadcast_to(seg_ref[b, 0:1, :], (L, L)).T
-
-    def phase_a(g, _):
-        a_mats, keepers = [], []
-        for i in range(group):
-            b = g * group + i
-            base = pl.multiple_of(b * L, L)
-            per_head, strict_keep, _u = block_decay(b, seg_ref, ba_ref, rate, bias)
-            for h in range(2):
-                decay, carry, beta_row, beta_col, last_decay = per_head[h]
-                kc = slice(h * 128, h * 128 + 128)
-                vc = slice(h * 256, h * 256 + 256)
-                y = conv_block(b, qpad, cq_ref, seg_ref, kc, segpad)
-                q = y * sigmoid(y)
-                q = q * (lax.rsqrt(jnp.sum(q * q, axis=-1, keepdims=True) + 1e-06) * (128 ** -0.5))
-                y = conv_block(b, kpad, ck_ref, seg_ref, kc, segpad)
-                k = y * sigmoid(y)
-                k = k * lax.rsqrt(jnp.sum(k * k, axis=-1, keepdims=True) + 1e-06)
-                q_ref[pl.ds(base, L), kc] = q
-                k_ref[pl.ds(base, L), kc] = k
-                y = conv_block(b, vpad, cv_ref, seg_ref, vc, segpad)
-                v = y * sigmoid(y)
-                ks = split(k)
-                kk = mm3(ks, ks, NT)
-                a_mats.append(jnp.where(strict_keep, decay, 0.0) * kk * beta_row)
-                kw_s[pl.ds(base, L), kc] = k * (last_decay * beta_col)
-                keepers.append((b, base, h, kc, vc, v, k * carry))
-        xs = inverse_many(a_mats)
-        for x, (b, base, h, kc, vc, v, gk) in zip(xs, keepers):
-            x_ref[pl.ds(base, L), kc] = x
-            sx = split(x)
-            u0_s[pl.ds(base, L), vc] = mm3(sx, split(v))
-            w_s[pl.ds(base, L), kc] = mm3(sx, split(gk))
-        return 0
-
-    lax.fori_loop(0, blocks // group, phase_a, 0)
-
-    def phase_b(b, state):
-        base = pl.multiple_of(b * L, L)
-        per_head, strict_keep, _u = block_decay(b, seg_ref, ba_ref, rate, bias)
-        new = []
-        for h in range(2):
-            decay, carry, beta_row, beta_col, last_decay = per_head[h]
-            kc = slice(h * 128, h * 128 + 128)
-            vc = slice(h * 256, h * 256 + 256)
-            s = state[h]
-            s_ref[pl.ds(base, L), vc] = s
-            ss = split(s)
-            u = u0_s[pl.ds(base, L), vc] - mm3(split(w_s[pl.ds(base, L), kc]), ss)
-            u_ref[pl.ds(base, L), vc] = u
-            new.append(carry[L - 1:L, :] * s + mm3(split(kw_s[pl.ds(base, L), kc]), split(u), TN))
-        return tuple(new)
-
-    zero = jnp.zeros((128, 256), F32)
-    lax.fori_loop(0, blocks, phase_b, (zero, zero))
-
-    def phase_c(b, _):
-        base = pl.multiple_of(b * L, L)
-        per_head, strict_keep, _u = block_decay(b, seg_ref, ba_ref, rate, bias)
-        for h in range(2):
-            decay, carry, beta_row, beta_col, last_decay = per_head[h]
-            kc = slice(h * 128, h * 128 + 128)
-            vc = slice(h * 256, h * 256 + 256)
-            q = q_ref[pl.ds(base, L), kc]
-            qk = mm3(split(q), split(k_ref[pl.ds(base, L), kc]), NT)
-            p = decay * qk * beta_row
-            o = mm3(split(q * carry), split(s_ref[pl.ds(base, L), vc])) + mm3(split(p), split(u_ref[pl.ds(base, L), vc]))
-            o_ref[pl.ds(base, L), vc] = o
-            gp = gp_ref[pl.ds(base, L), vc]
-            n = o * lax.rsqrt(jnp.mean(o * o, axis=-1, keepdims=True) + 1e-05)
-            low_ref[pl.ds(base, L), vc] = (n * gain_ref[0:1, :] * (gp * sigmoid(gp))).astype(BF16)
-        return 0
-
-    lax.fori_loop(0, blocks, phase_c, 0)
-
-
-VM = pl.BlockSpec(memory_space=pltpu.VMEM)
-
-
-def mixer_fwd(seg3, qp, kp, vp, gp, ba, cq, ck, cv, rate, bias, gain, group=2):
-    T = qp.shape[0]
-    blocks = T // L
-    sd = jax.ShapeDtypeStruct
-    return pl.pallas_call(
-        functools.partial(fwd_kernel, blocks, group),
-        out_shape=(sd((T, 512), BF16), sd((T, 256), F32), sd((T, 256), F32), sd((T, 256), F32), sd((T, 512), F32),
-                   sd((T, 512), F32), sd((T, 512), F32)),
-        in_specs=[VM] * 12, out_specs=[VM] * 7,
-        scratch_shapes=[pltpu.VMEM((T + PAD, 256), F32), pltpu.VMEM((T + PAD, 256), F32), pltpu.VMEM((T + PAD, 512), F32),
-                        pltpu.VMEM((T + PAD, L), F32), pltpu.VMEM((T, 256), F32), pltpu.VMEM((T, 512), F32), pltpu.VMEM((T, 256), F32)],
-        compiler_params=pltpu.CompilerParams(vmem_limit_bytes=56 * 2 ** 20),
-        name="mixer_forward",
-    )(seg3, qp, kp, vp, gp, ba, cq, ck, cv, rate, bias, gain)
-
-
 MESH = pl.DeviceIdType.MESH
 NT_ = 8
 ZH, YH = 512, 512
@@ -277,7 +151,7 @@
 
 ZA, ZB, ZZ = pl.ds(0, ZH), pl.ds(ZH, ZH), pl.ds(0, 2 * ZH)
 YA, YB, YY = pl.ds(2 * ZH, YH), pl.ds(2 * ZH + YH, YH), pl.ds(2 * ZH, 2 * YH)
-GZH, GYH = 640, 384
+GZH, GYH = 768, 256
 GZA, GZB, GZZ = pl.ds(0, GZH), pl.ds(GZH, GZH), pl.ds(0, 2 * GZH)
 GYA, GYB, GYY = pl.ds(2 * GZH, GYH), pl.ds(2 * GZH + GYH, GYH), pl.ds(2 * GZH, 2 * GYH)
 ZLO, ZHI, YLO, YHI = pl.ds(0, ZH), pl.ds(ZH, ZH), pl.ds(0, YH), pl.ds(YH, YH)
@@ -302,15 +176,16 @@
 
 
 class Scatter:
-    def __init__(self, ring, part, scratch, own):
+    def __init__(self, ring, part, scratch, own, source=None):
         self.ring, self.part, self.own = ring, part, own
+        self.source = part if source is None else source
         self.yb, self.zb, self.yr, self.zsend, self.zf, ssem, rsem = scratch
         self.s = Sends(ssem, rsem)
 
     ORDER = (2, 1, 3, 0)
 
     def start(self, k):
-        g, s, p, own = self.ring, self.s, self.part, self.own
+        g, s, p, own = self.ring, self.s, self.source, self.own
         if k == 2:
             s.go(0, p.at[g.quarter(2, own), ZB], self.zb.at[0], g.right)
             s.go(1, p.at[g.quarter(2, own), ZA], self.zb.at[1], g.left)
@@ -582,10 +457,303 @@
 ANY = pl.BlockSpec(memory_space=pl.ANY)
 
 
-def bwd_kernel(blocks, seg_ref, ga_ref, wout_ref, low_ref, ffn_ref, resid_ref, qp_ref, kp_ref, vp_ref, gp_ref, ba_ref, cq_ref, ck_ref, cv_ref, rate_ref, bias_ref, gain_ref,
-               q_ref, k_ref, x_ref, u_ref, s_ref, o_ref,
-               dqp_ref, dkp_ref, dvp_ref, dgp_ref, dba_ref, dtap_ref, dsmall_ref, dgain_ref, oshard_ref, grads_ref,
-               qpad, kpad, vpad, segpad, gm_ref, do_s, y_s, z_s, ds_s, dq_s, dk_s, left, *rest):
+def decay_rows(dlog_ref, dbias_ref):
+    lane = lax.broadcasted_iota(jnp.int32, (1, L), 1)
+
+    def place(ref):
+        return jnp.where(lane == 2, ref[0:1, 0:1], jnp.where(lane == 3, ref[0:1, 1:2], 0.0))
+
+    return jnp.where((lane == 2) | (lane == 3), -jnp.exp(place(dlog_ref)), 0.0), place(dbias_ref)
+
+
+def doc_masks(segpad, base, n, ahead):
+    s = segpad[pl.ds(base + (PAD if ahead else 0), n + PAD), :]
+    if ahead:
+        return [(s[k:k + n] == s[:n]).astype(F32) for k in range(1, 4)]
+    return [(s[PAD - k:PAD - k + n] == s[PAD:]).astype(F32) for k in range(1, 4)]
+
+
+def conv_block(base, pre_ref, taps_ref, cols, masks, n=L):
+    z = pre_ref[pl.ds(base, n + PAD), cols]
+    total = z[PAD:] * taps_ref[0:1, cols]
+    for k in range(1, 4):
+        total = total + z[PAD - k:PAD - k + n] * (masks[k - 1] * taps_ref[k:k + 1, cols])
+    return total
+
+
+def inverse_many(mats):
+    r = lax.broadcasted_iota(jnp.int32, (L, L), 0)
+    c = lax.broadcasted_iota(jnp.int32, (L, L), 1)
+    eye = (r == c).astype(F32)
+    xs = [eye - jnp.where((r // 2 == c // 2), a, 0.0) for a in mats]
+    s = 2
+    while s < L:
+        pick = (r // (2 * s) == c // (2 * s)) & (r // s != c // s)
+        sx = [split(x) for x in xs]
+        sa = [split(jnp.where(pick, a, 0.0)) for a in mats]
+        t = [mm3(x, a) for x, a in zip(sx, sa)]
+        xs = [x - mm3(split(y), z) for x, y, z in zip(xs, t, sx)]
+        s *= 2
+    return xs
+
+
+def front_kernel(blocks, group, x_ref, again_ref, wq_any, wk_any, wv_any, wt_any, wba_any, wout_any, segments_ref, cq_ref, ck_ref, cv_ref,
+                 dlog_ref, dbias_ref, gain_ref, fgain_ref,
+                 hidmid_ref, resid_ref, *rest):
+    outs, rest = rest[:23], rest[23:]
+    saved, rest = rest[:23], rest[23:]
+    (hid, low_ref, qpad, kpad, vpad, segpad, gp_ref, ba_ref, q_ref, k_ref, x_s, u_ref, s_ref, o_ref,
+     fq, fk, fv, pp, kkp, db, z_s, cols_s, brow) = saved
+    wq, wk, wv, wt, wba, wout, w_s, u0_s, kw_s, part, whole, seg_ref, wsem, osem = rest[:14]
+    scr, gsem = rest[14:21], rest[21:23]
+    T = blocks * L
+    own = resid_ref.shape[0]
+    fetch = [pltpu.make_async_copy(src, dst, wsem.at[i]) for i, (src, dst) in enumerate(
+        ((wq_any, wq), (wk_any, wk), (wv_any, wv), (wt_any, wt), (wba_any, wba), (wout_any, wout)))]
+    leave = [pltpu.make_async_copy(src, dst, osem.at[i]) for i, (src, dst) in enumerate(zip(saved, outs))]
+    for f in fetch:
+        f.start()
+    rate, bias = decay_rows(dlog_ref, dbias_ref)
+
+    def norm(i, _):
+        r = pl.ds(pl.multiple_of(i * 32, 32), 32)
+        v = x_ref[r, :].astype(F32)
+        n = v * lax.rsqrt(jnp.mean(v * v, axis=-1, keepdims=True) + 1e-05)
+        hid[r, :] = (n * again_ref[0:1, :]).astype(BF16)
+        return 0
+
+    lax.fori_loop(0, T // 32, norm, 0)
+    for pad in (qpad, kpad, vpad):
+        pad[0:PAD, :] = jnp.zeros((PAD, pad.shape[1]), F32)
+    segpad[0:PAD, :] = jnp.full((PAD, L), -1.0, F32)
+    segpad[PAD + T:, :] = jnp.full((PAD, L), -1.0, F32)
+    for b in range(blocks):
+        seg_ref[b, 0:1, :] = segments_ref[0:1, b * L:(b + 1) * L].astype(F32)
+        seg_ref[b, 1:2, :] = jnp.broadcast_to(segments_ref[0:1, max(b * L - 1, 0):max(b * L - 1, 0) + 1].astype(F32), (1, L))
+        segpad[PAD + b * L:PAD + (b + 1) * L, :] = jnp.broadcast_to(seg_ref[b, 0:1, :], (L, L)).T
+    for i, (w, dst, lead) in enumerate(((wq, qpad, PAD), (wk, kpad, PAD), (wv, vpad, PAD), (wt, gp_ref, 0), (wba, ba_ref, 0))):
+        fetch[i].wait()
+
+        def project(j, _):
+            r = pl.multiple_of(j * 256, 256)
+            dst[pl.ds(r + lead, 256), :] = mm1(hid[pl.ds(r, 256), :], w[...], NT if w is wba else NN)
+            return 0
+
+        lax.fori_loop(0, T // 256, project, 0)
+    for i in range(8):
+        if i != 1:
+            leave[i].start()
+
+    def phase_a(g, _):
+        a_mats, keepers = [], []
+        for i in range(group):
+            b = g * group + i
+            base = pl.multiple_of(b * L, L)
+            here = pl.ds(base, L)
+            per_head, strict_keep, _u = block_decay(b, seg_ref, ba_ref, rate, bias)
+            masks = doc_masks(segpad, base, L, False)
+            for h in range(2):
+                decay, carry, beta_row, beta_col, last_decay = per_head[h]
+                kc = slice(h * 128, h * 128 + 128)
+                vc = slice(h * 256, h * 256 + 256)
+                y = conv_block(base, qpad, cq_ref, kc, masks)
+                sg = sigmoid(y)
+                q = y * sg
+                r = lax.rsqrt(jnp.sum(q * q, axis=-1, keepdims=True) + 1e-06) * (128 ** -0.5)
+                q_ref[here, kc] = q * r
+                fq[here, kc] = r * (sg + q * (1.0 - sg))
+                y = conv_block(base, kpad, ck_ref, kc, masks)
+                sg = sigmoid(y)
+                k = y * sg
+                r = lax.rsqrt(jnp.sum(k * k, axis=-1, keepdims=True) + 1e-06)
+                fk[here, kc] = r * (sg + k * (1.0 - sg))
+                k = k * r
+                k_ref[here, kc] = k
+                halves = []
+                for j in range(2):
+                    c = slice(h * 256 + j * 128, h * 256 + j * 128 + 128)
+                    y = conv_block(base, vpad, cv_ref, c, masks)
+                    sg = sigmoid(y)
+                    v = y * sg
+                    fv[here, c] = sg + v * (1.0 - sg)
+                    halves.append(v)
+                ks = split(k)
+                kk = jnp.where(strict_keep, decay, 0.0) * mm3(ks, ks, NT)
+                kkp[here, kc] = kk
+                a_mats.append(kk * beta_row)
+                kw_s[here, kc] = k * (last_decay * beta_col)
+                keepers.append((here, kc, vc, jnp.concatenate(halves, axis=1), k * carry))
+        xs = inverse_many(a_mats)
+        for x, (here, kc, vc, v, gk) in zip(xs, keepers):
+            x_s[here, kc] = x
+            sx = split(x)
+            u0_s[here, vc] = mm3(sx, split(v))
+            w_s[here, kc] = mm3(sx, split(gk))
+        return 0
+
+    lax.fori_loop(0, blocks // group, phase_a, 0)
+
+    def phase_b(b, state):
+        base = pl.multiple_of(b * L, L)
+        here = pl.ds(base, L)
+        per_head, strict_keep, _u = block_decay(b, seg_ref, ba_ref, rate, bias)
+        new = []
+        for h in range(2):
+            decay, carry, beta_row, beta_col, last_decay = per_head[h]
+            kc = slice(h * 128, h * 128 + 128)
+            vc = slice(h * 256, h * 256 + 256)
+            s = state[h]
+            s_ref[here, vc] = s
+            u = u0_s[here, vc] - mm3(split(w_s[here, kc]), split(s))
+            u_ref[here, vc] = u
+            new.append(carry[L - 1:L, :] * s + mm3(split(kw_s[here, kc]), split(u), TN))
+        return tuple(new)
+
+    zero = jnp.zeros((128, 256), F32)
+    lax.fori_loop(0, blocks, phase_b, (zero, zero))
+
+    def phase_c(b, _):
+        base = pl.multiple_of(b * L, L)
+        here = pl.ds(base, L)
+        per_head, strict_keep, _u = block_decay(b, seg_ref, ba_ref, rate, bias)
+        for h in range(2):
+            decay, carry, beta_row, beta_col, last_decay = per_head[h]
+            kc = slice(h * 128, h * 128 + 128)
+            vc = slice(h * 256, h * 256 + 256)
+            q = q_ref[here, kc]
+            qk = decay * mm3(split(q), split(k_ref[here, kc]), NT)
+            pp[here, kc] = qk
+            o = mm3(split(q * carry), split(s_ref[here, vc])) + mm3(split(qk * beta_row), split(u_ref[here, vc]))
+            o_ref[here, vc] = o
+            gp = gp_ref[here, vc]
+            n = o * lax.rsqrt(jnp.mean(o * o, axis=-1, keepdims=True) + 1e-05)
+            low_ref[here, vc] = (n * gain_ref[0:1, :] * (gp * sigmoid(gp))).astype(BF16)
+        return 0
+
+    lax.fori_loop(0, blocks, phase_c, 0)
+
+    ring = Ring()
+    mine = ring.rows(0, False, own)
+    fetch[5].wait()
+    greet([ring.right, ring.left, ring.flip])
+    sc = Scatter(ring, part, scr, own)
+    for k in sc.ORDER:
+        quarter = ring.quarter(k, own)
+
+        def partial(n, _):
+            c = pl.ds(pl.multiple_of(n * 512, 512), 512)
+            part[quarter, c] = mm1(low_ref[quarter, :], wout[:, c], NN)
+            return 0
+
+        lax.fori_loop(0, part.shape[1] // 512, partial, 0)
+        sc.start(k)
+    for i in (1, 8, 9, 10, 11, 12, 13, 14, 15, 16, 17, 18):
+        leave[i].start()
+
+    def prepare(b, _):
+        base = pl.multiple_of(b * L, L)
+        here = pl.ds(base, L)
+        per_head, strict_keep, _u = block_decay(b, seg_ref, ba_ref, rate, bias)
+        lane = lax.broadcasted_iota(jnp.int32, (L, L), 1)
+        row = lax.broadcasted_iota(jnp.int32, (8, L), 0)
+        tile, flat = jnp.zeros((L, L), F32), jnp.zeros((8, L), F32)
+        for h in range(2):
+            decay, carry, beta_row, beta_col, last_decay = per_head[h]
+            kc = slice(h * 128, h * 128 + 128)
+            db[here, kc] = decay * beta_row
+            z_s[here, kc] = mm3(split(x_s[here, kc]), split(kw_s[here, kc]), TN)
+            tile = tile + (jnp.where(lane == h, carry, 0.0) + jnp.where(lane == 2 + h, last_decay * beta_col, 0.0)
+                           + jnp.where(lane == 4 + h, last_decay, 0.0))
+            flat = flat + jnp.where(row == h, beta_row, 0.0)
+        cols_s[here, :] = tile
+        brow[b] = flat
+        return 0
+
+    steps = sc.middle()
+    run(steps, 1)
+    lax.fori_loop(0, blocks // 2, prepare, 0)
+    run(steps, 1)
+    lax.fori_loop(blocks // 2, blocks, prepare, 0)
+    for i in range(19, 23):
+        leave[i].start()
+    run(steps)
+    sc.finish()
+
+    def finish(i, _):
+        r = pl.multiple_of(i * 16, 16)
+        at = pl.ds(pl.multiple_of(mine.start + r, 16), 16)
+        resid = x_ref[at, :].astype(F32) + sc.value(r)
+        resid_ref[pl.ds(r, 16), :] = resid
+        n = resid * lax.rsqrt(jnp.mean(resid * resid, axis=-1, keepdims=True) + 1e-05)
+        whole[at, :] = (n * fgain_ref[0:1, :]).astype(BF16).astype(F32)
+        return 0
+
+    lax.fori_loop(0, own // 16, finish, 0)
+    ga = Gather(ring, whole, gsem, own)
+    ga.start()
+    run(ga.middle())
+    ga.finish()
+
+    def cast(i, _):
+        r = pl.ds(pl.multiple_of(i * 32, 32), 32)
+        hidmid_ref[r, :] = whole[r, :].astype(BF16)
+        return 0
+
+    lax.fori_loop(0, whole.shape[0] // 32, cast, 0)
+    sc.s.drain()
+    ga.s.drain()
+    for c in leave:
+        c.wait()
+
+
+def front(x, again, wq, wk, wv, wt, wba, wout, segments, cq, ck, cv, dlog, dbias, gain, fgain, group=2):
+    T, D = x.shape
+    blocks = T // L
+    own = T // NT_
+    sd = jax.ShapeDtypeStruct
+    saved = [((T, D), BF16), ((T, 512), BF16), ((T + PAD, 256), F32), ((T + PAD, 256), F32), ((T + PAD, 512), F32), ((T + 2 * PAD, L), F32),
+             ((T, 512), F32), ((T, 128), F32), ((T, 256), F32), ((T, 256), F32), ((T, 256), F32), ((T, 512), F32), ((T, 512), F32), ((T, 512), F32),
+             ((T, 256), F32), ((T, 256), F32), ((T, 512), F32), ((T, 256), F32), ((T, 256), F32), ((T, 256), F32), ((T, 256), F32),
+             ((T, 128), F32), ((blocks, 8, L), F32)]
+    vm = lambda s, t: pltpu.VMEM(s, t)
+    return pl.pallas_call(
+        functools.partial(front_kernel, blocks, group),
+        out_shape=[sd((T, D), BF16), sd((own, D), F32)] + [sd(*s) for s in saved],
+        in_specs=[VM, VM] + [ANY] * 6 + [VM] * 8, out_specs=[VM, VM] + [ANY] * 23,
+        scratch_shapes=[vm(*s) for s in saved] + [vm(w.shape, BF16) for w in (wq, wk, wv, wt, wba, wout)]
+        + [vm((T, 256), F32), vm((T, 512), F32), vm((T, 256), F32), vm((T, D), F32), vm((T, D), F32), vm((blocks, 8, L), F32),
+           pltpu.SemaphoreType.DMA((6,)), pltpu.SemaphoreType.DMA((23,))] + scatter_scratch(own) + gather_sems(),
+        compiler_params=params(1, 62),
+        name="front",
+    )(x, again, wq, wk, wv, wt, wba, wout, segments, cq, ck, cv, dlog, dbias, gain, fgain)
+
+
+SMALL = 40
+TAPS = 40
+
+
+BACK = ("ga", "wout", "low", "ffn", "o", "gp", "pp", "x", "q", "cols", "brow", "k", "z", "u", "s", "db", "kkp", "ba",
+        "qpad", "kpad", "vpad", "segpad", "fq", "fk", "fv")
+
+
+def bwd_kernel(blocks, *refs):
+    count = len(BACK)
+    sources, rest = refs[:count], refs[count:]
+    (resid_ref, cq_ref, ck_ref, cv_ref, dlog_ref, dbias_ref, gain_ref,
+     dqp_ref, dkp_ref, dvp_ref, dgp_ref, dba_ref, dtap_ref, dgain_ref, oshard_ref, grads_ref) = rest[:16]
+    held, rest = rest[16:16 + count], rest[16 + count:]
+    fsem, gm_ref, do_s, y_s, ds_s, dq_s, dk_s, left, tap_s = rest[:9]
+    rest = rest[9:]
+    (ga_ref, wout_ref, low_ref, ffn_ref, o_ref, gp_ref, pp, x_ref, q_ref, cols_s, brow, k_ref, z_s, u_ref, s_ref, db, kkp, ba_ref,
+     qpad, kpad, vpad, segpad, fq, fk, fv) = held
+    fetch = [pltpu.make_async_copy(src, dst, fsem.at[i]) for i, (src, dst) in enumerate(zip(sources, held))]
+    for c in fetch:
+        c.start()
+
+    def need(first, last):
+        for c in fetch[first:last]:
+            c.wait()
+
     T = blocks * L
     scr, dscr = rest[:7], rest[7:]
     own = resid_ref.shape[0]
@@ -596,9 +764,10 @@
 
     dp = DpScatter(ring, dscr, compute)
     greet([ring.right, ring.left, ring.flip] + dp.devices())
-    sc = Scatter(ring, ffn_ref, scr, own)
+    sc = Scatter(ring, ffn_ref, scr, own, sources[3])
     for k in sc.ORDER:
         sc.start(k)
+    need(0, 3)
     left[...] = low_ref[...].T
     steps, cores, along = sc.middle(), dp.cores(), dp.along()
     run(cores)
@@ -609,25 +778,20 @@
         return 0
 
     lax.fori_loop(0, T // 256, mixed_back, 0)
+    run(along, 1)
+    need(3, 4)
+    run(steps, 2)
     run(along)
-    run(steps, 1)
-    rate, bias = rate_ref[0:1, :], bias_ref[0:1, :]
-    for pad, src in ((qpad, qp_ref), (kpad, kp_ref), (vpad, vp_ref)):
-        pad[0:PAD, :] = jnp.zeros((PAD, pad.shape[1]), F32)
-        pad[PAD:PAD + T, :] = src[...]
-    segpad[0:PAD, :] = jnp.full((PAD, L), -1.0, F32)
-    segpad[PAD + T:, :] = jnp.full((PAD, L), -1.0, F32)
-    for b in range(blocks):
-        segpad[PAD + b * L:PAD + (b + 1) * L, :] = jnp.broadcast_to(seg_ref[b, 0:1, :], (L, L)).T
+    need(4, 11)
+    rate, bias = decay_rows(dlog_ref, dbias_ref)
     dgain_ref[...] = jnp.zeros_like(dgain_ref)
-    dsmall_ref[...] = jnp.zeros_like(dsmall_ref)
-    dtap_ref[...] = jnp.zeros_like(dtap_ref)
+    dtap_ref[32:40, :] = jnp.zeros((8, 128), F32)
+    tap_s[...] = jnp.zeros_like(tap_s)
 
     def phase_1(b, _):
         base = pl.multiple_of(b * L, L)
-        per_head, strict_keep, _u = block_decay(b, seg_ref, ba_ref, rate, bias)
         for h in range(2):
-            decay, carry, beta_row, beta_col, last_decay = per_head[h]
+            carry = cols_s[pl.ds(base, L), h:h + 1]
             kc = slice(h * 128, h * 128 + 128)
             vc = slice(h * 256, h * 256 + 256)
             o = o_ref[pl.ds(base, L), vc]
@@ -640,18 +804,16 @@
             act = gp * sg
             gn = gm * n
             dgain_ref[0:1, :] = dgain_ref[0:1, :] + jnp.sum(gn * act, axis=0, keepdims=True)
-            dgp_ref[pl.ds(base, L), vc] = (gn * gain * (sg * (1.0 + gp * (1.0 - sg)))).astype(BF16)
+            dgp_ref[pl.ds(base, L), vc] = (gn * gain * (sg + act * (1.0 - sg))).astype(BF16)
             dn = gm * gain * act
             do = r * (dn - n * jnp.mean(dn * n, axis=-1, keepdims=True))
             do_s[pl.ds(base, L), vc] = do
-            q, k = q_ref[pl.ds(base, L), kc], k_ref[pl.ds(base, L), kc]
-            p = decay * mm3(split(q), split(k), NT) * beta_row
+            q = q_ref[pl.ds(base, L), kc]
+            p = pp[pl.ds(base, L), kc] * brow[b, h:h + 1, :]
             sdo = split(do)
             sx = split(x_ref[pl.ds(base, L), kc])
             y0 = mm3(sx, split(mm3(split(p), sdo, TN)), TN)
-            z = mm3(sx, split(k * (last_decay * beta_col)), TN)
             y_s[pl.ds(base, L), vc] = y0
-            z_s[pl.ds(base, L), kc] = z
             ds_s[pl.ds(base, L), vc] = mm3(split(q * carry), sdo, TN)
         return 0
 
@@ -660,14 +822,14 @@
     lax.fori_loop(blocks // 2, blocks, phase_1, 0)
     run(steps, 1)
     dp.second()
+    need(11, 13)
 
     def phase_2(i, grads):
         b = blocks - 1 - i
         base = pl.multiple_of(b * L, L)
-        per_head, strict_keep, _u = block_decay(b, seg_ref, ba_ref, rate, bias)
         new = []
         for h in range(2):
-            decay, carry, beta_row, beta_col, last_decay = per_head[h]
+            carry = cols_s[pl.ds(base, L), h:h + 1]
             kc = slice(h * 128, h * 128 + 128)
             vc = slice(h * 256, h * 256 + 256)
             ds = grads[h]
@@ -683,22 +845,22 @@
     lax.fori_loop(0, blocks, phase_2, (zero, zero))
     run(steps)
     dp.third()
+    need(13, 18)
 
     def phase_3(b, _):
         base = pl.multiple_of(b * L, L)
-        per_head, strict_keep, (tile, seg_col) = block_decay(b, seg_ref, ba_ref, rate, bias)
         lane = lax.broadcasted_iota(jnp.int32, (L, L), 1)
         rowi = lax.broadcasted_iota(jnp.int32, (L, L), 0)
         row_tile = jnp.zeros((L, L), F32)
         col_tile = jnp.zeros((L, L), F32)
         for h in range(2):
-            decay, carry, beta_row, beta_col, last_decay = per_head[h]
+            carry, weight, last_decay = (cols_s[pl.ds(base, L), j:j + 1] for j in (h, 2 + h, 4 + h))
+            beta_row = brow[b, h:h + 1, :]
             kc = slice(h * 128, h * 128 + 128)
             vc = slice(h * 256, h * 256 + 256)
             q, k = q_ref[pl.ds(base, L), kc], k_ref[pl.ds(base, L), kc]
             sq, sk = split(q), split(k)
-            kk = mm3(sk, sk, NT)
-            qk = mm3(sq, sk, NT)
+            decay_beta = db[pl.ds(base, L), kc]
             s, u = s_ref[pl.ds(base, L), vc], u_ref[pl.ds(base, L), vc]
             do, y, ds = do_s[pl.ds(base, L), vc], y_s[pl.ds(base, L), vc], ds_s[pl.ds(base, L), vc]
             ss, su, sdo, sy, sds = split(s), split(u), split(do), split(y), split(ds)
@@ -710,16 +872,14 @@
             dcarry = jnp.sum(q * do_st - k * y_st, axis=-1, keepdims=True)
             dcarry_last = jnp.sum(jnp.sum(ds * s, axis=0, keepdims=True), axis=1, keepdims=True)
             dw = jnp.sum(u_dst * k, axis=-1, keepdims=True)
-            dpd = dp * decay
-            dad = jnp.where(strict_keep, da * decay, 0.0)
-            dqk = dpd * beta_row
-            dkk = dad * beta_row
-            prod = dpd * qk + dad * kk
+            dqk = dp * decay_beta
+            dkk = jnp.where(rowi > lane, da * decay_beta, 0.0)
+            prod = dp * pp[pl.ds(base, L), kc] + da * kkp[pl.ds(base, L), kc]
             dbeta_row = jnp.sum(prod, axis=0, keepdims=True)
             dec_grad = prod * beta_row
             dc_col = jnp.sum(dec_grad, axis=1, keepdims=True) + dcarry * carry
             dc_row = -jnp.sum(dec_grad, axis=0, keepdims=True)
-            dlast = dw * beta_col * last_decay
+            dlast = dw * weight
             row1 = rowi[:, 0:1]
             dc_col = dc_col - dlast
             dc_col = dc_col + jnp.where(row1 == L - 1, jnp.sum(dlast, axis=0, keepdims=True) + dcarry_last * carry, 0.0)
@@ -729,19 +889,60 @@
             sdqk, sdkk = split(dqk), split(dkk + dkk.T)
             dq_s[pl.ds(base, L), kc] = carry * do_st + mm3(sdqk, sk)
             dk_s[pl.ds(base, L), kc] = (mm3(sdqk, sq, TN) + mm3(sdkk, sk) - carry * y_st
-                                        + (last_decay * beta_col) * u_dst)
+                                        + weight * u_dst)
         grad = col_tile + row_tile.T
         dld = tri_sum(grad, TN)
         ba = rows(ba_ref, b)
+        tile = decay_tile(ba, rate, bias)
         sig_alpha = sigmoid(ba + bias)
         dalpha = dld * rate * sig_alpha
         dpre = jnp.where(lane < 2, grad * tile * (1.0 - tile), jnp.where(lane < 4, dalpha, 0.0))
         dba_ref[pl.ds(base, L), :] = dpre.astype(BF16)
-        dsmall_ref[0:1, :] = dsmall_ref[0:1, :] + jnp.sum(dpre, axis=0, keepdims=True)
-        dsmall_ref[1:2, :] = dsmall_ref[1:2, :] + jnp.sum(dld * tile, axis=0, keepdims=True)
+        dtap_ref[32:33, :] = dtap_ref[32:33, :] + jnp.sum(dpre, axis=0, keepdims=True)
+        dtap_ref[33:34, :] = dtap_ref[33:34, :] + jnp.sum(dld * tile, axis=0, keepdims=True)
         return 0
 
     lax.fori_loop(0, blocks, phase_3, 0)
+
+    need(18, count)
+
+    R = 64
+    groups = []
+    for h in range(2):
+        c = slice(h * 128, h * 128 + 128)
+        groups.append((qpad, cq_ref, dq_s, dqp_ref, fq, c, h * 128, q_ref, 128.0))
+        groups.append((kpad, ck_ref, dk_s, dkp_ref, fk, c, 256 + h * 128, k_ref, 1.0))
+    for j in range(4):
+        groups.append((vpad, cv_ref, y_s, dvp_ref, fv, slice(j * 128, j * 128 + 128), 512 + j * 128, None, None))
+    for src in (dq_s, dk_s, y_s):
+        src[T:, :] = jnp.zeros((PAD, src.shape[1]), F32)
+
+    def conv_back(i, _):
+        base = pl.multiple_of((T // R - 1 - i) * R, R)
+        here = pl.ds(base, R)
+        behind, ahead = doc_masks(segpad, base, R, False), doc_masks(segpad, base, R, True)
+        for pre, taps, src, out_ref, factor, c, tc, unit, size in groups:
+            d = src[here, c]
+            if unit is not None:
+                v = unit[here, c]
+                d = d - v * (size * jnp.sum(d * v, axis=-1, keepdims=True))
+            dy = factor[here, c] * d
+            src[here, c] = dy
+            z = pre[pl.ds(base, R + PAD), c]
+            both = src[pl.ds(base, R + PAD), c]
+            tc = slice(tc, tc + 128)
+            total = dy * taps[0:1, c]
+            tap_s[0, :, tc] = tap_s[0, :, tc] + jnp.sum((dy * z[PAD:]).reshape(R // 8, 8, 128), axis=0)
+            for t in range(1, 4):
+                total = total + both[t:t + R] * (ahead[t - 1] * taps[t:t + 1, c])
+                tap_s[t, :, tc] = tap_s[t, :, tc] + jnp.sum((dy * (z[PAD - t:PAD - t + R] * behind[t - 1])).reshape(R // 8, 8, 128), axis=0)
+            out_ref[here, c] = total.astype(BF16)
+        return 0
+
+    lax.fori_loop(0, T // R, conv_back, 0)
+    for t in range(4):
+        for j in range(8):
+            dtap_ref[t * 8 + j:t * 8 + j + 1, :] = jnp.sum(tap_s[t, :, j * 128:(j + 1) * 128], axis=0, keepdims=True)
     sc.finish()
 
     def finish(i, _):
@@ -753,136 +954,25 @@
     dp.finish(grads_ref)
     sc.s.drain()
 
-    def conv_back(pre, taps_ref, src, out_ref, cols, tap_cols, scale):
-        do_s[T:, cols] = jnp.zeros((PAD, 128), F32)
-
-        def one(b, tap_grads):
-            base = pl.multiple_of(b * L, L)
-            y = conv_block(b, pre, taps_ref, None, cols, segpad)
-            sg = sigmoid(y)
-            act = y * sg
-            d = src[pl.ds(base, L), cols]
-            if scale is not None:
-                r = lax.rsqrt(jnp.sum(act * act, axis=-1, keepdims=True) + 1e-06)
-                d = (scale * r) * (d - act * (r * r * jnp.sum(d * act, axis=-1, keepdims=True)))
-            dy = d * (sg * (1.0 + y * (1.0 - sg)))
-            do_s[pl.ds(base, L), cols] = dy
-            z = pre[pl.ds(base, L + PAD), cols]
-            s = segpad[pl.ds(base, L + PAD), 0:1]
-            new = [tap_grads[0] + jnp.sum(dy * z[PAD:], axis=0, keepdims=True)]
-            for t in range(1, 4):
-                same = (s[PAD - t:PAD - t + L] == s[PAD:]).astype(F32)
-                new.append(tap_grads[t] + jnp.sum(dy * (z[PAD - t:PAD - t + L] * same), axis=0, keepdims=True))
-            return tuple(new)
-
-        zero = jnp.zeros((1, 128), F32)
-        res = lax.fori_loop(0, blocks, one, (zero,) * 4)
-        for t in range(4):
-            dtap_ref[t:t + 1, tap_cols] = res[t]
-
-        def two(b, _):
-            base = pl.multiple_of(b * L, L)
-            dy = do_s[pl.ds(base, L + PAD), cols]
-            s = segpad[pl.ds(base + PAD, L + PAD), 0:1]
-            total = dy[:L] * taps_ref[0:1, cols]
-            for t in range(1, 4):
-                same = (s[t:t + L] == s[:L]).astype(F32)
-                total = total + dy[t:t + L] * same * taps_ref[t:t + 1, cols]
-            out_ref[pl.ds(base, L), cols] = total.astype(BF16)
-            return 0
-
-        lax.fori_loop(0, blocks, two, 0)
-
-    for h in range(2):
-        c = slice(h * 128, h * 128 + 128)
-        conv_back(qpad, cq_ref, dq_s, dqp_ref, c, slice(h * 128, h * 128 + 128), 128 ** -0.5)
-        conv_back(kpad, ck_ref, dk_s, dkp_ref, c, slice(256 + h * 128, 256 + h * 128 + 128), 1.0)
-    for j in range(4):
-        c = slice(j * 128, j * 128 + 128)
-        conv_back(vpad, cv_ref, y_s, dvp_ref, c, slice(512 + j * 128, 512 + j * 128 + 128), None)
-
-
-def mixer_bwd(seg3, ga, wout, low, ffn, resid, qp, kp, vp, gp, ba, cq, ck, cv, rate, bias, gain, q, k, x, u, s, o):
-    T = qp.shape[0]
+
+def mixer_bwd(resid, cq, ck, cv, dlog, dbias, gain, **held):
+    T, D = held["ga"].shape
     blocks = T // L
-    own, D = resid.shape
-    n = low.shape[1]
+    own = resid.shape[0]
+    n = held["low"].shape[1]
     sd = jax.ShapeDtypeStruct
-    vm = lambda r, w: pltpu.VMEM((r, w), F32)
+    vm = lambda *r: pltpu.VMEM(r, F32)
     return pl.pallas_call(
         functools.partial(bwd_kernel, blocks),
         out_shape=(sd((T, 256), BF16), sd((T, 256), BF16), sd((T, 512), BF16), sd((T, 512), BF16), sd((T, 128), BF16),
-                   sd((8, 1024), F32), sd((8, 128), F32), sd((8, 256), F32), sd((own, D), F32), sd((n, 128), F32)),
-        in_specs=[VM] * 23, out_specs=[VM] * 10,
-        scratch_shapes=[vm(T + PAD, 256), vm(T + PAD, 256), vm(T + PAD, 512), vm(T + 2 * PAD, L), vm(T, 512),
-                        vm(T + PAD, 512), vm(T, 512), vm(T, 256), vm(T, 512), vm(T, 256), vm(T, 256), pltpu.VMEM((n, T), BF16)]
-        + scatter_scratch(own) + dp_scratch(n),
-        compiler_params=params(4, 60),
+                   sd((TAPS, 128), F32), sd((8, 256), F32), sd((own, D), F32), sd((n, 128), F32)),
+        in_specs=[ANY] * len(BACK) + [VM] * 7, out_specs=[VM] * 9,
+        scratch_shapes=[pltpu.VMEM(held[name].shape, held[name].dtype) for name in BACK]
+        + [pltpu.SemaphoreType.DMA((len(BACK),)), vm(T, 512), vm(T, 512), vm(T + PAD, 512), vm(T, 512), vm(T + PAD, 256), vm(T + PAD, 256),
+           pltpu.VMEM((n, T), BF16), vm(4, 8, 1024)] + scatter_scratch(own) + dp_scratch(n, 4),
+        compiler_params=params(4, 62),
         name="mixer_backward",
-    )(seg3, ga, wout, low, ffn, resid, qp, kp, vp, gp, ba, cq, ck, cv, rate, bias, gain, q, k, x, u, s, o)
-
-
-def attn_kernel(low_ref, w_ref, x_ref, gain_ref, hid_ref, resid_ref, part, whole, xown, csem, *rest):
-    scr, gsem = rest[:7], rest[7:]
-    ring = Ring()
-    own = resid_ref.shape[0]
-    mine = ring.rows(0, False, own)
-    fetch = pltpu.make_async_copy(x_ref.at[mine], xown, csem)
-    fetch.start()
-
-    greet([ring.right, ring.left, ring.flip])
-    sc = Scatter(ring, part, scr, own)
-    for k in sc.ORDER:
-        quarter = ring.quarter(k, own)
-
-        def partial(n, _):
-            cols = pl.ds(pl.multiple_of(n * 512, 512), 512)
-            part[quarter, cols] = mm1(low_ref[quarter, :], w_ref[:, cols], NN)
-            return 0
-
-        lax.fori_loop(0, part.shape[1] // 512, partial, 0)
-        sc.start(k)
-    fetch.wait()
-    run(sc.middle())
-    sc.finish()
-
-    def finish(i, _):
-        r = pl.multiple_of(i * 16, 16)
-        resid = xown[pl.ds(r, 16), :].astype(F32) + sc.value(r)
-        resid_ref[pl.ds(r, 16), :] = resid
-        n = resid * lax.rsqrt(jnp.mean(resid * resid, axis=-1, keepdims=True) + 1e-05)
-        whole[pl.ds(pl.multiple_of(mine.start + r, 16), 16), :] = (n * gain_ref[0:1, :]).astype(BF16).astype(F32)
-        return 0
-
-    lax.fori_loop(0, own // 16, finish, 0)
-    ga = Gather(ring, whole, gsem, own)
-    ga.start()
-    run(ga.middle())
-    ga.finish()
-
-    def cast(i, _):
-        r = pl.ds(pl.multiple_of(i * 32, 32), 32)
-        hid_ref[r, :] = whole[r, :].astype(BF16)
-        return 0
-
-    lax.fori_loop(0, whole.shape[0] // 32, cast, 0)
-    sc.s.drain()
-    ga.s.drain()
-
-
-def attn_exchange(low, w_out, inputs, gain):
-    T, D = inputs.shape
-    own = T // NT_
-    sd = jax.ShapeDtypeStruct
-    return pl.pallas_call(
-        attn_kernel,
-        out_shape=(sd((T, D), BF16), sd((own, D), F32)),
-        in_specs=[VM, VM, ANY, VM], out_specs=[VM, VM],
-        scratch_shapes=[pltpu.VMEM((T, D), F32), pltpu.VMEM((T, D), F32), pltpu.VMEM((own, D), BF16),
-                        pltpu.SemaphoreType.DMA(())] + scatter_scratch(own) + gather_sems(),
-        compiler_params=params(1, 56),
-        name="attn_exchange",
-    )(low, w_out, inputs, gain)
+    )(*[held[name] for name in BACK], resid, cq, ck, cv, dlog, dbias, gain)
 
 
 def mid_kernel(wg_ref, wu_ref, wd_any, hid_ref, og_any, resid_any, gain_ref,
@@ -999,14 +1089,15 @@
     )(wg, wu, wd, hid, og, resid, gain)
 
 
-SMALL = 40
-TAPS = 40
-
-
-def in_kernel(gq, gk, gv, gt, gba, inner_ref, wq, wk, wv, wt, wba, hid_ref, og_ref, gres_ref, x_ref, gain_ref, gains_ref, taps_ref, oshard_ref,
-              whole, out_whole, grads_ref, gains_out, taps_out,
-              part, shard, left, xown, g_own, g_recv, s_own, s_recv, csem, ssem, srsem, *rest):
+def in_kernel(*refs):
+    sources, (gres_ref, x_ref, gain_ref, fpart_ref, hgain_ref, taps_ref, oshard_ref), rest = refs[:13], refs[13:20], refs[20:]
+    whole, out_whole, grads_ref, gains_out, taps_out = rest[:5]
+    held, rest = rest[5:18], rest[18:]
+    gq, gk, gv, gt, gba, wq, wk, wv, wt, wba, inner_ref, hid_ref, og_ref = held
+    part, shard, left, xown, g_own, g_recv, s_own, s_recv, fsem, csem, ssem, srsem = rest[:12]
+    rest = rest[12:]
     scr, gsem, osem, dscr = rest[:7], rest[7:9], rest[9:11], rest[11:]
+    loads = [pltpu.make_async_copy(src, dst, fsem.at[i]) for i, (src, dst) in enumerate(zip(sources, held))]
     ring = Ring()
     own = gres_ref.shape[0]
     mine = ring.rows(0, False, own)
@@ -1014,13 +1105,16 @@
     fetch.start()
     place_out = pltpu.make_async_copy(oshard_ref, out_whole.at[mine], csem.at[1])
     place_out.start()
+    for c in loads:
+        c.start()
     t_peers = [(ring.d, lax.rem(ring.t + j, NT_)) for j in range(1, NT_)]
     d_peers = [(lax.rem(ring.d + j, 16), ring.t) for j in range(1, 16)]
     greet(t_peers + d_peers)
     place_out.wait()
     go = Gather(ring, out_whole, osem, own)
     go.start()
-
+    for c in loads[:10]:
+        c.wait()
     sc = Scatter(ring, part, scr, own)
     for k in sc.ORDER:
         quarter = ring.quarter(k, own)
@@ -1029,7 +1123,7 @@
             rows_w = pl.ds(pl.multiple_of(i * 512, 512), 512)
             total = mm1(gq[quarter, :], wq[rows_w, :], NT) + mm1(gk[quarter, :], wk[rows_w, :], NT)
             total = total + mm1(gv[quarter, :], wv[rows_w, :], NT) + mm1(gt[quarter, :], wt[rows_w, :], NT)
-            part[quarter, rows_w] = total + mm1(gba[quarter, :], wba[rows_w, :], NT)
+            part[quarter, rows_w] = total + mm1(gba[quarter, :], wba[:, rows_w], NN)
             return 0
 
         lax.fori_loop(0, part.shape[1] // 512, partial, 0)
@@ -1047,6 +1141,8 @@
     left[512:1024, :] = gv[...].T
     left[1024:1536, :] = gt[...].T
     left[1536:1552, :] = gba[...].T[0:16]
+    for c in loads[10:]:
+        c.wait()
     left[1552:, :] = inner_ref[...].T
     outs = go.middle()
     run(outs, 1)
@@ -1054,7 +1150,12 @@
     run(outs, 2)
     fetch.wait()
     sc.finish()
-    g_own[...] = gains_ref[...]
+    g_own[...] = jnp.zeros_like(g_own)
+    ffn_gain = jnp.sum(fpart_ref[...], axis=0, keepdims=True)
+    for j in range(16):
+        g_own[16 + j:17 + j, :] = ffn_gain[:, j * 128:(j + 1) * 128]
+    for j in range(2):
+        g_own[32 + j:33 + j, :] = hgain_ref[0:1, j * 128:(j + 1) * 128]
 
     def finish(i, total):
         r = pl.multiple_of(i * 16, 16)
@@ -1110,78 +1211,109 @@
     ga.s.drain()
 
 
-def in_exchange(grads, inner, weights, hid, og, gres, inputs, gain, gains, taps, oshard):
+def in_exchange(grads, weights, inner, hid, og, gres, inputs, gain, ffn_part, hgain, taps, oshard):
     T, D = inputs.shape
     own = T // NT_
     n = 1552 + inner.shape[1]
     sd = jax.ShapeDtypeStruct
     vm = lambda *s: pltpu.VMEM(s, F32)
+    held = (*grads, *weights, inner, hid, og)
     return pl.pallas_call(
         in_kernel,
         out_shape=(sd((T, D), F32), sd((T, D), F32), sd((n, 128), F32), sd((SMALL, 128), F32), sd((TAPS, 128), F32)),
-        in_specs=[VM] * 14 + [ANY] + [VM] * 4, out_specs=[ANY, ANY, VM, VM, VM],
-        scratch_shapes=[vm(T, D), vm(own, D), pltpu.VMEM((n, T), BF16), pltpu.VMEM((own, D), BF16),
-                        vm(SMALL, 128), vm(7, SMALL, 128), vm(SMALL + TAPS, 128), vm(15, SMALL + TAPS, 128),
-                        pltpu.SemaphoreType.DMA((3,)), pltpu.SemaphoreType.DMA((22,)), pltpu.SemaphoreType.DMA((22,))]
+        in_specs=[ANY] * 13 + [VM, ANY] + [VM] * 5, out_specs=[ANY, ANY, VM, VM, VM],
+        scratch_shapes=[pltpu.VMEM(h.shape, h.dtype) for h in held]
+        + [vm(T, D), vm(own, D), pltpu.VMEM((n, T), BF16), pltpu.VMEM((own, D), BF16),
+           vm(SMALL, 128), vm(7, SMALL, 128), vm(SMALL + TAPS, 128), vm(15, SMALL + TAPS, 128),
+           pltpu.SemaphoreType.DMA((13,)), pltpu.SemaphoreType.DMA((3,)), pltpu.SemaphoreType.DMA((22,)), pltpu.SemaphoreType.DMA((22,))]
         + scatter_scratch(own) + gather_sems() + gather_sems() + dp_scratch(n, 4),
-        compiler_params=params(3, 60),
+        compiler_params=params(3, 62),
         name="in_exchange",
-    )(*grads, inner, *weights, hid, og, gres, inputs, gain, gains, taps, oshard)
-
-
-def matmul(left, right):
-    return jnp.dot(left, right, preferred_element_type=F32)
-
-
-def rows8(v):
-    return jnp.broadcast_to(v[None, :], (8, v.shape[0]))
+    )(*held, gres, inputs, gain, ffn_part, hgain, taps, oshard)
+
+
+def last_kernel(ig_ref, out_ref, gin_ref, gmid_ref, gout_ref, gains_ref, taps_ref,
+                ig_low, out_low, gq, gk, gv, gt, gbeta, galpha, cq, ck, cv, dlog, dbias, hgain, again, fgain, gug, gup, gdown, gout):
+    ig_low[...] = ig_ref[...].astype(BF16)
+    out_low[...] = out_ref[...].astype(BF16)
+
+    @pl.when(pl.program_id(0) == 0)
+    def _():
+        gq[...] = gin_ref[0:256, :].T
+        gk[...] = gin_ref[256:512, :].T
+        gv[...] = gin_ref[512:1024, :].T
+        gt[...] = gin_ref[1024:1536, :].T
+        gbeta[...] = gin_ref[1536:1538, :]
+        galpha[...] = gin_ref[1538:1540, :]
+        gdown[...] = gin_ref[1552:, :]
+        n = gug.shape[0]
+        gug[...] = gmid_ref[0:n, :]
+        gup[...] = gmid_ref[n:, :]
+        gout[...] = gout_ref[...]
+        for t in range(4):
+            for j in range(8):
+                row = taps_ref[t * 8 + j:t * 8 + j + 1, :]
+                ref, at = ((cq, j), (ck, j - 2), (cv, j - 4))[0 if j < 2 else 1 if j < 4 else 2]
+                ref[t:t + 1, at * 128:(at + 1) * 128] = row
+        dbias[...] = taps_ref[32:33, 2:4]
+        dlog[...] = taps_ref[33:34, 2:4]
+        again[...] = gains_ref[0:16, :]
+        fgain[...] = gains_ref[16:32, :]
+        hgain[...] = gains_ref[32:34, :]
+
+
+def last(ig, out, gin, gmid, gout, gains, taps):
+    T, D = ig.shape
+    n = gmid.shape[0] // 2
+    sd = lambda *s: jax.ShapeDtypeStruct(s, F32)
+    step = lambda: pl.BlockSpec((128, D), lambda i: (i, 0))
+    fixed = lambda s: pl.BlockSpec(s, lambda i: (0, 0))
+    small = [sd(128, 256), sd(128, 256), sd(128, 512), sd(128, 512), sd(2, 128), sd(2, 128), sd(4, 256), sd(4, 256), sd(4, 512),
+             sd(1, 2), sd(1, 2), sd(2, 128), sd(16, 128), sd(16, 128), sd(n, 128), sd(n, 128), sd(gin.shape[0] - 1552, 128), sd(gout.shape[0], 128)]
+    return pl.pallas_call(
+        last_kernel,
+        grid=(T // 128,),
+        out_shape=[jax.ShapeDtypeStruct((T, D), BF16)] * 2 + small,
+        in_specs=[step(), step()] + [fixed(a.shape) for a in (gin, gmid, gout, gains, taps)],
+        out_specs=[step(), step()] + [fixed(a.shape) for a in small],
+        compiler_params=pltpu.CompilerParams(vmem_limit_bytes=48 * 2 ** 20),
+        name="last",
+    )(ig, out, gin, gmid, gout, gains, taps)
+
+
+def row(v):
+    return v.reshape(1, v.shape[0])
 
 
 def per_device(inputs, segments, attn_gain, w_query, w_key, w_value, w_gate, w_beta, w_alpha, conv_query, conv_key, conv_value,
                decay_log, decay_bias, head_gain, w_out, ffn_gain, w_up_gate, w_up, w_down, out_grad):
-    T, D = inputs.shape
-    blocks = T // L
-    tokens_in = inputs.astype(F32)
-    scale_in = lax.rsqrt(jnp.mean(tokens_in * tokens_in, axis=-1, keepdims=True) + 1e-05)
-    hidden_in = (tokens_in * scale_in * attn_gain).astype(BF16)
-    w_ba = jnp.concatenate([w_beta, w_alpha, jnp.zeros((D, 124), BF16)], axis=1)
-    qp, kp, vp, gp = (matmul(hidden_in, w) for w in (w_query, w_key, w_value, w_gate))
-    ba = matmul(hidden_in, w_ba)
-    rate = jnp.zeros((8, 128), F32).at[:, 2:4].set(-jnp.exp(decay_log))
-    bias = jnp.zeros((8, 128), F32).at[:, 2:4].set(decay_bias)
-    seg = segments.astype(F32).reshape(blocks, 1, L)
-    prev = jnp.concatenate([seg[:1, :, :1], seg[:-1, :, L - 1:]], axis=0)
-    seg3 = jnp.concatenate([seg, jnp.broadcast_to(prev, seg.shape), jnp.zeros((blocks, 6, L), F32)], axis=1)
-    gain8 = rows8(head_gain)
-    low, q, k, x, u, s, o = mixer_fwd(seg3, qp, kp, vp, gp, ba, conv_query, conv_key, conv_value, rate, bias, gain8)
-    hidden_mid, resid = attn_exchange(low, w_out, inputs, rows8(ffn_gain))
+    D = inputs.shape[1]
+    w_ba = jnp.concatenate([w_beta.T, w_alpha.T, jnp.zeros((124, D), BF16)], axis=0)
+    dlog, dbias, hgain = row(decay_log), row(decay_bias), row(head_gain)
+    hidden_mid, resid, hidden_in, low, *saved = front(
+        inputs, row(attn_gain), w_query, w_key, w_value, w_gate, w_ba, w_out, segments, conv_query, conv_key, conv_value,
+        dlog, dbias, hgain, row(ffn_gain))
+    names = ("qpad", "kpad", "vpad", "segpad", "gp", "ba", "q", "k", "x", "u", "s", "o", "fq", "fk", "fv", "pp", "kkp", "db", "z", "cols", "brow")
     grad_attn, inner, ffn, grad_resid, ffn_gain_part, grads_mid = mid_exchange(
-        w_up_gate.T, w_up.T, w_down, hidden_mid, out_grad, resid, rows8(ffn_gain))
-    gq, gk, gv, gt, gba, taps, small, hgain, oshard, grads_out = mixer_bwd(
-        seg3, grad_attn, w_out, low, ffn, resid, qp, kp, vp, gp, ba, conv_query, conv_key, conv_value, rate, bias, gain8, q, k, x, u, s, o)
-    gains_in = jnp.concatenate([jnp.zeros((16, 128), F32), jnp.sum(ffn_gain_part, axis=0).reshape(16, 128), hgain[0].reshape(2, 128),
-                                jnp.zeros((SMALL - 34, 128), F32)], axis=0)
-    taps_in = jnp.concatenate([taps[:4].reshape(32, 128), small], axis=0)
-    ig, out32, grads_in, gains, taps_sum = in_exchange(
-        (gq, gk, gv, gt, gba), inner, (w_query, w_key, w_value, w_gate, w_ba), hidden_in, out_grad, grad_resid, inputs,
-        rows8(attn_gain), gains_in, taps_in, oshard)
-    input_grad = ig.astype(BF16)
-    outputs = out32.astype(BF16)
-    n = w_up.shape[1]
-    ct = taps_sum[:32].reshape(4, 1024)
-    return (outputs, input_grad, gains[:16].reshape(D), grads_in[0:256].T, grads_in[256:512].T, grads_in[512:1024].T, grads_in[1024:1536].T,
-            grads_in[1536:1538].T, grads_in[1538:1540].T, ct[:, 0:256], ct[:, 256:512], ct[:, 512:],
-            taps_sum[33, 2:4], taps_sum[32, 2:4], gains[32:34].reshape(256), grads_out, gains[16:32].reshape(D),
-            grads_mid[0:n].T, grads_mid[n:2 * n].T, grads_in[1552:])
+        w_up_gate.T, w_up.T, w_down, hidden_mid, out_grad, resid, row(ffn_gain))
+    *grads, taps, hgain_part, oshard, grads_out = mixer_bwd(
+        resid, conv_query, conv_key, conv_value, dlog, dbias, hgain, ga=grad_attn, wout=w_out, low=low, ffn=ffn, **dict(zip(names, saved)))
+    ig, out, grads_in, gains, taps = in_exchange(
+        grads, (w_query, w_key, w_value, w_gate, w_ba), inner, hidden_in, out_grad, grad_resid, inputs,
+        row(attn_gain), ffn_gain_part, hgain_part, taps, oshard)
+    (input_grad, outputs, gq, gk, gv, gt, gbeta, galpha, cq, ck, cv, g_dlog, g_dbias, g_hgain, g_again, g_fgain,
+     gug, gup, gdown, gout) = last(ig, out, grads_in, grads_mid, grads_out, gains, taps)
+    return (outputs, input_grad, g_again.reshape(D), gq, gk, gv, gt, gbeta.T, galpha.T, cq, ck, cv,
+            g_dlog.reshape(2), g_dbias.reshape(2), g_hgain.reshape(head_gain.shape), gout, g_fgain.reshape(D), gug.T, gup.T, gdown)
 
 
 def solution(mesh):
-    col, row, rep = P(None, "tensor"), P("tensor", None), P()
+    col, rows_t, rep = P(None, "tensor"), P("tensor", None), P()
     tok, both, head = P("dp", None), P("dp", "tensor"), P("tensor")
     return jax.shard_map(
         per_device,
         mesh=mesh,
-        in_specs=(tok, tok, rep, col, col, col, col, col, col, col, col, col, head, head, rep, row, rep, col, col, row, tok),
+        in_specs=(tok, tok, rep, col, col, col, col, col, col, col, col, col, head, head, rep, rows_t, rep, col, col, rows_t, tok),
         out_specs=(tok, tok, rep, both, both, both, both, both, both, col, col, col, head, head, rep, P("tensor", "dp"), rep, both, both, P("tensor", "dp")),
         check_vma=False,
     )

time: 533 us -> 478 us (0.90)
  other arithmetic: 18.5 us -> 1.61 us
  matrix products: 13.7 us -> 0 us
  local copies, waits for them, and re-layouts: 15.5 us -> 2.8 us
  Pallas kernels: 475 us -> 463 us
    pallas_call x2, Pallas kernels: 123 us -> 143 us  [the longest x1 134 us: front(): pl.pallas_call(functools.partial(front_kernel, blocks, group), out_shape=...]
    pallas_call x1, Pallas kernels: 79 us -> 59.8 us  [mixer_bwd(): pl.pallas_call(functools.partial(bwd_kernel, blocks), out_shape=(sd((T, 2...]
    dot_general x5 -> x0, matrix products: 13.7 us -> none  [matmul(): return jnp.dot(left, right, preferred_element_type=F32)]
    convert_element_type x3 -> x0, other arithmetic: 9.67 us -> none  [the longest x1 5.09 us: per_device(): outputs = out32.astype(BF16)]
    pallas_call x1, Pallas kernels: 163 us -> 154 us  [in_exchange(): pl.pallas_call(in_kernel, out_shape=(sd((T, D), F32), sd((T, D), F32), sd...]
where the time goes in v4:
time: 478 us; the launch traced here: 469 us
  Pallas kernels  463 us (97%)
    pallas_call x1, Pallas kernels, in_exchange(): pl.pallas_call(in_kernel, out_shape=(sd((T, D), F32), sd((T, D), F32), sd...  154 us
    pallas_call x1, Pallas kernels, front(): pl.pallas_call(functools.partial(front_kernel, blocks, group), out_shape=...  134 us
    pallas_call x1, Pallas kernels, mid_exchange(): pl.pallas_call(mid_kernel, out_shape=(sd((T, D), BF16), sd((T, m), BF16),...  106 us
    pallas_call x1, Pallas kernels, mixer_bwd(): pl.pallas_call(functools.partial(bwd_kernel, blocks), out_shape=(sd((T, 2...  59.8 us

profile of v4, /device:TPU:24, one launch (start us, length us, event | category | flops | bytes accessed | tf_op | source)
XLA Modules:
  0.0 469.0 jit_solution(3775352222601054772)
XLA Ops:
  0.7 0.1 pad.2.clone
  0.7 1.6 maximum_maximum_fusion.wba_any.refs_9_
  2.4 133.6 %front.1 = (bf16[768,2048]{1,0:T(8,128)(2,1)}, f32[96,2048]{1,0:T(8,128)}, bf16[768,2048]{1,0:T(8,128)(2,1)}, bf16[768,512]{1,0:T(8,128)(2,1)}, f32[776,256]{1,0...) custom-call(bf16[768,2048]{1,0:T(8,128)(2,1)} %refs_14_.1, ...), custom_call_target="tpu_custom_call" | custom-call | tf_op jit(solution)/shard_map/front/pallas_call | solution.py:719
  136.0 106.2 %mid_exchange.1 = (bf16[768,2048]{1,0:T(8,128)(2,1)}, bf16[768,704]{1,0:T(8,128)(2,1)}, f32[768,2048]{1,0:T(8,128)}, f32[96,2048]{1,0:T(8,128)}, f32[8,2048]{1,0:T(8,128)}, /*index=5*/f32[1408,128]{1,0:T(8,128)}) custom-call(bf16[704,2048]{1,0:T(8,128)(2,1)} %bitcast.18, bf16[704,2048]{1,0:T(8,128)(2,1)} %bitcast.19, bf16[704,2048]{1,0:T(8,128)(2,1)} %wd_any.1, ...), custom_call_target="tpu_custom_call" | custom-call | tf_op jit(solution)/shard_map/mid_exchange/pallas_call | solution.py:1079
  242.2 59.8 %mixer_backward.1 = (bf16[768,256]{1,0:T(8,128)(2,1)}, bf16[768,256]{1,0:T(8,128)(2,1)}, bf16[768,512]{1,0:T(8,128)(2,1)}, bf16[768,512]{1,0:T(8,128)(2,1)}, bf1...) custom-call(bf16[768,2048]{1,0:T(8,128)(2,1)} %get-tuple-element.87., ...), custom_call_target="tpu_custom_call" | custom-call | tf_op jit(solution)/shard_map/mixer_backward/pallas_call | solution.py:965
  302.0 0.0 copy-start.1
  302.0 0.0 copy-start.2
  302.0 154.4 %in_exchange.1 = (f32[768,2048]{1,0:T(8,128)}, f32[768,2048]{1,0:T(8,128)}, f32[2256,128]{1,0:T(8,128)}, f32[40,128]{1,0:T(8,128)}, f32[40,128]{1,0:T(8,128)}) custom-call(bf16[768,256]{1,0:T(8,128)(2,1)} %get-tuple-element.111.refs_0_, bf16[768,256]{1,0:T(8,128)(2,1)} %get-tuple-element.112.refs_1_, bf16[768,512]{1,0:T(8,128)(2,1)} %get-tuple-element.113.refs_2_, ...), custom_call_target="tpu_custom_call" | custom-call | tf_op jit(solution)/shard_map/in_exchange/pallas_call | solution.py:1221
  456.5 0.0 copy-done.1
  456.5 0.0 copy-done.2
  456.5 0.0 copy-start
  456.5 1.3 copy-done
  457.8 0.0 copy-start.3
  457.8 0.7 copy-done.3
  458.5 0.0 copy-start.4
  458.5 0.7 copy-done.4
  459.2 9.3 %last.1 = (bf16[768,2048]{1,0:T(8,128)(2,1)}, bf16[768,2048]{1,0:T(8,128)(2,1)}, f32[128,256]{1,0:T(8,128)}, f32[128,256]{1,0:T(8,128)}, f32[128,512]{1,0:T(8,12...) custom-call(f32[768,2048]{1,0:T(8,128)} %get-tuple-element.123.ig_re, ...), custom_call_target="tpu_custom_call" | custom-call | tf_op jit(solution)/shard_map/last/pallas_call | solution.py:1273
  (1 shorter events, 0.0 us)
Async XLA Ops:
  302.0 154.5 %copy-start.1 = (f32[1408,128]{1,0:T(8,128)S(1)}, f32[1408,128]{1,0:T(8,128)}, u32[]{:S(2)}) copy-start(f32[1408,128]{1,0:T(8,128)} %get-tuple-element.126.gmid_ref) | copy-start | bytes 2162692
  302.0 154.5 %copy-start.2 = (f32[512,128]{1,0:T(8,128)S(1)}, f32[512,128]{1,0:T(8,128)}, u32[]{:S(2)}) copy-start(f32[512,128]{1,0:T(8,128)} %get-tuple-element.127.gout_ref) | copy-start | bytes 786436
  456.5 1.3 copy-start
  457.8 0.7 copy-start.3
  458.5 0.7 copy-start.4

commit v5 on v4

--- a/solution.py
+++ b/solution.py
@@ -151,9 +151,6 @@
 
 ZA, ZB, ZZ = pl.ds(0, ZH), pl.ds(ZH, ZH), pl.ds(0, 2 * ZH)
 YA, YB, YY = pl.ds(2 * ZH, YH), pl.ds(2 * ZH + YH, YH), pl.ds(2 * ZH, 2 * YH)
-GZH, GYH = 768, 256
-GZA, GZB, GZZ = pl.ds(0, GZH), pl.ds(GZH, GZH), pl.ds(0, 2 * GZH)
-GYA, GYB, GYY = pl.ds(2 * GZH, GYH), pl.ds(2 * GZH + GYH, GYH), pl.ds(2 * GZH, 2 * GYH)
 ZLO, ZHI, YLO, YHI = pl.ds(0, ZH), pl.ds(ZH, ZH), pl.ds(0, YH), pl.ds(YH, YH)
 
 
@@ -270,8 +267,11 @@
 
 
 class Gather:
-    def __init__(self, ring, whole, sems, own):
+    def __init__(self, ring, whole, sems, own, yh=256):
         self.ring, self.whole, self.own = ring, whole, own
+        zh = whole.shape[1] // 2 - yh
+        self.za, self.zb, self.zz = pl.ds(0, zh), pl.ds(zh, zh), pl.ds(0, 2 * zh)
+        self.ya, self.yb, self.yy = pl.ds(2 * zh, yh), pl.ds(2 * zh + yh, yh), pl.ds(2 * zh, 2 * yh)
         self.s = Sends(*sems)
 
     def _go(self, i, rows, cols, device):
@@ -284,54 +284,54 @@
     def start(self):
         g, own = self.ring, self.own
         mine = g.rows(0, False, own)
-        self._go(0, mine, GYY, g.right)
-        self._go(1, mine, GYY, g.left)
-        self._go(2, mine, GZZ, g.flip)
-        self._go(3, mine, GZZ, g.right)
-        self._go(4, mine, GZZ, g.left)
-        self._go(5, mine, GYY, g.flip)
+        self._go(0, mine, self.yy, g.right)
+        self._go(1, mine, self.yy, g.left)
+        self._go(2, mine, self.zz, g.flip)
+        self._go(3, mine, self.zz, g.right)
+        self._go(4, mine, self.zz, g.left)
+        self._go(5, mine, self.yy, g.flip)
 
     def middle(self):
         g, own = self.ring, self.own
         lf, rt = g.rows(3, False, own), g.rows(1, False, own)
         lo, ro = g.rows(3, True, own), g.rows(1, True, own)
         far, faro, other = g.rows(2, False, own), g.rows(2, True, own), g.rows(0, True, own)
-        self._got(0, lf, GYY, g.left)
-        self._go(6, lf, GYB, g.right)
-        self._go(7, lf, GYY, g.flip)
-        self._got(1, rt, GYY, g.right)
-        self._go(8, rt, GYA, g.left)
-        self._go(9, rt, GYY, g.flip)
-        self._got(2, other, GZZ, g.flip)
-        self._go(10, other, GZZ, g.right)
-        self._go(11, other, GZZ, g.left)
+        self._got(0, lf, self.yy, g.left)
+        self._go(6, lf, self.yb, g.right)
+        self._go(7, lf, self.yy, g.flip)
+        self._got(1, rt, self.yy, g.right)
+        self._go(8, rt, self.ya, g.left)
+        self._go(9, rt, self.yy, g.flip)
+        self._got(2, other, self.zz, g.flip)
+        self._go(10, other, self.zz, g.right)
+        self._go(11, other, self.zz, g.left)
         yield
-        self._got(6, far, GYB, g.left)
-        self._got(8, far, GYA, g.right)
-        self._go(12, far, GYY, g.flip)
+        self._got(6, far, self.yb, g.left)
+        self._got(8, far, self.ya, g.right)
+        self._go(12, far, self.yy, g.flip)
         yield
-        self._got(3, lf, GZZ, g.left)
-        self._go(13, lf, GZB, g.right)
-        self._got(4, rt, GZZ, g.right)
-        self._go(14, rt, GZA, g.left)
+        self._got(3, lf, self.zz, g.left)
+        self._go(13, lf, self.zb, g.right)
+        self._got(4, rt, self.zz, g.right)
+        self._go(14, rt, self.za, g.left)
         yield
-        self._got(10, lo, GZZ, g.left)
-        self._go(15, lo, GZB, g.right)
-        self._got(11, ro, GZZ, g.right)
-        self._go(16, ro, GZA, g.left)
+        self._got(10, lo, self.zz, g.left)
+        self._go(15, lo, self.zb, g.right)
+        self._got(11, ro, self.zz, g.right)
+        self._go(16, ro, self.za, g.left)
         yield
 
     def finish(self):
         g, own = self.ring, self.own
         far, faro, other = g.rows(2, False, own), g.rows(2, True, own), g.rows(0, True, own)
-        self._got(5, other, GYY, g.flip)
-        self._got(7, g.rows(3, True, own), GYY, g.flip)
-        self._got(9, g.rows(1, True, own), GYY, g.flip)
-        self._got(12, faro, GYY, g.flip)
-        self._got(13, far, GZB, g.left)
-        self._got(14, far, GZA, g.right)
-        self._got(15, faro, GZB, g.left)
-        self._got(16, faro, GZA, g.right)
+        self._got(5, other, self.yy, g.flip)
+        self._got(7, g.rows(3, True, own), self.yy, g.flip)
+        self._got(9, g.rows(1, True, own), self.yy, g.flip)
+        self._got(12, faro, self.yy, g.flip)
+        self._got(13, far, self.zb, g.left)
+        self._got(14, far, self.za, g.right)
+        self._got(15, faro, self.zb, g.left)
+        self._got(16, faro, self.za, g.right)
 
 
 class DpScatter:
@@ -497,32 +497,39 @@
     return xs
 
 
-def front_kernel(blocks, group, x_ref, again_ref, wq_any, wk_any, wv_any, wt_any, wba_any, wout_any, segments_ref, cq_ref, ck_ref, cv_ref,
+PARTS = 3
+
+
+def place_of(t, g):
+    return t * 96 + g * 32
+
+
+def natural_of(t, g):
+    return g * 256 + t * 32
+
+
+def front_kernel(blocks, x_ref, again_ref, wq_any, wk_any, wv_any, wt_any, wba_any, wout_any, segments_ref, cq_ref, ck_ref, cv_ref,
                  dlog_ref, dbias_ref, gain_ref, fgain_ref,
                  hidmid_ref, resid_ref, *rest):
     outs, rest = rest[:23], rest[23:]
     saved, rest = rest[:23], rest[23:]
     (hid, low_ref, qpad, kpad, vpad, segpad, gp_ref, ba_ref, q_ref, k_ref, x_s, u_ref, s_ref, o_ref,
      fq, fk, fv, pp, kkp, db, z_s, cols_s, brow) = saved
-    wq, wk, wv, wt, wba, wout, w_s, u0_s, kw_s, part, whole, seg_ref, wsem, osem = rest[:14]
-    scr, gsem = rest[14:21], rest[21:23]
+    wq, wk, wv, wt, wba, wout, w_s, kw_s, seg_ref, state, wsem, osem = rest[:12]
+    parts, wholes, rest = rest[12:15], rest[15:18], rest[18:]
     T = blocks * L
-    own = resid_ref.shape[0]
+    span = T // PARTS
+    own = span // NT_
+    group = span // L
     fetch = [pltpu.make_async_copy(src, dst, wsem.at[i]) for i, (src, dst) in enumerate(
         ((wq_any, wq), (wk_any, wk), (wv_any, wv), (wt_any, wt), (wba_any, wba), (wout_any, wout)))]
     leave = [pltpu.make_async_copy(src, dst, osem.at[i]) for i, (src, dst) in enumerate(zip(saved, outs))]
     for f in fetch:
         f.start()
     rate, bias = decay_rows(dlog_ref, dbias_ref)
-
-    def norm(i, _):
-        r = pl.ds(pl.multiple_of(i * 32, 32), 32)
-        v = x_ref[r, :].astype(F32)
-        n = v * lax.rsqrt(jnp.mean(v * v, axis=-1, keepdims=True) + 1e-05)
-        hid[r, :] = (n * again_ref[0:1, :]).astype(BF16)
-        return 0
-
-    lax.fori_loop(0, T // 32, norm, 0)
+    ring = Ring()
+    scatters = [Scatter(ring, parts[g], rest[7 * g:7 * g + 7], own) for g in range(PARTS)]
+    gathers = [Gather(ring, wholes[g], rest[7 * PARTS + 2 * g:7 * PARTS + 2 * g + 2], own, 384) for g in range(PARTS)]
     for pad in (qpad, kpad, vpad):
         pad[0:PAD, :] = jnp.zeros((PAD, pad.shape[1]), F32)
     segpad[0:PAD, :] = jnp.full((PAD, L), -1.0, F32)
@@ -531,24 +538,27 @@
         seg_ref[b, 0:1, :] = segments_ref[0:1, b * L:(b + 1) * L].astype(F32)
         seg_ref[b, 1:2, :] = jnp.broadcast_to(segments_ref[0:1, max(b * L - 1, 0):max(b * L - 1, 0) + 1].astype(F32), (1, L))
         segpad[PAD + b * L:PAD + (b + 1) * L, :] = jnp.broadcast_to(seg_ref[b, 0:1, :], (L, L)).T
-    for i, (w, dst, lead) in enumerate(((wq, qpad, PAD), (wk, kpad, PAD), (wv, vpad, PAD), (wt, gp_ref, 0), (wba, ba_ref, 0))):
-        fetch[i].wait()
-
-        def project(j, _):
-            r = pl.multiple_of(j * 256, 256)
-            dst[pl.ds(r + lead, 256), :] = mm1(hid[pl.ds(r, 256), :], w[...], NT if w is wba else NN)
+    state[...] = jnp.zeros_like(state)
+
+    def project(g):
+        def norm(i, _):
+            r = pl.ds(pl.multiple_of(g * span + i * 32, 32), 32)
+            v = x_ref[r, :].astype(F32)
+            n = v * lax.rsqrt(jnp.mean(v * v, axis=-1, keepdims=True) + 1e-05)
+            hid[r, :] = (n * again_ref[0:1, :]).astype(BF16)
             return 0
 
-        lax.fori_loop(0, T // 256, project, 0)
-    for i in range(8):
-        if i != 1:
-            leave[i].start()
-
-    def phase_a(g, _):
+        lax.fori_loop(0, span // 32, norm, 0)
+        for i, (w, dst, lead) in enumerate(((wq, qpad, PAD), (wk, kpad, PAD), (wv, vpad, PAD), (wt, gp_ref, 0), (wba, ba_ref, 0))):
+            if g == 0:
+                fetch[i].wait()
+            dst[g * span + lead:(g + 1) * span + lead, :] = mm1(hid[g * span:(g + 1) * span, :], w[...], NT if w is wba else NN)
+
+    def phase_a(g):
         a_mats, keepers = [], []
         for i in range(group):
             b = g * group + i
-            base = pl.multiple_of(b * L, L)
+            base = b * L
             here = pl.ds(base, L)
             per_head, strict_keep, _u = block_decay(b, seg_ref, ba_ref, rate, bias)
             masks = doc_masks(segpad, base, L, False)
@@ -587,30 +597,23 @@
         for x, (here, kc, vc, v, gk) in zip(xs, keepers):
             x_s[here, kc] = x
             sx = split(x)
-            u0_s[here, vc] = mm3(sx, split(v))
+            u_ref[here, vc] = mm3(sx, split(v))
             w_s[here, kc] = mm3(sx, split(gk))
-        return 0
-
-    lax.fori_loop(0, blocks // group, phase_a, 0)
-
-    def phase_b(b, state):
+
+    def phase_b(b, _):
         base = pl.multiple_of(b * L, L)
         here = pl.ds(base, L)
         per_head, strict_keep, _u = block_decay(b, seg_ref, ba_ref, rate, bias)
-        new = []
         for h in range(2):
             decay, carry, beta_row, beta_col, last_decay = per_head[h]
             kc = slice(h * 128, h * 128 + 128)
             vc = slice(h * 256, h * 256 + 256)
             s = state[h]
             s_ref[here, vc] = s
-            u = u0_s[here, vc] - mm3(split(w_s[here, kc]), split(s))
+            u = u_ref[here, vc] - mm3(split(w_s[here, kc]), split(s))
             u_ref[here, vc] = u
-            new.append(carry[L - 1:L, :] * s + mm3(split(kw_s[here, kc]), split(u), TN))
-        return tuple(new)
-
-    zero = jnp.zeros((128, 256), F32)
-    lax.fori_loop(0, blocks, phase_b, (zero, zero))
+            state[h] = carry[L - 1:L, :] * s + mm3(split(kw_s[here, kc]), split(u), TN)
+        return 0
 
     def phase_c(b, _):
         base = pl.multiple_of(b * L, L)
@@ -630,25 +633,37 @@
             low_ref[here, vc] = (n * gain_ref[0:1, :] * (gp * sigmoid(gp))).astype(BF16)
         return 0
 
-    lax.fori_loop(0, blocks, phase_c, 0)
-
-    ring = Ring()
-    mine = ring.rows(0, False, own)
-    fetch[5].wait()
-    greet([ring.right, ring.left, ring.flip])
-    sc = Scatter(ring, part, scr, own)
-    for k in sc.ORDER:
-        quarter = ring.quarter(k, own)
+    def mix(g):
+        phase_a(g)
+        lax.fori_loop(g * group, (g + 1) * group, phase_b, 0)
+        lax.fori_loop(g * group, (g + 1) * group, phase_c, 0)
+        if g == 0:
+            fetch[5].wait()
 
         def partial(n, _):
             c = pl.ds(pl.multiple_of(n * 512, 512), 512)
-            part[quarter, c] = mm1(low_ref[quarter, :], wout[:, c], NN)
+            parts[g][:, c] = mm1(low_ref[g * span:(g + 1) * span, :], wout[:, c], NN)
             return 0
 
-        lax.fori_loop(0, part.shape[1] // 512, partial, 0)
-        sc.start(k)
-    for i in (1, 8, 9, 10, 11, 12, 13, 14, 15, 16, 17, 18):
-        leave[i].start()
+        lax.fori_loop(0, wout.shape[1] // 512, partial, 0)
+        for k in Scatter.ORDER:
+            scatters[g].start(k)
+
+    def normed(g):
+        sc, whole = scatters[g], wholes[g]
+        sc.finish()
+
+        def finish(i, _):
+            r = pl.multiple_of(i * 16, 16)
+            at = pl.multiple_of(ring.t * own + r, 16)
+            resid = x_ref[pl.ds(pl.multiple_of(g * span + at, 16), 16), :].astype(F32) + sc.value(r)
+            resid_ref[pl.ds(pl.multiple_of(g * own + r, 16), 16), :] = resid
+            n = resid * lax.rsqrt(jnp.mean(resid * resid, axis=-1, keepdims=True) + 1e-05)
+            whole[pl.ds(at, 16), :] = (n * fgain_ref[0:1, :]).astype(BF16).astype(F32)
+            return 0
+
+        lax.fori_loop(0, own // 16, finish, 0)
+        gathers[g].start()
 
     def prepare(b, _):
         base = pl.multiple_of(b * L, L)
@@ -669,60 +684,76 @@
         brow[b] = flat
         return 0
 
-    steps = sc.middle()
-    run(steps, 1)
-    lax.fori_loop(0, blocks // 2, prepare, 0)
-    run(steps, 1)
-    lax.fori_loop(blocks // 2, blocks, prepare, 0)
+    def cast(g):
+        def one(t, _):
+            r = pl.multiple_of(t * own, own)
+            hidmid_ref[pl.ds(pl.multiple_of(place_of(t, g), own), own), :] = wholes[g][pl.ds(r, own), :].astype(BF16)
+            return 0
+
+        lax.fori_loop(0, NT_, one, 0)
+
+    first, second, third = (sc.middle() for sc in scatters)
+    project(0)
+    greet([ring.right, ring.left, ring.flip])
+    mix(0)
+    project(1)
+    mix(1)
+    run(first, 2)
+    project(2)
+    for i in (0, 2, 3, 4, 5, 6, 7):
+        leave[i].start()
+    mix(2)
+    for i in (1, 8, 9, 10, 11, 12, 13, 14, 15, 16, 17, 18):
+        leave[i].start()
+    run(first)
+    run(second, 2)
+    lax.fori_loop(0, blocks, prepare, 0)
     for i in range(19, 23):
         leave[i].start()
-    run(steps)
-    sc.finish()
-
-    def finish(i, _):
-        r = pl.multiple_of(i * 16, 16)
-        at = pl.ds(pl.multiple_of(mine.start + r, 16), 16)
-        resid = x_ref[at, :].astype(F32) + sc.value(r)
-        resid_ref[pl.ds(r, 16), :] = resid
-        n = resid * lax.rsqrt(jnp.mean(resid * resid, axis=-1, keepdims=True) + 1e-05)
-        whole[at, :] = (n * fgain_ref[0:1, :]).astype(BF16).astype(F32)
-        return 0
-
-    lax.fori_loop(0, own // 16, finish, 0)
-    ga = Gather(ring, whole, gsem, own)
-    ga.start()
-    run(ga.middle())
-    ga.finish()
-
-    def cast(i, _):
-        r = pl.ds(pl.multiple_of(i * 32, 32), 32)
-        hidmid_ref[r, :] = whole[r, :].astype(BF16)
-        return 0
-
-    lax.fori_loop(0, whole.shape[0] // 32, cast, 0)
-    sc.s.drain()
-    ga.s.drain()
+    normed(0)
+    run(second)
+    run(third, 2)
+    normed(1)
+    ahead = [ga.middle() for ga in gathers]
+    run(ahead[0], 1)
+    run(third)
+    run(ahead[0])
+    run(ahead[1], 1)
+    normed(2)
+    run(ahead[1])
+    run(ahead[2])
+    for g in range(PARTS):
+        gathers[g].finish()
+        cast(g)
+    for c in scatters + gathers:
+        c.s.drain()
     for c in leave:
         c.wait()
 
 
-def front(x, again, wq, wk, wv, wt, wba, wout, segments, cq, ck, cv, dlog, dbias, gain, fgain, group=2):
+def front(x, again, wq, wk, wv, wt, wba, wout, segments, cq, ck, cv, dlog, dbias, gain, fgain):
     T, D = x.shape
     blocks = T // L
-    own = T // NT_
+    own, span = T // NT_, T // PARTS
     sd = jax.ShapeDtypeStruct
     saved = [((T, D), BF16), ((T, 512), BF16), ((T + PAD, 256), F32), ((T + PAD, 256), F32), ((T + PAD, 512), F32), ((T + 2 * PAD, L), F32),
              ((T, 512), F32), ((T, 128), F32), ((T, 256), F32), ((T, 256), F32), ((T, 256), F32), ((T, 512), F32), ((T, 512), F32), ((T, 512), F32),
              ((T, 256), F32), ((T, 256), F32), ((T, 512), F32), ((T, 256), F32), ((T, 256), F32), ((T, 256), F32), ((T, 256), F32),
              ((T, 128), F32), ((blocks, 8, L), F32)]
     vm = lambda s, t: pltpu.VMEM(s, t)
+    scratch = [vm(*s) for s in saved] + [vm(w.shape, BF16) for w in (wq, wk, wv, wt, wba, wout)]
+    scratch += [vm((T, 256), F32), vm((T, 256), F32), vm((blocks, 8, L), F32), vm((2, 128, 256), F32),
+                pltpu.SemaphoreType.DMA((6,)), pltpu.SemaphoreType.DMA((23,))]
+    scratch += [vm((span, D), F32)] * (2 * PARTS)
+    for _ in range(PARTS):
+        scratch += scatter_scratch(span // NT_)
+    for _ in range(PARTS):
+        scratch += gather_sems()
     return pl.pallas_call(
-        functools.partial(front_kernel, blocks, group),
+        functools.partial(front_kernel, blocks),
         out_shape=[sd((T, D), BF16), sd((own, D), F32)] + [sd(*s) for s in saved],
         in_specs=[VM, VM] + [ANY] * 6 + [VM] * 8, out_specs=[VM, VM] + [ANY] * 23,
-        scratch_shapes=[vm(*s) for s in saved] + [vm(w.shape, BF16) for w in (wq, wk, wv, wt, wba, wout)]
-        + [vm((T, 256), F32), vm((T, 512), F32), vm((T, 256), F32), vm((T, D), F32), vm((T, D), F32), vm((blocks, 8, L), F32),
-           pltpu.SemaphoreType.DMA((6,)), pltpu.SemaphoreType.DMA((23,))] + scatter_scratch(own) + gather_sems(),
+        scratch_shapes=scratch,
         compiler_params=params(1, 62),
         name="front",
     )(x, again, wq, wk, wv, wt, wba, wout, segments, cq, ck, cv, dlog, dbias, gain, fgain)
@@ -975,13 +1006,18 @@
     )(*[held[name] for name in BACK], resid, cq, ck, cv, dlog, dbias, gain)
 
 
+def in_places(source, dest, sems):
+    return [pltpu.make_async_copy(source.at[pl.ds(natural_of(t, g), 32)], dest.at[pl.ds(place_of(t, g), 32)], sems.at[t * PARTS + g])
+            for t in range(NT_) for g in range(PARTS)]
+
+
 def mid_kernel(wg_ref, wu_ref, wd_any, hid_ref, og_any, resid_any, gain_ref,
                ga_ref, inner_ref, ffn_any, gres_ref, dgain_ref, grads_ref,
-               part, whole, left, gg_ref, gu_ref, wd_ref, og_ref, resid_in, csem, *rest):
+               part, whole, left, gg_ref, gu_ref, wd_ref, og_ref, resid_in, csem, gsem_og, *rest):
     scr, gsem, dscr = rest[:7], rest[7:9], rest[9:]
-    fetches = [pltpu.make_async_copy(src, dst, csem.at[i]) for i, (src, dst) in enumerate(
-        ((wd_any, wd_ref), (og_any, og_ref), (resid_any, resid_in)))]
-    for f in fetches:
+    fetches = [pltpu.make_async_copy(wd_any, wd_ref, csem.at[0]), pltpu.make_async_copy(resid_any, resid_in, csem.at[1])]
+    reorder = in_places(og_any, og_ref, gsem_og)
+    for f in fetches + reorder:
         f.start()
     ring = Ring()
     own = gres_ref.shape[0]
@@ -1005,8 +1041,8 @@
         act = gate * sig
         inner_ref[quarter, :] = (act * up).astype(BF16)
         if k == 2:
-            fetches[0].wait()
-            fetches[1].wait()
+            for f in fetches[:1] + reorder:
+                f.wait()
         back = mm1(og_ref[quarter, :], wd_ref[...], NT)
         gg_ref[quarter, :] = (back * up * sig * (1.0 + gate * (1.0 - sig))).astype(BF16)
         gu_ref[quarter, :] = (back * act).astype(BF16)
@@ -1021,7 +1057,7 @@
     left[0:n, :] = gg_ref[...].T
     left[n:2 * n, :] = gu_ref[...].T
     together(sc, dp)
-    fetches[2].wait()
+    fetches[1].wait()
     sc.finish()
     dgain_ref[...] = jnp.zeros_like(dgain_ref)
 
@@ -1061,11 +1097,11 @@
     ga.finish()
 
     def cast(i, _):
-        r = pl.ds(pl.multiple_of(i * 32, 32), 32)
-        ga_ref[r, :] = whole[r, :].astype(BF16)
+        t, g = i // PARTS, lax.rem(i, PARTS)
+        ga_ref[pl.ds(pl.multiple_of(natural_of(t, g), 32), 32), :] = whole[pl.ds(pl.multiple_of(place_of(t, g), 32), 32), :].astype(BF16)
         return 0
 
-    lax.fori_loop(0, whole.shape[0] // 32, cast, 0)
+    lax.fori_loop(0, NT_ * PARTS, cast, 0)
     dp.finish(grads_ref)
     leave.wait()
     ga.s.drain()
@@ -1082,7 +1118,7 @@
         in_specs=[VM, VM, ANY, VM, ANY, ANY, VM], out_specs=[VM, VM, ANY, VM, VM, VM],
         scratch_shapes=[pltpu.VMEM((T, D), F32), pltpu.VMEM((T, D), F32), pltpu.VMEM((2 * m, T), BF16),
                         pltpu.VMEM((T, m), BF16), pltpu.VMEM((T, m), BF16), pltpu.VMEM((m, D), BF16), pltpu.VMEM((T, D), BF16),
-                        pltpu.VMEM((own, D), F32), pltpu.SemaphoreType.DMA((4,))]
+                        pltpu.VMEM((own, D), F32), pltpu.SemaphoreType.DMA((4,)), pltpu.SemaphoreType.DMA((NT_ * PARTS,))]
         + scatter_scratch(own) + gather_sems() + dp_scratch(2 * m, 4),
         compiler_params=params(2, 62),
         name="mid_exchange",
@@ -1094,15 +1130,18 @@
     whole, out_whole, grads_ref, gains_out, taps_out = rest[:5]
     held, rest = rest[5:18], rest[18:]
     gq, gk, gv, gt, gba, wq, wk, wv, wt, wba, inner_ref, hid_ref, og_ref = held
-    part, shard, left, xown, g_own, g_recv, s_own, s_recv, fsem, csem, ssem, srsem = rest[:12]
-    rest = rest[12:]
+    part, shard, left, xown, g_own, g_recv, s_own, s_recv, fsem, csem, ssem, srsem, gsem_og = rest[:13]
+    rest = rest[13:]
     scr, gsem, osem, dscr = rest[:7], rest[7:9], rest[9:11], rest[11:]
-    loads = [pltpu.make_async_copy(src, dst, fsem.at[i]) for i, (src, dst) in enumerate(zip(sources, held))]
+    loads = [pltpu.make_async_copy(src, dst, fsem.at[i]) for i, (src, dst) in enumerate(zip(sources[:12], held))]
+    loads += in_places(sources[12], og_ref, gsem_og)
     ring = Ring()
     own = gres_ref.shape[0]
     mine = ring.rows(0, False, own)
-    fetch = pltpu.make_async_copy(x_ref.at[mine], xown, csem.at[0])
-    fetch.start()
+    fetch = [pltpu.make_async_copy(x_ref.at[pl.ds(pl.multiple_of(natural_of(ring.t, g), 32), 32)], xown.at[pl.ds(g * 32, 32)], csem.at[3 + g])
+             for g in range(PARTS)]
+    for c in fetch:
+        c.start()
     place_out = pltpu.make_async_copy(oshard_ref, out_whole.at[mine], csem.at[1])
     place_out.start()
     for c in loads:
@@ -1119,11 +1158,15 @@
     for k in sc.ORDER:
         quarter = ring.quarter(k, own)
 
+        def chosen(ref):
+            return jnp.concatenate([ref[pl.ds(pl.multiple_of(natural_of(ring.at(k) * 2 + y, g), 32), 32), :] for y in range(2) for g in range(PARTS)],
+                                   axis=0)
+
         def partial(i, _):
             rows_w = pl.ds(pl.multiple_of(i * 512, 512), 512)
-            total = mm1(gq[quarter, :], wq[rows_w, :], NT) + mm1(gk[quarter, :], wk[rows_w, :], NT)
-            total = total + mm1(gv[quarter, :], wv[rows_w, :], NT) + mm1(gt[quarter, :], wt[rows_w, :], NT)
-            part[quarter, rows_w] = total + mm1(gba[quarter, :], wba[:, rows_w], NN)
+            total = mm1(chosen(gq), wq[rows_w, :], NT) + mm1(chosen(gk), wk[rows_w, :], NT)
+            total = total + mm1(chosen(gv), wv[rows_w, :], NT) + mm1(chosen(gt), wt[rows_w, :], NT)
+            part[quarter, rows_w] = total + mm1(chosen(gba), wba[:, rows_w], NN)
             return 0
 
         lax.fori_loop(0, part.shape[1] // 512, partial, 0)
@@ -1148,7 +1191,8 @@
     run(outs, 1)
     together(sc, dp)
     run(outs, 2)
-    fetch.wait()
+    for c in fetch:
+        c.wait()
     sc.finish()
     g_own[...] = jnp.zeros_like(g_own)
     ffn_gain = jnp.sum(fpart_ref[...], axis=0, keepdims=True)
@@ -1225,7 +1269,8 @@
         scratch_shapes=[pltpu.VMEM(h.shape, h.dtype) for h in held]
         + [vm(T, D), vm(own, D), pltpu.VMEM((n, T), BF16), pltpu.VMEM((own, D), BF16),
            vm(SMALL, 128), vm(7, SMALL, 128), vm(SMALL + TAPS, 128), vm(15, SMALL + TAPS, 128),
-           pltpu.SemaphoreType.DMA((13,)), pltpu.SemaphoreType.DMA((3,)), pltpu.SemaphoreType.DMA((22,)), pltpu.SemaphoreType.DMA((22,))]
+           pltpu.SemaphoreType.DMA((12,)), pltpu.SemaphoreType.DMA((3 + PARTS,)), pltpu.SemaphoreType.DMA((22,)), pltpu.SemaphoreType.DMA((22,)),
+           pltpu.SemaphoreType.DMA((NT_ * PARTS,))]
         + scatter_scratch(own) + gather_sems() + gather_sems() + dp_scratch(n, 4),
         compiler_params=params(3, 62),
         name="in_exchange",
@@ -1234,8 +1279,9 @@
 
 def last_kernel(ig_ref, out_ref, gin_ref, gmid_ref, gout_ref, gains_ref, taps_ref,
                 ig_low, out_low, gq, gk, gv, gt, gbeta, galpha, cq, ck, cv, dlog, dbias, hgain, again, fgain, gug, gup, gdown, gout):
-    ig_low[...] = ig_ref[...].astype(BF16)
-    out_low[...] = out_ref[...].astype(BF16)
+    for t in range(NT_):
+        ig_low[t * 32:(t + 1) * 32, :] = ig_ref[t, 0].astype(BF16)
+        out_low[t * 32:(t + 1) * 32, :] = out_ref[t, 0].astype(BF16)
 
     @pl.when(pl.program_id(0) == 0)
     def _():
@@ -1266,19 +1312,20 @@
     T, D = ig.shape
     n = gmid.shape[0] // 2
     sd = lambda *s: jax.ShapeDtypeStruct(s, F32)
-    step = lambda: pl.BlockSpec((128, D), lambda i: (i, 0))
+    step = lambda: pl.BlockSpec((T // PARTS, D), lambda i: (i, 0))
+    shares = lambda: pl.BlockSpec((NT_, 1, 32, D), lambda i: (0, i, 0, 0))
     fixed = lambda s: pl.BlockSpec(s, lambda i: (0, 0))
     small = [sd(128, 256), sd(128, 256), sd(128, 512), sd(128, 512), sd(2, 128), sd(2, 128), sd(4, 256), sd(4, 256), sd(4, 512),
              sd(1, 2), sd(1, 2), sd(2, 128), sd(16, 128), sd(16, 128), sd(n, 128), sd(n, 128), sd(gin.shape[0] - 1552, 128), sd(gout.shape[0], 128)]
     return pl.pallas_call(
         last_kernel,
-        grid=(T // 128,),
+        grid=(PARTS,),
         out_shape=[jax.ShapeDtypeStruct((T, D), BF16)] * 2 + small,
-        in_specs=[step(), step()] + [fixed(a.shape) for a in (gin, gmid, gout, gains, taps)],
+        in_specs=[shares(), shares()] + [fixed(a.shape) for a in (gin, gmid, gout, gains, taps)],
         out_specs=[step(), step()] + [fixed(a.shape) for a in small],
         compiler_params=pltpu.CompilerParams(vmem_limit_bytes=48 * 2 ** 20),
         name="last",
-    )(ig, out, gin, gmid, gout, gains, taps)
+    )(*(a.reshape(NT_, PARTS, 32, D) for a in (ig, out)), gin, gmid, gout, gains, taps)
 
 
 def row(v):

time: 478 us -> 461 us (0.964)
  Pallas kernels: 463 us -> 446 us
    pallas_call x2, Pallas kernels: 143 us -> 125 us  [the longest x1 116 us: front(): pl.pallas_call(functools.partial(front_kernel, blocks), out_shape=[sd((T,...]
where the time goes in v5:
time: 461 us; the launch traced here: 452 us
  Pallas kernels  446 us (97%)
    pallas_call x1, Pallas kernels, in_exchange(): pl.pallas_call(in_kernel, out_shape=(sd((T, D), F32), sd((T, D), F32), sd...  154 us
    pallas_call x1, Pallas kernels, front(): pl.pallas_call(functools.partial(front_kernel, blocks), out_shape=[sd((T,...  116 us
    pallas_call x1, Pallas kernels, mid_exchange(): pl.pallas_call(mid_kernel, out_shape=(sd((T, D), BF16), sd((T, m), BF16),...  107 us
    pallas_call x1, Pallas kernels, mixer_bwd(): pl.pallas_call(functools.partial(bwd_kernel, blocks), out_shape=(sd((T, 2...  59.8 us

profile of v5, /device:TPU:24, one launch (start us, length us, event | category | flops | bytes accessed | tf_op | source)
XLA Modules:
  0.0 451.7 jit_solution(17301401511730466351)
XLA Ops:
  0.7 0.1 pad.2.clone
  0.7 1.6 maximum_maximum_fusion.wba_any.refs_9_
  2.4 116.1 %front.1 = (bf16[768,2048]{1,0:T(8,128)(2,1)}, f32[96,2048]{1,0:T(8,128)}, bf16[768,2048]{1,0:T(8,128)(2,1)}, bf16[768,512]{1,0:T(8,128)(2,1)}, f32[776,256]{1,0...) custom-call(bf16[768,2048]{1,0:T(8,128)(2,1)} %refs_14_.1, ...), custom_call_target="tpu_custom_call" | custom-call | tf_op jit(solution)/shard_map/front/pallas_call | solution.py:752
  118.4 107.0 %mid_exchange.1 = (bf16[768,2048]{1,0:T(8,128)(2,1)}, bf16[768,704]{1,0:T(8,128)(2,1)}, f32[768,2048]{1,0:T(8,128)}, f32[96,2048]{1,0:T(8,128)}, f32[8,2048]{1,0:T(8,128)}, /*index=5*/f32[1408,128]{1,0:T(8,128)}) custom-call(bf16[704,2048]{1,0:T(8,128)(2,1)} %bitcast.22, bf16[704,2048]{1,0:T(8,128)(2,1)} %bitcast.23, bf16[704,2048]{1,0:T(8,128)(2,1)} %wd_any.1, ...), custom_call_target="tpu_custom_call" | custom-call | tf_op jit(solution)/shard_map/mid_exchange/pallas_call | solution.py:1115
  225.4 59.8 %mixer_backward.1 = (bf16[768,256]{1,0:T(8,128)(2,1)}, bf16[768,256]{1,0:T(8,128)(2,1)}, bf16[768,512]{1,0:T(8,128)(2,1)}, bf16[768,512]{1,0:T(8,128)(2,1)}, bf1...) custom-call(bf16[768,2048]{1,0:T(8,128)(2,1)} %get-tuple-element.87., ...), custom_call_target="tpu_custom_call" | custom-call | tf_op jit(solution)/shard_map/mixer_backward/pallas_call | solution.py:996
  285.2 0.0 copy-start.1
  285.2 0.0 copy-start.2
  285.2 154.5 %in_exchange.1 = (f32[768,2048]{1,0:T(8,128)}, f32[768,2048]{1,0:T(8,128)}, f32[2256,128]{1,0:T(8,128)}, f32[40,128]{1,0:T(8,128)}, f32[40,128]{1,0:T(8,128)}) custom-call(bf16[768,256]{1,0:T(8,128)(2,1)} %get-tuple-element.111.refs_0_, bf16[768,256]{1,0:T(8,128)(2,1)} %get-tuple-element.112.refs_1_, bf16[768,512]{1,0:T(8,128)(2,1)} %get-tuple-element.113.refs_2_, ...), custom_call_target="tpu_custom_call" | custom-call | tf_op jit(solution)/shard_map/in_exchange/pallas_call | solution.py:1265
  439.7 0.0 copy-done.1
  439.7 0.0 copy-done.2
  439.7 0.0 copy-start
  439.7 1.3 copy-done
  441.0 0.0 copy-start.3
  441.0 0.7 copy-done.3
  441.7 0.0 copy-start.4
  441.7 0.7 copy-done.4
  442.4 8.9 %last.1 = (bf16[768,2048]{1,0:T(8,128)(2,1)}, bf16[768,2048]{1,0:T(8,128)(2,1)}, f32[128,256]{1,0:T(8,128)}, f32[128,256]{1,0:T(8,128)}, f32[128,512]{1,0:T(8,12...) custom-call(f32[8,3,32,2048]{3,2,1,0:T(8,128)} %bitcast.20, ...), custom_call_target="tpu_custom_call" | custom-call | tf_op jit(solution)/shard_map/last/pallas_call | solution.py:1320
  (1 shorter events, 0.0 us)
Async XLA Ops:
  285.2 154.5 %copy-start.1 = (f32[1408,128]{1,0:T(8,128)S(1)}, f32[1408,128]{1,0:T(8,128)}, u32[]{:S(2)}) copy-start(f32[1408,128]{1,0:T(8,128)} %get-tuple-element.126.gmid_ref) | copy-start | bytes 2162692
  285.2 154.5 %copy-start.2 = (f32[512,128]{1,0:T(8,128)S(1)}, f32[512,128]{1,0:T(8,128)}, u32[]{:S(2)}) copy-start(f32[512,128]{1,0:T(8,128)} %get-tuple-element.127.gout_ref) | copy-start | bytes 786436
  439.7 1.3 copy-start
  441.0 0.7 copy-start.3
  441.7 0.7 copy-start.4

commit v6 on v5

--- a/solution.py
+++ b/solution.py
@@ -1323,7 +1323,7 @@
         out_shape=[jax.ShapeDtypeStruct((T, D), BF16)] * 2 + small,
         in_specs=[shares(), shares()] + [fixed(a.shape) for a in (gin, gmid, gout, gains, taps)],
         out_specs=[step(), step()] + [fixed(a.shape) for a in small],
-        compiler_params=pltpu.CompilerParams(vmem_limit_bytes=48 * 2 ** 20),
+        compiler_params=pltpu.CompilerParams(vmem_limit_bytes=62 * 2 ** 20),
         name="last",
     )(*(a.reshape(NT_, PARTS, 32, D) for a in (ig, out)), gin, gmid, gout, gains, taps)
 

time: 461 us -> 458 us (level)
  no operation moved by 1% of the time
where the time goes in v6:
time: 458 us; the launch traced here: 450 us
  Pallas kernels  447 us (98%)
    pallas_call x1, Pallas kernels, in_exchange(): pl.pallas_call(in_kernel, out_shape=(sd((T, D), F32), sd((T, D), F32), sd...  154 us
    pallas_call x1, Pallas kernels, front(): pl.pallas_call(functools.partial(front_kernel, blocks), out_shape=[sd((T,...  116 us
    pallas_call x1, Pallas kernels, mid_exchange(): pl.pallas_call(mid_kernel, out_shape=(sd((T, D), BF16), sd((T, m), BF16),...  107 us
    pallas_call x1, Pallas kernels, mixer_bwd(): pl.pallas_call(functools.partial(bwd_kernel, blocks), out_shape=(sd((T, 2...  59.7 us
    pallas_call x1, Pallas kernels, last(): pl.pallas_call(last_kernel, grid=(PARTS,), out_shape=[jax.ShapeDtypeStruc...  9.53 us

profile of v6, /device:TPU:24, one launch (start us, length us, event | category | flops | bytes accessed | tf_op | source)
XLA Modules:
  0.0 449.5 jit_solution(7969157474379481651)
XLA Ops:
  0.7 0.1 pad.2.clone
  0.7 1.6 maximum_maximum_fusion.wba_any.refs_9_
  2.4 116.0 %front.1 = (bf16[768,2048]{1,0:T(8,128)(2,1)}, f32[96,2048]{1,0:T(8,128)}, bf16[768,2048]{1,0:T(8,128)(2,1)}, bf16[768,512]{1,0:T(8,128)(2,1)}, f32[776,256]{1,0...) custom-call(bf16[768,2048]{1,0:T(8,128)(2,1)} %refs_14_.1, ...), custom_call_target="tpu_custom_call" | custom-call | tf_op jit(solution)/shard_map/front/pallas_call | solution.py:752
  118.4 107.0 %mid_exchange.1 = (bf16[768,2048]{1,0:T(8,128)(2,1)}, bf16[768,704]{1,0:T(8,128)(2,1)}, f32[768,2048]{1,0:T(8,128)}, f32[96,2048]{1,0:T(8,128)}, f32[8,2048]{1,0:T(8,128)}, /*index=5*/f32[1408,128]{1,0:T(8,128)}) custom-call(bf16[704,2048]{1,0:T(8,128)(2,1)} %bitcast.22, bf16[704,2048]{1,0:T(8,128)(2,1)} %bitcast.23, bf16[704,2048]{1,0:T(8,128)(2,1)} %wd_any.1, ...), custom_call_target="tpu_custom_call" | custom-call | tf_op jit(solution)/shard_map/mid_exchange/pallas_call | solution.py:1115
  225.4 59.7 %mixer_backward.1 = (bf16[768,256]{1,0:T(8,128)(2,1)}, bf16[768,256]{1,0:T(8,128)(2,1)}, bf16[768,512]{1,0:T(8,128)(2,1)}, bf16[768,512]{1,0:T(8,128)(2,1)}, bf1...) custom-call(bf16[768,2048]{1,0:T(8,128)(2,1)} %get-tuple-element.87., ...), custom_call_target="tpu_custom_call" | custom-call | tf_op jit(solution)/shard_map/mixer_backward/pallas_call | solution.py:996
  285.2 154.4 %in_exchange.1 = (f32[768,2048]{1,0:T(8,128)}, f32[768,2048]{1,0:T(8,128)}, f32[2256,128]{1,0:T(8,128)}, f32[40,128]{1,0:T(8,128)}, f32[40,128]{1,0:T(8,128)}) custom-call(bf16[768,256]{1,0:T(8,128)(2,1)} %get-tuple-element.111.refs_0_, bf16[768,256]{1,0:T(8,128)(2,1)} %get-tuple-element.112.refs_1_, bf16[768,512]{1,0:T(8,128)(2,1)} %get-tuple-element.113.refs_2_, ...), custom_call_target="tpu_custom_call" | custom-call | tf_op jit(solution)/shard_map/in_exchange/pallas_call | solution.py:1265
  439.6 9.5 %last.1 = (bf16[768,2048]{1,0:T(8,128)(2,1)}, bf16[768,2048]{1,0:T(8,128)(2,1)}, f32[128,256]{1,0:T(8,128)}, f32[128,256]{1,0:T(8,128)}, f32[128,512]{1,0:T(8,12...) custom-call(f32[8,3,32,2048]{3,2,1,0:T(8,128)} %bitcast.20, ...), custom_call_target="tpu_custom_call" | custom-call | tf_op jit(solution)/shard_map/last/pallas_call | solution.py:1320
  (1 shorter events, 0.0 us)
